TPU v7x, 32 devices: a whole 2x2x4 slice. The times are simulated.
32 devices in a mesh: table: 8 (over z, core), user: 4 (over y, x).
Axes of the slice: x: 2, y: 2, z: 4, core: 2. Of those that a mesh axis runs over, the one named last changes fastest.
Arguments:
- item_table: bfloat16 [32768, 512], P(None, 'table')
- event_ids: int32 [16384], P('user'), may hold values from 0 to 32767
- seq_lengths: int32 [4, 16], P('user'), may hold values from 128 to 640, as said below
- seq_owner: int32 [4, 16], P('user'), may hold values from 0 to 7, as said below
- negative_ids: int32 [1024], P('user'), may hold values from 0 to 32767
- w_in: bfloat16 [512, 2048], replicated, may hold values from -0.25 to 0.25
- w_mid: bfloat16 [2048, 512], replicated, may hold values from -0.125 to 0.125
- w_uvqk: bfloat16 [512, 2048], replicated, may hold values from -0.25 to 0.25
- w_proj: bfloat16 [512, 512], replicated, may hold values from -0.25 to 0.25
Outputs:
- state_grad: float32 [24576, 512], P(('table', 'user'))
Inputs may be any that keep to these rules, and one draw needn't show every extreme that they name: `seq_lengths`: lengths are multiples of 128; each row sums to 4096; the sequences one owner receives from a batch row total at most 768 events, and in every row some owner receives exactly that many and some sequence has the largest length. `seq_owner`: in each row every owner index appears exactly twice.
All inputs are finite; a program needn't handle non-finite values.
Results may differ from a plain program's by a relative error of at most 0.004.
Values may be sent and summed in bfloat16 or wider, within the bound.
No kernel may reach another device: no remote copies, remote signals or barrier semaphores. Data moves between devices by JAX's collectives and lax.ppermute only.
A program may use at most 64 MiB of HBM per device.

v0:
```python
import math

import jax
import jax.numpy as jnp
from jax import lax
from jax.sharding import PartitionSpec as P

HEADS = 4
PAGE = 128
CAP_PAGES = 6


SCORE_SHARPNESS = 0.02
NORM_EPSILON = 1e-06
LAYER_EPSILON = 1e-05


def page_plan(lengths, owners, cap_pages, page_size, tables):
    page_count = lengths // page_size
    seq_count = lengths.shape[0]
    src_start = jnp.cumsum(page_count) - page_count
    seq_order = jnp.arange(seq_count, dtype=jnp.int32)
    before = (owners[:, None] == owners[None, :]) & (seq_order[None, :] < seq_order[:, None])
    dst_start = jnp.sum(jnp.where(before, page_count[None, :], 0), axis=1)
    owner_grid = jnp.arange(tables, dtype=jnp.int32)[:, None, None]
    slot_grid = jnp.arange(cap_pages, dtype=jnp.int32)[None, :, None]
    matched = (
        (owners[None, None, :] == owner_grid)
        & (dst_start <= slot_grid)
        & (slot_grid < dst_start + page_count)
    )
    matched = matched.astype(jnp.int32)
    src_page = jnp.sum(matched * (src_start + slot_grid - dst_start), axis=2)
    filled = jnp.sum(matched, axis=2)
    segment = jnp.sum(matched * (seq_order + 1), axis=2) - 1
    seq_length = jnp.sum(matched * lengths, axis=2)

    def spread(per_page):
        return jnp.repeat(per_page, page_size, axis=1)

    return (src_page, filled, spread(segment), spread(seq_length))


def feed_forward(inputs, w_in, w_mid):
    hidden = jax.nn.silu(jnp.dot(inputs, w_in, preferred_element_type=jnp.float32)).astype(
        jnp.bfloat16
    )
    return jnp.dot(hidden, w_mid, preferred_element_type=jnp.float32).astype(jnp.bfloat16)


def layer_state(mixed_rows, segment, seq_length, w_uvqk, w_proj, head_count):
    row_count, model_width = mixed_rows.shape
    head_width = model_width // head_count
    projected = jax.nn.silu(jnp.dot(mixed_rows, w_uvqk, preferred_element_type=jnp.float32)).astype(
        jnp.bfloat16
    )
    position = jnp.arange(row_count, dtype=jnp.int32)
    allowed = (
        (segment[:, None] == segment[None, :])
        & (position[None, :] <= position[:, None])
        & (segment[:, None] >= 0)
    )
    divisor = jnp.maximum(seq_length, 1).astype(jnp.float32)[:, None]
    outputs = []
    for head_number in range(head_count):
        offset = head_number * head_width
        values = projected[:, model_width + offset : model_width + offset + head_width]
        queries = projected[:, 2 * model_width + offset : 2 * model_width + offset + head_width]
        key_part = projected[:, 3 * model_width + offset : 3 * model_width + offset + head_width]
        scores = lax.dot_general(
            queries, key_part, (((1,), (1,)), ((), ())), preferred_element_type=jnp.float32
        ) / math.sqrt(head_width)
        weights = (jnp.where(allowed, jax.nn.silu(scores), 0.0) / divisor).astype(jnp.bfloat16)
        outputs.append(jnp.dot(weights, values, preferred_element_type=jnp.float32))
    attended = jnp.concatenate(outputs, axis=1)
    average = jnp.mean(attended, axis=1, keepdims=True)
    centered = attended - average
    variance = jnp.mean(centered * centered, axis=1, keepdims=True)
    gate_part = projected[:, :model_width].astype(jnp.float32)
    gated = (centered * lax.rsqrt(variance + LAYER_EPSILON) * gate_part).astype(jnp.bfloat16)
    return mixed_rows.astype(jnp.float32) + jnp.dot(
        gated, w_proj, preferred_element_type=jnp.float32
    )


def unit_rows(matrix):
    return matrix * lax.rsqrt(jnp.sum(matrix * matrix, axis=1, keepdims=True) + NORM_EPSILON)


def state_gradient(state_rows, inputs, segment, negatives):
    user_vector_rescaled = unit_rows(state_rows).astype(jnp.bfloat16)
    unit_items = unit_rows(inputs.astype(jnp.float32)).astype(jnp.bfloat16)
    correct_next_products = jnp.concatenate(
        [unit_items[1:], jnp.zeros_like(unit_items[:1])], axis=0
    )
    next_segment = jnp.concatenate([segment[1:], jnp.full((1,), -1, jnp.int32)], axis=0)
    has_next = (segment >= 0) & (next_segment == segment)
    correct_next_products = jnp.where(
        has_next[:, None], correct_next_products, jnp.zeros_like(correct_next_products)
    )
    distractor_vectors_rescaled = unit_rows(negatives.astype(jnp.float32)).astype(jnp.bfloat16)
    sampled_distractor_scores = (
        lax.dot_general(
            user_vector_rescaled,
            distractor_vectors_rescaled,
            (((1,), (1,)), ((), ())),
            preferred_element_type=jnp.float32,
        )
        / SCORE_SHARPNESS
    )
    correct_pair_score = (
        jnp.sum(
            user_vector_rescaled.astype(jnp.float32) * correct_next_products.astype(jnp.float32),
            axis=1,
        )
        / SCORE_SHARPNESS
    )
    neg_exp = jnp.exp(sampled_distractor_scores)
    correct_score_power = jnp.exp(correct_pair_score)
    partition_function_total = jnp.sum(neg_exp, axis=1) + correct_score_power
    probabilities = (neg_exp / partition_function_total[:, None]).astype(jnp.bfloat16)
    result_derivative = jnp.dot(
        probabilities, distractor_vectors_rescaled, preferred_element_type=jnp.float32
    )
    result_derivative = (
        result_derivative
        + (correct_score_power / partition_function_total - 1.0)[:, None]
        * correct_next_products.astype(jnp.float32)
    ) / SCORE_SHARPNESS
    return jnp.where(has_next[:, None], result_derivative, 0.0)


def page_selector(src_page, filled, page_total):
    page_grid = jnp.arange(page_total, dtype=jnp.int32)
    picked = (src_page[..., None] == page_grid) & (filled[..., None] > 0)
    return picked.astype(jnp.bfloat16)


def outgoing_pages(looked_pages, selector):
    sending = jnp.einsum(
        "tcp,pk->tck", selector, looked_pages, preferred_element_type=jnp.float32
    ).astype(jnp.bfloat16)
    return sending.reshape(sending.shape[0], sending.shape[1], 1, sending.shape[2])


def unpack_pages(block, tables, width):
    pages = block.shape[1]
    shaped = block.reshape(pages, tables, PAGE, width)
    return jnp.transpose(shaped, (0, 2, 1, 3)).reshape(pages * PAGE, tables * width)


def on_device(
    item_table, event_ids, seq_lengths, seq_owner, negative_ids, w_in, w_mid, w_uvqk, w_proj
):
    tables = lax.axis_size("table")
    owner_index = lax.axis_index("table")
    width = item_table.shape[1]
    event_count = event_ids.shape[0]
    page_total = event_count // PAGE
    src_page, filled, segment, seq_length = page_plan(
        seq_lengths[0], seq_owner[0], CAP_PAGES, PAGE, tables
    )
    own_segment = lax.dynamic_index_in_dim(segment, owner_index, 0, keepdims=False)
    own_length = lax.dynamic_index_in_dim(seq_length, owner_index, 0, keepdims=False)
    selector = page_selector(src_page, filled, page_total)
    looked_pages = item_table[event_ids].reshape(page_total, PAGE * width)
    sending = outgoing_pages(looked_pages, selector)
    arrived = lax.all_to_all(sending, "table", split_axis=0, concat_axis=2, tiled=True)
    inputs = unpack_pages(arrived, tables, width)
    mixed_rows = feed_forward(inputs, w_in, w_mid)
    own_negatives = item_table[negative_ids]
    own_count = own_negatives.shape[0]
    flat_negatives = own_negatives.reshape(1, own_count * width)
    gathered_negatives = lax.all_gather(flat_negatives, "user", axis=0, tiled=True)
    neg_part = gathered_negatives.reshape(gathered_negatives.shape[0] * own_count, width)
    neg_count = neg_part.shape[0]
    flat_part = neg_part.reshape(1, neg_count * width)
    all_columns = lax.all_gather(flat_part, "table", axis=0, tiled=True)
    negatives = jnp.transpose(all_columns.reshape(tables, neg_count, width), (1, 0, 2)).reshape(
        neg_count, tables * width
    )
    state_rows = layer_state(mixed_rows, own_segment, own_length, w_uvqk, w_proj, HEADS)
    return state_gradient(state_rows, inputs, own_segment, negatives)


def solution(mesh):
    return jax.shard_map(
        on_device,
        mesh=mesh,
        in_specs=(
            P(None, "table"),
            P("user"),
            P("user", None),
            P("user", None),
            P("user"),
            P(),
            P(),
            P(),
            P(),
        ),
        out_specs=P(("table", "user"), None),
        check_vma=False,
    )
```

profile of v0, /device:TPU:1, one launch (start us, length us, event | category | flops | bytes accessed | tf_op | source)
XLA Modules:
  0.0 149.5 jit_solution(17214933789857161074)
XLA Ops:
  6.5 0.0 copy-start
  6.5 0.8 fusion.70
  7.3 0.7 and_select_fusion
  8.0 0.7 iota_compare_fusion.5
  8.7 0.9 select_reduce_fusion.3
  9.6 0.1 copy.45
  9.7 0.1 reduce.12
  9.8 0.7 fusion.86
  10.5 1.1 select_reduce_fusion.2
  11.7 0.7 fusion.64
  12.4 8.4 %copy.46 = bf16[32768,64]{1,0:T(8,128)(2,1)} copy(bf16[32768,64]{0,1:T(8,128)(2,1)} %param.9) | data formatting | bytes 8388608 | tf_op args[0]
  20.8 15.5 %gather_fusion = bf16[4096,64]{1,0:T(8,128)(2,1)S(1)} fusion(bf16[32768,64]{1,0:T(8,128)(2,1)} %copy.46, s32[4096]{0:T(1024)S(1)} %fusion.64), kind=kCustom, calls=%fused_computation | custom fusion | bytes 1064960 | tf_op jit(solution)/shard_map/gather | solution.py:166
  36.3 1.6 %reshape.429 = bf16[32,8192,1]{1,0,2:T(8,128)(2,1)} reshape(bf16[4096,64]{1,0:T(8,128)(2,1)S(1)} %gather_fusion) | data formatting | bytes 1048576 | tf_op jit(solution)/shard_map/reshape | solution.py:166
  37.9 1.5 fusion
  39.4 1.4 copy.47
  40.8 6.4 %all-to-all-start = ((bf16[8,6,1,8192]{3,1,2,0:T(8,128)(2,1)}), bf16[8,6,1,8192]{3,1,2,0:T(8,128)(2,1)S(1)}, u32[]{:S(2)}, u32[]{:S(2)}) async-start(bf16[8,6,1,8192]{3,1,2,0:T(8,128)(2,1)} %copy.47), calls=%async_computation | async-start | bytes 2097152 | tf_op jit(solution)/shard_map/all_to_all | solution.py:168
  47.2 0.0 all-gather.4.cloned.1.call-start
  47.2 0.0 copy-done.4
  47.2 5.2 %gather_fusion.1 = bf16[256,64]{1,0:T(8,128)(2,1)S(1)} fusion(bf16[32768,64]{1,0:T(8,128)(2,1)} %copy.46, s32[1024]{0:T(1024)S(1)} %pad_clamp_fusion), kind=kCustom, calls=%fused_computation.1 | custom fusion | bytes 66560 | tf_op jit(solution)/shard_map/gather | solution.py:171
  52.4 0.1 reshape.419
  52.5 8.5 %all-gather = bf16[4,1,16384]{2,1,0:T(2,128)(2,1)} all-gather(bf16[1,1,16384]{2,1,0:T(2,128)(2,1)S(1)} %reshape.419), channel_id=1, replica_groups=mesh['table'=8,'user'=4] {'user'}, dimensions={0}, use_global_device_ids=true | all-gather | bytes 163840 | tf_op jit(solution)/shard_map/all_gather | solution.py:174
  61.0 0.0 all-gather.4.cloned.1.call-update
  61.1 0.1 broadcast_bitcast_fusion.1
  61.2 0.1 dynamic-slice_reduce_fusion
  61.3 0.1 broadcast_bitcast_fusion
  61.4 0.1 fusion.68
  61.4 11.4 %all-to-all-done = bf16[8,6,1,8192]{3,1,2,0:T(8,128)(2,1)S(1)} async-done(((bf16[8,6,1,8192]{3,1,2,0:T(8,128)(2,1)}), bf16[8,6,1,8192]{3,1,2,0:T(8,128)(2,1)S(1)}, u32[]{:S(2)}, u32[]{:S(2)}) %all-to-all-start) | async-done | bytes 786464 | tf_op jit(solution)/shard_map/all_to_all | solution.py:168
  72.9 1.3 copy.48
  74.2 3.4 %reshape.395 = bf16[6,8,128,64]{3,2,1,0:T(8,128)(2,1)} reshape(bf16[1,6,8,1,8192]{4,2,1,3,0:T(8,128)(2,1)} %copy.48) | data formatting | bytes 1572864 | tf_op jit(solution)/shard_map/reshape | solution.py:148
  77.6 1.9 %multiply_reduce_fusion = f32[6,128]{1,0:T(8,128)S(1)} fusion(bf16[6,8,128,64]{3,2,1,0:T(8,128)(2,1)} %reshape.395), kind=kLoop, calls=%fused_computation.7 | loop fusion | flops 1178880 | bytes 789504 | tf_op jit(solution)/shard_map/reduce_sum | solution.py:87
  79.5 2.1 %copy.49 = bf16[6,128,8,64]{1,0,3,2:T(8,128)(2,1)S(1)} copy(bf16[6,128,8,64]{3,1,2,0:T(8,128)(2,1)} %bitcast.54) | data formatting | bytes 1572864 | tf_op jit(solution)/shard_map/transpose | solution.py:149
  81.7 1.0 copy.61
  82.7 6.3 %fusion.13 = bf16[768,512]{0,1:T(8,128)(2,1)S(1)} fusion(bf16[2048,512]{1,0:T(8,128)(2,1)} %param.15, bf16[768,512]{0,1:T(8,128)(2,1)} %bitcast.57, bf16[512,2048]{1,0:T(8,128)(2,1)} %param.14), kind=kOutput, calls=%fused_computation.37 | convolution fusion | flops 3229483008 | bytes 5767168 | tf_op jit(solution)/shard_map/dot_general | solution.py:48
  89.0 0.0 copy-done
  89.0 0.0 copy-start.5
  89.0 4.4 %multiply_convert_fusion = bf16[768,2048]{1,0:T(8,128)(2,1)} fusion(bf16[768,512]{0,1:T(8,128)(2,1)S(1)} %fusion.13, bf16[512,2048]{1,0:T(8,128)(2,1)S(1)} %copy-done), kind=kOutput, calls=%fused_computation.4 | convolution fusion | flops 1618477056 | bytes 6029312 | tf_op jit(solution)/shard_map/dot_general | solution.py:54
  93.5 0.0 copy-done.5
  93.5 2.3 %fusion.92 = (f32[768]{0:T(1024)S(1)}, f32[768,128]{0,1:T(8,128)S(1)}) fusion(bf16[768,2048]{1,0:T(8,128)(2,1)} %multiply_convert_fusion, f32[768]{0:T(1024)S(1)} %convert_reduce_fusion.2, pred[768]{0:T(1024)(128)(4,1)S(1)} %get-tuple-element.16, s32[768]{0:T(1024)S(1)} %dynamic-slice_reduce_fusion.1), kind=kOutput, calls=%fused_computation.146 | convolution fusion | flops 309165312 | bytes 999424 | tf_op jit(solution)/shard_map/dot_general | solution.py:74
  95.8 2.3 %fusion.97 = (f32[768]{0:T(1024)S(1)}, f32[768,128]{0,1:T(8,128)S(1)}) fusion(bf16[768,2048]{1,0:T(8,128)(2,1)} %multiply_convert_fusion, f32[768]{0:T(1024)S(1)} %convert_reduce_fusion.2, pred[768]{0:T(1024)(128)(4,1)S(1)} %get-tuple-element.16, s32[768]{0:T(1024)S(1)} %dynamic-slice_reduce_fusion.1), kind=kOutput, calls=%fused_computation.147 | convolution fusion | flops 309165312 | bytes 999424 | tf_op jit(solution)/shard_map/dot_general | solution.py:74
  98.1 3.1 %fusion.87 = (f32[768]{0:T(1024)S(1)}, f32[768,128]{0,1:T(8,128)}) fusion(bf16[768,2048]{1,0:T(8,128)(2,1)} %multiply_convert_fusion, f32[768]{0:T(1024)S(1)} %convert_reduce_fusion.2, pred[768]{0:T(1024)(128)(4,1)S(1)} %get-tuple-element.16, s32[768]{0:T(1024)S(1)} %dynamic-slice_reduce_fusion.1), kind=kOutput, calls=%fused_computation.145 | convolution fusion | flops 309165312 | bytes 999424 | tf_op jit(solution)/shard_map/dot_general | solution.py:74
  101.2 3.1 %fusion.102 = (f32[768]{0:T(1024)S(1)}, f32[768,128]{0,1:T(8,128)}) fusion(bf16[768,2048]{1,0:T(8,128)(2,1)} %multiply_convert_fusion, f32[768]{0:T(1024)S(1)} %convert_reduce_fusion.2, pred[768]{0:T(1024)(128)(4,1)S(1)} %get-tuple-element.16, s32[768]{0:T(1024)S(1)} %dynamic-slice_reduce_fusion.1), kind=kOutput, calls=%fused_computation.148 | convolution fusion | flops 309165312 | bytes 999424 | tf_op jit(solution)/shard_map/dot_general | solution.py:74
  104.3 0.1 slice.79
  104.4 0.2 copy.52
  104.5 0.2 copy.50
  104.7 1.2 copy.51
  105.9 1.9 %copy.53 = f32[768,128]{1,0:T(8,128)} copy(f32[768,128]{0,1:T(8,128)} %get-tuple-element.18) | data formatting | bytes 786432 | tf_op jit(solution)/shard_map/dot_general | solution.py:74
  107.8 1.3 multiply_reduce_fusion.3
  109.1 0.0 copy-start.1
  109.1 2.8 %multiply_reduce_fusion.2 = (f32[768]{0:T(1024)S(1)}, f32[768,512]{0,1:T(8,128)S(1)}) fusion(bf16[512,512]{1,0:T(8,128)(2,1)} %param.17, f32[768,128]{1,0:T(8,128)} %copy.53, f32[768,128]{1,0:T(8,128)S(1)} %copy.52, f32[768,128]{1,0:T(8,128)S(1)} %copy.51, f32[768,128]{1,0:T(8,128)S(1)} %copy.50, bf16[768,2048]{1,0:T(8,128)(2,1)} %multiply_convert_fusion, ...), kind=kOutput, calls=%fused_computation.32 | convolution fusion | flops 407371008 | bytes 5252096 | tf_op jit(solution)/shard_map/dot_general | solution.py:81
  111.9 0.0 copy-start.2
  112.0 0.4 multiply_convert_fusion.3
  112.3 0.7 copy-done.2
  113.1 0.3 fusion.8
  113.4 0.0 all-gather.4.cloned.1.call-done
  113.4 10.3 %multiply_reduce_fusion.1 = (f32[65536]{0:T(1024)}, f32[8,65536]{1,0:T(8,128)}) fusion(bf16[8,1,65536]{2,1,0:T(2,128)(2,1)} %all-gather.4.cloned.1.call-done), kind=kLoop, calls=%fused_computation.21 | loop fusion | flops 1507328 | bytes 3407872 | tf_op jit(solution)/shard_map/reduce_sum | solution.py:87
  123.7 1.1 reduce_sum.163
  124.8 0.2 reduce_sum.164
  125.0 5.2 %reshape.400 = f32[8,1024,64]{2,1,0:T(8,128)} reshape(f32[8,65536]{1,0:T(8,128)} %get-tuple-element.6) | data formatting | bytes 4194304 | tf_op jit(solution)/shard_map/convert_element_type | solution.py:101
  130.2 3.8 %copy.55 = f32[1024,8,64]{0,2,1:T(8,128)} copy(f32[1024,8,64]{2,0,1:T(8,128)} %bitcast.53) | data formatting | bytes 4194304 | tf_op jit(solution)/shard_map/convert_element_type | solution.py:101
  134.0 2.0 %fusion.7 = bf16[1024,512]{0,1:T(8,128)(2,1)S(1)} fusion(f32[1024,8,64]{0,2,1:T(8,128)} %copy.55, f32[1024]{0:T(1024)S(1)} %add_rsqrt_fusion), kind=kLoop, calls=%fused_computation.20 | loop fusion | flops 1048576 | bytes 3149824 | tf_op jit(solution)/shard_map/convert_element_type | solution.py:101
  136.0 0.1 copy-done.3
  136.0 1.2 fusion.2
  137.2 2.4 %fusion.11 = f32[768,512]{0,1:T(8,128)} fusion(bf16[1024,512]{0,1:T(8,128)(2,1)S(1)} %fusion.7, f32[768,1024]{1,0:T(8,128)S(1)} %get-tuple-element.28, f32[768]{0:T(1024)S(1)} %get-tuple-element.14, f32[768]{0:T(1024)S(1)} %get-tuple-element.13, pred[768]{0:T(1024)(128)(4,1)S(1)} %get-tuple-element.15, bf16[767,512]{0,1:T(8,128)(2,1)S(1)} %multiply_convert_fusion.3), kind=kOutput, calls=%fused_computation.28 | convolution fusion | flops 810024960 | bytes 6559488 | tf_op jit(solution)/shard_map/dot_general | solution.py:122
  139.6 3.0 %copy.57 = f32[768,512]{1,0:T(8,128)} copy(f32[768,512]{0,1:T(8,128)} %fusion.11) | data formatting | bytes 3145728 | tf_op jit(solution)/shard_map/jit(_where)/select_n | solution.py:130
  (20 shorter events, 0.2 us)
Async XLA Ops:
  6.5 82.5 %copy-start = (bf16[512,2048]{1,0:T(8,128)(2,1)S(1)}, bf16[512,2048]{1,0:T(8,128)(2,1)}, u32[]{:S(2)}) copy-start(bf16[512,2048]{1,0:T(8,128)(2,1)} %param.16) | copy-start | bytes 6291460
  37.9 9.3 %copy-start.4 = (s32[256]{0:T(256)S(1)}, s32[256]{0:T(256)}, u32[]{:S(2)}) copy-start(s32[256]{0:T(256)} %param.13) | copy-start | bytes 3076
  40.8 32.1 %all-to-all-start = ((bf16[8,6,1,8192]{3,1,2,0:T(8,128)(2,1)}), bf16[8,6,1,8192]{3,1,2,0:T(8,128)(2,1)S(1)}, u32[]{:S(2)}, u32[]{:S(2)}) async-start(bf16[8,6,1,8192]{3,1,2,0:T(8,128)(2,1)} %copy.47), calls=%async_computation | async-start | bytes 2097152 | tf_op jit(solution)/shard_map/all_to_all | solution.py:168
  47.2 66.2 %all-gather.4.cloned.1.call-start = ((), (), s32[]{:S(2)}) async-start(), calls=%async_computation.1 | async-start | bytes 2359296 | tf_op jit(solution)/shard_map/all_gather | solution.py:178
  89.0 4.5 %copy-start.5 = (bf16[768,512]{0,1:T(8,128)(2,1)}, bf16[768,512]{0,1:T(8,128)(2,1)S(1)}, u32[]{:S(2)}) copy-start(bf16[768,512]{0,1:T(8,128)(2,1)S(1)} %fusion.13) | copy-start | bytes 2359300
  109.1 2.8 %copy-start.1 = (bf16[64,8,6,128]{3,1,2,0:T(8,128)(2,1)S(1)}, bf16[64,8,6,128]{3,1,2,0:T(8,128)(2,1)}, u32[]{:S(2)}) copy-start(bf16[64,8,6,128]{3,1,2,0:T(8,128)(2,1)} %copy.61) | copy-start | bytes 2359300
  111.9 1.1 copy-start.2
  134.0 2.0 %copy-start.3 = (f32[768,512]{0,1:T(8,128)S(1)}, f32[768,512]{0,1:T(8,128)}, u32[]{:S(2)}) copy-start(f32[768,512]{0,1:T(8,128)} %copy-done.2) | copy-start | bytes 4718596
Sparse Core Ops, SparseCore 0:
  61.2 30.7 all-gather.3
where the time goes:
time: 151 us; the launch traced here: 150 us
  local copies, waits for them, and re-layouts  57.8 us (38%)
  matrix products  29.4 us (19%)
  other arithmetic  22.3 us (15%)
  between operations  13.7 us (9%)
  waiting for transfers between devices  11.5 us (8%)
  blocking collectives  8.54 us (6%)
  starting transfers between devices  6.38 us (4%)
    gather x1, local copies, waits for them, and re-layouts, on_device(): looked_pages = item_table[event_ids].reshape(page_total, PAGE * width)  15.5 us
    reduce_sum x3, other arithmetic, unit_rows(): jnp.sum(matrix * matrix, axis=1, keepdims=True) + NORM_EPSILON  12.4 us
    all_to_all x1, waiting for transfers between devices, on_device(): lax.all_to_all(sending, 'table', split_axis=0, concat_axis=2, tiled=True)  11.4 us
    dot_general x4, matrix products, layer_state(): outputs.append(jnp.dot(weights, values, preferred_element_type=jnp.float32))  10.8 us
    unnamed x15, local copies, waits for them, and re-layouts  10.3 us
    convert_element_type x2, local copies, waits for them, and re-layouts, state_gradient(): negatives.astype(jnp.float32)  9.01 us
    all_gather x1, blocking collectives, on_device(): lax.all_gather(flat_negatives, 'user', axis=0, tiled=True)  8.54 us
    all_to_all x1, starting transfers between devices, on_device(): lax.all_to_all(sending, 'table', split_axis=0, concat_axis=2, tiled=True)  6.38 us
  transfers between devices with their start and end apart: 2, of which 1 were waited for; matrix products, arithmetic and copies ran while one was open for 30% of the time, Pallas kernels for 0%

commit v1 on v0

v1 whole, which is shorter than its diff:
```python
import functools
import math

import jax
import jax.numpy as jnp
from jax import lax
from jax.experimental import pallas as pl
from jax.experimental.pallas import tpu as pltpu
from jax.sharding import PartitionSpec as P

HEADS = 4
PAGE = 128
HALF = PAGE // 2
CAP_PAGES = 6
CHUNKS = (6,)
LANES = 128

SCORE_SHARPNESS = 0.02
NORM_EPSILON = 1e-06
LAYER_EPSILON = 1e-05

BF = jnp.bfloat16
F32 = jnp.float32
VMEM_BYTES = 60 * 1024 * 1024
COPY_PARTS = 8


def params():
    return pltpu.CompilerParams(vmem_limit_bytes=VMEM_BYTES)


def smem():
    return pl.BlockSpec(memory_space=pltpu.SMEM)


def vmem():
    return pl.BlockSpec(memory_space=pltpu.VMEM)


def hbm():
    return pl.BlockSpec(memory_space=pl.ANY)


def silu(v):
    return v * (0.5 + 0.5 * jnp.tanh(0.5 * v))


def swap_halves(v):
    width = v.shape[1] // 2
    if v.shape[1] == LANES:
        return pltpu.roll(v, width, 1)
    return jnp.concatenate([v[:, width:], v[:, :width]], axis=1)


def place_columns(ref, spare_ref, blocks, chips):
    width = blocks[0].shape[1]
    for s, block in enumerate(blocks):
        chip = source_chip(s, chips)
        if width == LANES:
            ref[:, pl.ds(pl.multiple_of(chip * width, width), width)] = block
        else:
            spare_ref[chip] = block
    if width != LANES:
        ref[...] = jnp.concatenate([spare_ref[chip] for chip in range(chips)], axis=1)


def spare_blocks(chips, rows, width):
    return pltpu.VMEM((chips, rows, width) if width != LANES else (1, 16, LANES), BF)


def lane_ids(shape):
    return lax.broadcasted_iota(jnp.int32, shape, len(shape) - 1)


def gather_kernel(tables, chunks, *refs):
    table_ref, ids_ref, neg_ref, len_ref, own_ref = refs[:5]
    count = len(chunks)
    keep_refs = refs[5 : 5 + count]
    give_refs = refs[5 + count : 5 + 2 * count]
    part_ref, rows_ref, stage_ref, next_ref, sem = refs[5 + 2 * count :]
    me = lax.axis_index("table")
    core = me % 2
    chip = me // 2
    chips = tables // 2
    width, vocab = table_ref.shape
    middle = vocab // 2
    piece = middle // COPY_PARTS

    def copy(side, i):
        at = pl.ds(side * middle + i * piece, piece)
        return pltpu.make_async_copy(table_ref.at[:, at], part_ref.at[:, at], sem.at[side, i])

    for i in range(COPY_PARTS):
        copy(0, i).start()
        copy(1, i).start()
    for i in range(COPY_PARTS):
        copy(0, i).wait()
        copy(1, i).wait()

        def turn(j, carry):
            at = pl.multiple_of(i * piece + j * LANES, LANES)
            low = part_ref[:, pl.ds(at, LANES)].astype(F32)
            high = part_ref[:, pl.ds(middle + at, LANES)].astype(F32)
            turned = jnp.concatenate([low, high], axis=0).T
            rows_ref[pl.ds(at, LANES), :] = turned
            rows_ref[pl.ds(middle + at, LANES), :] = swap_halves(turned)
            return carry

        lax.fori_loop(0, piece // LANES, turn, 0, unroll=4)

    first_xor = core * middle
    second_xor = middle - first_xor
    own_lanes = (lane_ids((1, 2 * width)) < width) == (core == 0)

    def fetch(source, base, half):
        def step(j, carry):
            at = pl.multiple_of(j * 8, 8)
            for k in range(8):
                first = source[base + at + k] ^ first_xor
                second = source[base + half + at + k] ^ second_xor
                picked = jnp.where(
                    own_lanes, rows_ref[pl.ds(first, 1), :], rows_ref[pl.ds(second, 1), :]
                )
                stage_ref[pl.ds(at + k, 1), :] = picked
            return carry

        lax.fori_loop(0, half // 8, step, 0)
        return stage_ref[0:half, :].astype(BF)

    neg_rows = neg_ref.shape[0] // 2
    neg_half = neg_rows // 2
    neg_at = chips * chunks[0] * HALF
    keep_refs[0][neg_at : neg_at + neg_half, :] = fetch(neg_ref, core * neg_rows, neg_half)
    give_refs[0][neg_at : neg_at + neg_half, :] = fetch(neg_ref, (1 - core) * neg_rows, neg_half)

    for t in range(tables):
        next_ref[t] = 0

    def sequence(i, page):
        owner = own_ref[0, i]
        pages = len_ref[0, i] // PAGE
        slot0 = next_ref[owner]
        next_ref[owner] = slot0 + pages
        shift = lax.rem(owner // 2 - chip + chips, chips)
        mine = owner % 2 == core

        def one_page(j, carry):
            block = fetch(ids_ref, (page + j) * PAGE, HALF)
            slot = slot0 + j
            start = 0
            for c, size in enumerate(chunks):
                inside = (slot >= start) & (slot < start + size)
                at = pl.multiple_of((shift * size + slot - start) * HALF, HALF)

                @pl.when(inside & mine)
                def _():
                    keep_refs[c][pl.ds(at, HALF), :] = block

                @pl.when(inside & jnp.logical_not(mine))
                def _():
                    give_refs[c][pl.ds(at, HALF), :] = block

                start += size
            return carry

        lax.fori_loop(0, pages, one_page, 0)
        return page + pages

    lax.fori_loop(0, len_ref.shape[1], sequence, 0)


def gather_rows(item_table, event_ids, negative_ids, seq_lengths, seq_owner, tables, chunks):
    vocab, width = item_table.shape
    chips = tables // 2
    neg_half = negative_ids.shape[0] // 4
    shapes = [
        jax.ShapeDtypeStruct((chips * size * HALF + (neg_half if c == 0 else 0), 2 * width), BF)
        for c, size in enumerate(chunks)
    ]
    outs = pl.pallas_call(
        functools.partial(gather_kernel, tables, chunks),
        out_shape=shapes + shapes,
        in_specs=[hbm(), smem(), smem(), smem(), smem()],
        out_specs=[vmem()] * (2 * len(chunks)),
        scratch_shapes=[
            pltpu.VMEM((width, vocab), BF),
            pltpu.VMEM((vocab, 2 * width), F32),
            pltpu.VMEM((max(HALF, neg_half), 2 * width), F32),
            pltpu.SMEM((tables,), jnp.int32),
            pltpu.SemaphoreType.DMA((2, COPY_PARTS)),
        ],
        compiler_params=params(),
        name="gather_rows",
    )(item_table.T, event_ids, negative_ids, seq_lengths, seq_owner)
    return outs[: len(chunks)], outs[len(chunks) :]


def merge_kernel(chips, pages, neg_half, keep_ref, got_ref, *out_refs):
    core = lax.axis_index("table") % 2
    width = keep_ref.shape[1] // 2
    own_lanes = (lane_ids((1, 2 * width)) < width) == (core == 0)

    def merged(at, half):
        own = keep_ref[at : at + half, :].astype(F32)
        other = got_ref[at : at + half, :].astype(F32)
        top = jnp.where(own_lanes, own, other)
        low = swap_halves(jnp.where(own_lanes, other, own))
        return top.astype(BF), low.astype(BF)

    if neg_half:
        top, low = merged(chips * pages * HALF, neg_half)
        at = pages * PAGE
        for s in range(chips):
            out_refs[s][at : at + neg_half, :] = top
            out_refs[s][at + neg_half : at + 2 * neg_half, :] = low
    for s in range(chips):
        for k in range(pages):
            top, low = merged((s * pages + k) * HALF, HALF)
            out_refs[s][k * PAGE : k * PAGE + HALF, :] = top
            out_refs[s][k * PAGE + HALF : (k + 1) * PAGE, :] = low


def merge_columns(keep, got, chips, pages, neg_half):
    shape = jax.ShapeDtypeStruct((pages * PAGE + 2 * neg_half, keep.shape[1]), BF)
    return pl.pallas_call(
        functools.partial(merge_kernel, chips, pages, neg_half),
        out_shape=[shape] * chips,
        in_specs=[vmem(), vmem()],
        out_specs=[vmem()] * chips,
        compiler_params=params(),
        name="merge_columns",
    )(keep, got)


def source_chip(s, chips):
    chip = lax.axis_index("table") // 2
    return lax.rem(chip - s + chips, chips)


def unit_negatives_kernel(chips, *refs):
    block_refs, out_ref, spare_ref = refs[:chips], refs[chips], refs[chips + 1]
    blocks = [ref[...].astype(F32) for ref in block_refs]
    squares = sum(jnp.sum(b * b, axis=1, keepdims=True) for b in blocks)
    scale = lax.rsqrt(squares + NORM_EPSILON)
    place_columns(out_ref, spare_ref, [(b * scale).astype(BF) for b in blocks], chips)


def unit_negatives(blocks, neg_rows):
    chips = len(blocks)
    tail = (blocks[0].shape[0] - neg_rows) // neg_rows
    lanes = blocks[0].shape[1]
    spec = pl.BlockSpec((neg_rows, lanes), lambda i: (tail, 0))
    return pl.pallas_call(
        functools.partial(unit_negatives_kernel, chips),
        grid=(1,),
        out_shape=jax.ShapeDtypeStruct((neg_rows, chips * lanes), BF),
        in_specs=[spec] * chips,
        out_specs=pl.BlockSpec((neg_rows, chips * lanes), lambda i: (0, 0)),
        scratch_shapes=[spare_blocks(chips, neg_rows, lanes)],
        compiler_params=params(),
        name="unit_negatives",
    )(*blocks)


def own_plan(len_ref, own_ref):
    me = lax.axis_index("table")
    segment = [jnp.int32(-1)] * CAP_PAGES
    length = [jnp.int32(1)] * CAP_PAGES
    start = jnp.int32(0)
    for i in range(len_ref.shape[1]):
        size = len_ref[0, i]
        mine = own_ref[0, i] == me
        end = jnp.where(mine, start + size // PAGE, start)
        for p in range(CAP_PAGES):
            inside = (start <= p) & (p < end)
            segment[p] = jnp.where(inside, i, segment[p])
            length[p] = jnp.where(inside, size, length[p])
        start = end
    return segment, length


def layer_kernel(chips, first, pages, last, *refs):
    len_ref, own_ref = refs[:2]
    block_refs = refs[2 : 2 + chips]
    refs = refs[2 + chips :]
    w_in, w_mid, w_uvqk, w_proj = refs[:4]
    refs = refs[4:]
    if first:
        prior_ref, refs = refs[0], refs[1:]
    unit_ref, item_ref = refs[:2]
    refs = refs[2:]
    if not last:
        kv_out, refs = refs[0], refs[1:]
    w_in_v, w_mid_v, w_uvqk_v, w_proj_v, x_ref, proj_ref, att_ref, spare_ref, sem = refs
    copies = [
        pltpu.make_async_copy(a, b, sem.at[i])
        for i, (a, b) in enumerate(
            ((w_in, w_in_v), (w_mid, w_mid_v), (w_uvqk, w_uvqk_v), (w_proj, w_proj_v))
        )
    ]
    for c in copies:
        c.start()
    width = w_in.shape[0]
    segment, length = own_plan(len_ref, own_ref)
    place_columns(x_ref, spare_ref, [ref[0 : pages * PAGE, :] for ref in block_refs], chips)
    for p in range(pages):
        part = slice(p * PAGE, (p + 1) * PAGE)
        page_x = x_ref[part, :]
        page_x = jnp.where(segment[first + p] >= 0, page_x, jnp.zeros_like(page_x))
        x_ref[part, :] = page_x
        x32 = page_x.astype(F32)
        item_ref[part, :] = (
            x32 * lax.rsqrt(jnp.sum(x32 * x32, axis=1, keepdims=True) + NORM_EPSILON)
        ).astype(BF)

    x = x_ref[...]
    hidden_width = w_in.shape[1]
    step = 512
    copies[0].wait()
    mixed = None
    for f in range(0, hidden_width, step):
        hidden = silu(
            jnp.dot(x, w_in_v[:, f : f + step], preferred_element_type=F32)
        ).astype(BF)
        if f == 0:
            copies[1].wait()
        part = jnp.dot(hidden, w_mid_v[f : f + step, :], preferred_element_type=F32)
        mixed = part if mixed is None else mixed + part
    mixed = mixed.astype(BF)
    copies[2].wait()
    for f in range(0, 4 * width, step):
        proj_ref[:, f : f + step] = silu(
            jnp.dot(mixed, w_uvqk_v[:, f : f + step], preferred_element_type=F32)
        ).astype(BF)
    if not last:
        kv_out[:, :width] = proj_ref[:, width : 2 * width]
        kv_out[:, width:] = proj_ref[:, 3 * width :]

    head_width = width // HEADS
    scale = 1.0 / math.sqrt(head_width)
    row_at = lax.broadcasted_iota(jnp.int32, (PAGE, PAGE), 0)
    causal = lane_ids((PAGE, PAGE)) <= row_at
    for p in range(pages):
        whole = first + p
        part = slice(p * PAGE, (p + 1) * PAGE)
        inverse = jnp.where(
            segment[whole] >= 0, 1.0 / jnp.full((1, PAGE), length[whole], jnp.int32).astype(F32), 0.0
        )
        factors = [
            jnp.where(segment[c] == segment[whole], inverse, 0.0) for c in range(whole)
        ]
        for h in range(HEADS):
            low = h * head_width
            query = proj_ref[part, 2 * width + low : 2 * width + low + head_width]
            keys = proj_ref[0 : (p + 1) * PAGE, 3 * width + low : 3 * width + low + head_width]
            values = proj_ref[0 : (p + 1) * PAGE, width + low : width + low + head_width]
            if first:
                keys = jnp.concatenate(
                    [prior_ref[:, width + low : width + low + head_width], keys], axis=0
                )
                values = jnp.concatenate([prior_ref[:, low : low + head_width], values], axis=0)
            scores = lax.dot_general(
                query, keys, (((1,), (1,)), ((), ())), preferred_element_type=F32
            )
            weights = []
            for c in range(whole + 1):
                score = silu(scores[:, c * PAGE : (c + 1) * PAGE] * scale)
                if c < whole:
                    weights.append((score * factors[c]).astype(BF))
                else:
                    weights.append(jnp.where(causal, score * inverse, 0.0).astype(BF))
            weights = weights[0] if whole == 0 else jnp.concatenate(weights, axis=1)
            att_ref[part, low : low + head_width] = jnp.dot(
                weights, values, preferred_element_type=F32
            )
    attended = att_ref[...]
    centered = attended - jnp.mean(attended, axis=1, keepdims=True)
    variance = jnp.mean(centered * centered, axis=1, keepdims=True)
    gated = (
        centered * lax.rsqrt(variance + LAYER_EPSILON) * proj_ref[:, :width].astype(F32)
    ).astype(BF)
    copies[3].wait()
    state = mixed.astype(F32) + jnp.dot(gated, w_proj_v[...], preferred_element_type=F32)
    unit_ref[...] = (
        state * lax.rsqrt(jnp.sum(state * state, axis=1, keepdims=True) + NORM_EPSILON)
    ).astype(BF)


def layer(seq_lengths, seq_owner, blocks, weights, prior, first, pages, last):
    chips = len(blocks)
    lanes = blocks[0].shape[1]
    width = chips * lanes
    rows = pages * PAGE
    wide = 4 * width
    operands = [seq_lengths, seq_owner, *blocks, *weights]
    in_specs = [smem(), smem()] + [vmem()] * chips + [hbm()] * 4
    if first:
        operands.append(prior)
        in_specs.append(vmem())
    out_shape = [jax.ShapeDtypeStruct((rows, width), BF)] * 2
    if not last:
        out_shape.append(jax.ShapeDtypeStruct((first * PAGE + rows, 2 * width), BF))
    return pl.pallas_call(
        functools.partial(layer_kernel, chips, first, pages, last),
        out_shape=out_shape,
        in_specs=in_specs,
        out_specs=[vmem()] * len(out_shape),
        scratch_shapes=[pltpu.VMEM(w.shape, BF) for w in weights]
        + [
            pltpu.VMEM((rows, width), BF),
            pltpu.VMEM((rows, wide), BF),
            pltpu.VMEM((rows, width), F32),
            spare_blocks(chips, rows, lanes),
            pltpu.SemaphoreType.DMA((4,)),
        ],
        compiler_params=params(),
        name="layer",
    )(*operands)


def gradient_kernel(count, *refs):
    len_ref, own_ref, near_ref, far_ref = refs[:4]
    unit_refs = refs[4 : 4 + count]
    item_refs = refs[4 + count : 4 + 2 * count]
    out_ref, neg_ref, next_ref = refs[4 + 2 * count :]
    half = near_ref.shape[0]
    neg_ref[:half, :] = near_ref[...]
    neg_ref[half:, :] = far_ref[...]
    rows = out_ref.shape[0]
    at = 0
    for ref in item_refs:
        next_ref[at : at + ref.shape[0], :] = ref[...].astype(F32)
        at += ref.shape[0]
    next_ref[rows:, :] = jnp.zeros_like(next_ref[rows:, :])
    segment, _ = own_plan(len_ref, own_ref)
    segment = segment + [jnp.int32(-1)]
    negatives = neg_ref[...]
    sharp = 1.0 / SCORE_SHARPNESS
    row_at = lax.broadcasted_iota(jnp.int32, (PAGE, 1), 0)
    at = 0
    for ref in unit_refs:
        for low in range(0, ref.shape[0], PAGE):
            page = at // PAGE
            unit = ref[low : low + PAGE, :]
            scores = lax.dot_general(
                unit, negatives, (((1,), (1,)), ((), ())), preferred_element_type=F32
            )
            targets = next_ref[at + 1 : at + 1 + PAGE, :]
            last_row = jnp.where(segment[page + 1] == segment[page], PAGE, PAGE - 1)
            limit = jnp.where(segment[page] >= 0, last_row, 0)
            has_next = row_at < limit
            targets = jnp.where(has_next, targets, 0.0)
            positive = jnp.exp(
                jnp.sum(unit.astype(F32) * targets, axis=1, keepdims=True) * sharp
            )
            powers = jnp.exp(scores * sharp)
            total = jnp.sum(powers, axis=1, keepdims=True) + positive
            inverse = 1.0 / total
            probs = (powers * inverse).astype(BF)
            grad = jnp.dot(probs, negatives, preferred_element_type=F32)
            grad = (grad + (positive * inverse - 1.0) * targets) * sharp
            out_ref[at : at + PAGE, :] = jnp.where(has_next, grad, 0.0)
            at += PAGE


def gradient(seq_lengths, seq_owner, near, far, units, items):
    rows = sum(u.shape[0] for u in units)
    half, width = near.shape
    return pl.pallas_call(
        functools.partial(gradient_kernel, len(units)),
        out_shape=jax.ShapeDtypeStruct((rows, width), F32),
        in_specs=[smem(), smem()] + [vmem()] * (2 + 2 * len(units)),
        out_specs=vmem(),
        scratch_shapes=[pltpu.VMEM((2 * half, width), BF), pltpu.VMEM((rows + 8, width), F32)],
        compiler_params=params(),
        name="gradient",
    )(seq_lengths, seq_owner, near, far, *units, *items)


def on_device(
    item_table, event_ids, seq_lengths, seq_owner, negative_ids, w_in, w_mid, w_uvqk, w_proj
):
    tables = lax.axis_size("table")
    users = lax.axis_size("user")
    chips = tables // 2
    neg_half = negative_ids.shape[0] // 4
    cores = [(t, t ^ 1) for t in range(tables)]
    keeps, gives = gather_rows(
        item_table, event_ids, negative_ids, seq_lengths, seq_owner, tables, CHUNKS
    )
    arrived = []
    for c, size in enumerate(CHUNKS):
        got = lax.ppermute(gives[c], "table", cores)
        blocks = list(merge_columns(keeps[c], got, chips, size, neg_half if c == 0 else 0))
        for s in range(1, chips):
            moves = [(t, (t // 2 + s) % chips * 2 + t % 2) for t in range(tables)]
            blocks[s] = lax.ppermute(blocks[s], "table", moves)
        arrived.append(blocks)

    own = unit_negatives(arrived[0], 2 * neg_half)
    parts = [own]
    for s in range(1, users):
        parts.append(lax.ppermute(own, "user", [(u, u ^ s) for u in range(users)]))
    near = jnp.concatenate(parts, axis=0)
    far = lax.ppermute(near, "table", cores)

    weights = (w_in, w_mid, w_uvqk, w_proj)
    units, items = [], []
    prior, first = None, 0
    for c, size in enumerate(CHUNKS):
        last = c == len(CHUNKS) - 1
        outs = layer(seq_lengths, seq_owner, arrived[c], weights, prior, first, size, last)
        units.append(outs[0])
        items.append(outs[1])
        if not last:
            prior = outs[2]
        first += size
    return gradient(seq_lengths, seq_owner, near, far, units, items)


def solution(mesh):
    return jax.shard_map(
        on_device,
        mesh=mesh,
        in_specs=(
            P(None, "table"),
            P("user"),
            P("user", None),
            P("user", None),
            P("user"),
            P(),
            P(),
            P(),
            P(),
        ),
        out_specs=P(("table", "user"), None),
        check_vma=False,
    )
```

time: 151 us -> 83.7 us (0.55)
  the two profiles are of different devices: /device:TPU:1 before, /device:TPU:11 now
where the time goes in v1:
time: 83.7 us; the launch traced here: 83.3 us
  Pallas kernels  44.4 us (53%)
  waiting for transfers between devices  27.9 us (33%)
  starting transfers between devices  7.82 us (9%)
  local copies, waits for them, and re-layouts  2.26 us (3%)
  other arithmetic  0.94 us (1%)
    ppermute x3, waiting for transfers between devices, on_device(): blocks[s] = lax.ppermute(blocks[s], 'table', moves)  19.6 us
    pallas_call x1, Pallas kernels, gather_rows(): pl.pallas_call(functools.partial(gather_kernel, tables, chunks), out_shap...  18.2 us
    pallas_call x1, Pallas kernels, layer(): pl.pallas_call(functools.partial(layer_kernel, chips, first, pages, last)...  15.1 us
    pallas_call x1, Pallas kernels, gradient(): pl.pallas_call(functools.partial(gradient_kernel, len(units)), out_shape=...  7.2 us
    ppermute x3, waiting for transfers between devices, on_device(): parts.append(lax.ppermute(own, 'user', [(u, u ^ s) for u in range(users)]))  6.69 us
    ppermute x3, starting transfers between devices, on_device(): blocks[s] = lax.ppermute(blocks[s], 'table', moves)  3.77 us
    ppermute x3, starting transfers between devices, on_device(): parts.append(lax.ppermute(own, 'user', [(u, u ^ s) for u in range(users)]))  2.65 us
    unnamed x12, local copies, waits for them, and re-layouts  2.26 us
  transfers between devices with their start and end apart: 8, of which 6 were waited for; matrix products, arithmetic and copies ran while one was open for 0% of the time, Pallas kernels for 18%

profile of v1, /device:TPU:11, one launch (start us, length us, event | category | flops | bytes accessed | tf_op | source)
XLA Modules:
  0.0 83.3 jit_solution(16074861777939727331)
XLA Ops:
  0.0 18.2 %gather_rows.1 = (bf16[1600,128]{1,0:T(8,128)(2,1)}, bf16[1600,128]{1,0:T(8,128)(2,1)}) custom-call(bf16[64,32768]{1,0:T(8,128)(2,1)} %bitcast.1, s32[4096]{0:T(1024)} %refs_1_.3, s32[256]{0:T(256)} %refs_2_.1, s32[1,16]{1,0:T(1,128)} %refs_0_.3, s32[1,16]{1,0:T(1,128)} %refs_1_.5), custom_call_target="tpu_custom_call" | custom-call | tf_op jit(solution)/shard_map/gather_rows/pallas_call | solution.py:180
  18.2 0.7 collective-permute-start
  18.9 1.6 %collective-permute-done.got_ref = bf16[1600,128]{1,0:T(8,128)(2,1)S(1)} collective-permute-done((bf16[1600,128]{1,0:T(8,128)(2,1)}, bf16[1600,128]{1,0:T(8,128)(2,1)S(1)}, u32[]{:S(2)}, u32[]{:S(2)}) %collective-permute-start) | collective-permute-done | bytes 409632 | tf_op jit(solution)/shard_map/ppermute | solution.py:493
  20.5 0.0 copy-start.5
  20.5 0.8 copy-done.5
  21.2 2.3 %merge_columns.1 = (bf16[896,128]{1,0:T(8,128)(2,1)}, bf16[896,128]{1,0:T(8,128)(2,1)}, bf16[896,128]{1,0:T(8,128)(2,1)}, bf16[896,128]{1,0:T(8,128)(2,1)}) custom-call(bf16[1600,128]{1,0:T(8,128)(2,1)} %get-tuple-element.13.keep_ref, bf16[1600,128]{1,0:T(8,128)(2,1)} %copy-done.5), custom_call_target="tpu_custom_call" | custom-call | tf_op jit(solution)/shard_map/merge_columns/pallas_call | solution.py:225
  23.5 1.3 %collective-permute-start.1 = (bf16[896,128]{1,0:T(8,128)(2,1)}, bf16[896,128]{1,0:T(8,128)(2,1)S(1)}, u32[]{:S(2)}, u32[]{:S(2)}) collective-permute-start(bf16[896,128]{1,0:T(8,128)(2,1)} %get-tuple-element.16), channel_id=1, source_target_pairs={{0,8},{4,12},{8,16},{12,20},{16,24},{20,28},{24,0},{28,4},{1,9},{5... | collective-permute-start | bytes 688136 | tf_op jit(solution)/shard_map/ppermute | solution.py:497
  24.8 1.0 %collective-permute-start.2 = (bf16[896,128]{1,0:T(8,128)(2,1)}, bf16[896,128]{1,0:T(8,128)(2,1)S(1)}, u32[]{:S(2)}, u32[]{:S(2)}) collective-permute-start(bf16[896,128]{1,0:T(8,128)(2,1)} %get-tuple-element.17), channel_id=1, source_target_pairs={{0,16},{4,20},{8,24},{12,28},{16,0},{20,4},{24,8},{28,12},{1,17},{... | collective-permute-start | bytes 688136 | tf_op jit(solution)/shard_map/ppermute | solution.py:497
  25.8 1.5 %collective-permute-start.3 = (bf16[896,128]{1,0:T(8,128)(2,1)}, bf16[896,128]{1,0:T(8,128)(2,1)S(1)}, u32[]{:S(2)}, u32[]{:S(2)}) collective-permute-start(bf16[896,128]{1,0:T(8,128)(2,1)} %get-tuple-element.18), channel_id=1, source_target_pairs={{0,24},{4,28},{8,0},{12,4},{16,8},{20,12},{24,16},{28,20},{1,25},{... | collective-permute-start | bytes 688136 | tf_op jit(solution)/shard_map/ppermute | solution.py:497
  27.3 3.3 %collective-permute-done.1.refs_1_.refs_3_ = bf16[896,128]{1,0:T(8,128)(2,1)S(1)} collective-permute-done((bf16[896,128]{1,0:T(8,128)(2,1)}, bf16[896,128]{1,0:T(8,128)(2,1)S(1)}, u32[]{:S(2)}, u32[]{:S(2)}) %collective-permute-start.1) | collective-permute-done | bytes 229408 | tf_op jit(solution)/shard_map/ppermute | solution.py:497
  30.5 0.0 copy-start.1
  30.5 13.9 %collective-permute-done.2.refs_2_.refs_4_ = bf16[896,128]{1,0:T(8,128)(2,1)S(1)} collective-permute-done((bf16[896,128]{1,0:T(8,128)(2,1)}, bf16[896,128]{1,0:T(8,128)(2,1)S(1)}, u32[]{:S(2)}, u32[]{:S(2)}) %collective-permute-start.2) | collective-permute-done | bytes 229408 | tf_op jit(solution)/shard_map/ppermute | solution.py:497
  44.5 0.0 copy-start.2
  44.5 2.4 %collective-permute-done.3.refs_3_.refs_5_ = bf16[896,128]{1,0:T(8,128)(2,1)S(1)} collective-permute-done((bf16[896,128]{1,0:T(8,128)(2,1)}, bf16[896,128]{1,0:T(8,128)(2,1)S(1)}, u32[]{:S(2)}, u32[]{:S(2)}) %collective-permute-start.3) | collective-permute-done | bytes 229408 | tf_op jit(solution)/shard_map/ppermute | solution.py:497
  46.9 0.0 copy-start.3
  46.9 0.0 copy-done.1
  46.9 0.0 copy-done.2
  46.9 0.7 copy-done.3
  47.6 1.6 %unit_negatives.1 = bf16[128,512]{1,0:T(8,128)(2,1)} custom-call(bf16[896,128]{1,0:T(8,128)(2,1)} %get-tuple-element.15.refs_0_.refs_2_, bf16[896,128]{1,0:T(8,128)(2,1)} %copy-done.1, bf16[896,128]{1,0:T(8,128)(2,1)} %copy-done.2, bf16[896,128]{1,0:T(8,128)(2,1)} %copy-done.3), custom_call_target="tpu_custom_call" | custom-call | tf_op jit(solution)/shard_map/unit_negatives/pallas_call | solution.py:253
  49.2 1.2 %collective-permute-start.6 = (bf16[128,512]{1,0:T(8,128)(2,1)}, bf16[128,512]{1,0:T(8,128)(2,1)S(1)}, u32[]{:S(2)}, u32[]{:S(2)}) collective-permute-start(bf16[128,512]{1,0:T(8,128)(2,1)} %unit_negatives.1), channel_id=1, source_target_pairs={{0,3},{1,2},{2,1},{3,0},{4,7},{5,6},{6,5},{7,4},{8,11},{9,10},{10,... | collective-permute-start | bytes 393224 | tf_op jit(solution)/shard_map/ppermute | solution.py:503
  50.4 0.2 collective-permute-start.5
  50.6 1.2 %collective-permute-start.4 = (bf16[128,512]{1,0:T(8,128)(2,1)}, bf16[128,512]{1,0:T(8,128)(2,1)S(1)}, u32[]{:S(2)}, u32[]{:S(2)}) collective-permute-start(bf16[128,512]{1,0:T(8,128)(2,1)} %unit_negatives.1), channel_id=1, source_target_pairs={{0,1},{1,0},{2,3},{3,2},{4,5},{5,4},{6,7},{7,6},{8,9},{9,8},{10,11... | collective-permute-start | bytes 393224 | tf_op jit(solution)/shard_map/ppermute | solution.py:503
  51.8 3.0 %collective-permute-done.6 = bf16[128,512]{1,0:T(8,128)(2,1)S(1)} collective-permute-done((bf16[128,512]{1,0:T(8,128)(2,1)}, bf16[128,512]{1,0:T(8,128)(2,1)S(1)}, u32[]{:S(2)}, u32[]{:S(2)}) %collective-permute-start.6) | collective-permute-done | bytes 131104 | tf_op jit(solution)/shard_map/ppermute | solution.py:503
  54.9 3.6 %collective-permute-done.5 = bf16[128,512]{1,0:T(8,128)(2,1)S(1)} collective-permute-done((bf16[128,512]{1,0:T(8,128)(2,1)}, bf16[128,512]{1,0:T(8,128)(2,1)S(1)}, u32[]{:S(2)}, u32[]{:S(2)}) %collective-permute-start.5) | collective-permute-done | bytes 131104 | tf_op jit(solution)/shard_map/ppermute | solution.py:503
  58.5 0.0 collective-permute-done.4
  58.5 0.9 %pad_maximum_fusion.refs_2_ = bf16[512,512]{1,0:T(8,128)(2,1)S(1)} fusion(bf16[128,512]{1,0:T(8,128)(2,1)S(1)} %collective-permute-done.6, bf16[128,512]{1,0:T(8,128)(2,1)S(1)} %collective-permute-done.5, bf16[128,512]{1,0:T(8,128)(2,1)S(1)} %collective-permute-done.4, bf16[128,512]{1,0:T(8,128)(2,1)} %unit_negatives.1), kind=kLoop, calls=%fused_computation | loop fusion | flops 2097152 | bytes 1048576 | tf_op jit(solution)/shard_map/concatenate | solution.py:504
  59.5 0.0 copy-start
  59.5 0.7 collective-permute-start.7
  60.1 15.1 %layer.1 = (bf16[768,512]{1,0:T(8,128)(2,1)}, bf16[768,512]{1,0:T(8,128)(2,1)}) custom-call(s32[1,16]{1,0:T(1,128)} %refs_0_.3, s32[1,16]{1,0:T(1,128)} %refs_1_.5, bf16[896,128]{1,0:T(8,128)(2,1)} %get-tuple-element.15.refs_0_.refs_2_, bf16[896,128]{1,0:T(8,128)(2,1)} %copy-done.1, bf16[896,128]{1,0:T(8,128)(2,1)} %copy-done.2, bf16[896,128]{1,0:T(8,128)(2,1)} %copy-done.3, ...), custom_call_target="tpu_custom_call" | custom-call | tf_op jit(solution)/shard_map/layer/pallas_call | solution.py:403
  75.3 0.0 copy-done
  75.3 0.0 collective-permute-done.7.refs_3_
  75.3 0.0 copy-start.4
  75.3 0.8 copy-done.4
  76.1 7.2 %gradient.1 = f32[768,512]{1,0:T(8,128)} custom-call(s32[1,16]{1,0:T(1,128)} %refs_0_.3, s32[1,16]{1,0:T(1,128)} %refs_1_.5, bf16[512,512]{1,0:T(8,128)(2,1)} %copy-done, bf16[512,512]{1,0:T(8,128)(2,1)} %copy-done.4, bf16[768,512]{1,0:T(8,128)(2,1)} %get-tuple-element.19.refs_4_, bf16[768,512]{1,0:T(8,128)(2,1)} %get-tuple-element.20.refs_5_), custom_call_target="tpu_custom_call" | custom-call | tf_op jit(solution)/shard_map/gradient/pallas_call | solution.py:469
Async XLA Ops:
  18.2 2.3 %collective-permute-start = (bf16[1600,128]{1,0:T(8,128)(2,1)}, bf16[1600,128]{1,0:T(8,128)(2,1)S(1)}, u32[]{:S(2)}, u32[]{:S(2)}) collective-permute-start(bf16[1600,128]{1,0:T(8,128)(2,1)} %get-tuple-element.14), channel_id=1, source_target_pairs={{0,4},{4,0},{8,12},{12,8},{16,20},{20,16},{24,28},{28,24},{1,5},{5... | collective-permute-start | bytes 1228808 | tf_op jit(solution)/shard_map/ppermute | solution.py:493
  20.5 0.8 copy-start.5
  23.5 7.0 %collective-permute-start.1 = (bf16[896,128]{1,0:T(8,128)(2,1)}, bf16[896,128]{1,0:T(8,128)(2,1)S(1)}, u32[]{:S(2)}, u32[]{:S(2)}) collective-permute-start(bf16[896,128]{1,0:T(8,128)(2,1)} %get-tuple-element.16), channel_id=1, source_target_pairs={{0,8},{4,12},{8,16},{12,20},{16,24},{20,28},{24,0},{28,4},{1,9},{5... | collective-permute-start | bytes 688136 | tf_op jit(solution)/shard_map/ppermute | solution.py:497
  24.8 19.7 %collective-permute-start.2 = (bf16[896,128]{1,0:T(8,128)(2,1)}, bf16[896,128]{1,0:T(8,128)(2,1)S(1)}, u32[]{:S(2)}, u32[]{:S(2)}) collective-permute-start(bf16[896,128]{1,0:T(8,128)(2,1)} %get-tuple-element.17), channel_id=1, source_target_pairs={{0,16},{4,20},{8,24},{12,28},{16,0},{20,4},{24,8},{28,12},{1,17},{... | collective-permute-start | bytes 688136 | tf_op jit(solution)/shard_map/ppermute | solution.py:497
  25.8 21.1 %collective-permute-start.3 = (bf16[896,128]{1,0:T(8,128)(2,1)}, bf16[896,128]{1,0:T(8,128)(2,1)S(1)}, u32[]{:S(2)}, u32[]{:S(2)}) collective-permute-start(bf16[896,128]{1,0:T(8,128)(2,1)} %get-tuple-element.18), channel_id=1, source_target_pairs={{0,24},{4,28},{8,0},{12,4},{16,8},{20,12},{24,16},{28,20},{1,25},{... | collective-permute-start | bytes 688136 | tf_op jit(solution)/shard_map/ppermute | solution.py:497
  30.5 16.3 %copy-start.1 = (bf16[896,128]{1,0:T(8,128)(2,1)}, bf16[896,128]{1,0:T(8,128)(2,1)S(1)}, u32[]{:S(2)}) copy-start(bf16[896,128]{1,0:T(8,128)(2,1)S(1)} %collective-permute-done.1.refs_1_.refs_3_) | copy-start | bytes 688132
  44.5 2.4 %copy-start.2 = (bf16[896,128]{1,0:T(8,128)(2,1)}, bf16[896,128]{1,0:T(8,128)(2,1)S(1)}, u32[]{:S(2)}) copy-start(bf16[896,128]{1,0:T(8,128)(2,1)S(1)} %collective-permute-done.2.refs_2_.refs_4_) | copy-start | bytes 688132
  46.9 0.7 copy-start.3
  49.2 5.7 %collective-permute-start.6 = (bf16[128,512]{1,0:T(8,128)(2,1)}, bf16[128,512]{1,0:T(8,128)(2,1)S(1)}, u32[]{:S(2)}, u32[]{:S(2)}) collective-permute-start(bf16[128,512]{1,0:T(8,128)(2,1)} %unit_negatives.1), channel_id=1, source_target_pairs={{0,3},{1,2},{2,1},{3,0},{4,7},{5,6},{6,5},{7,4},{8,11},{9,10},{10,... | collective-permute-start | bytes 393224 | tf_op jit(solution)/shard_map/ppermute | solution.py:503
  50.4 8.1 %collective-permute-start.5 = (bf16[128,512]{1,0:T(8,128)(2,1)}, bf16[128,512]{1,0:T(8,128)(2,1)S(1)}, u32[]{:S(2)}, u32[]{:S(2)}) collective-permute-start(bf16[128,512]{1,0:T(8,128)(2,1)} %unit_negatives.1), channel_id=1, source_target_pairs={{0,2},{1,3},{2,0},{3,1},{4,6},{5,7},{6,4},{7,5},{8,10},{9,11},{10,... | collective-permute-start | bytes 393224 | tf_op jit(solution)/shard_map/ppermute | solution.py:503
  50.6 7.9 %collective-permute-start.4 = (bf16[128,512]{1,0:T(8,128)(2,1)}, bf16[128,512]{1,0:T(8,128)(2,1)S(1)}, u32[]{:S(2)}, u32[]{:S(2)}) collective-permute-start(bf16[128,512]{1,0:T(8,128)(2,1)} %unit_negatives.1), channel_id=1, source_target_pairs={{0,1},{1,0},{2,3},{3,2},{4,5},{5,4},{6,7},{7,6},{8,9},{9,8},{10,11... | collective-permute-start | bytes 393224 | tf_op jit(solution)/shard_map/ppermute | solution.py:503
  59.5 15.8 %copy-start = (bf16[512,512]{1,0:T(8,128)(2,1)}, bf16[512,512]{1,0:T(8,128)(2,1)S(1)}, u32[]{:S(2)}) copy-start(bf16[512,512]{1,0:T(8,128)(2,1)S(1)} %pad_maximum_fusion.refs_2_) | copy-start | bytes 1572868
  59.5 15.8 %collective-permute-start.7 = (bf16[512,512]{1,0:T(8,128)(2,1)S(1)}, bf16[512,512]{1,0:T(8,128)(2,1)S(1)}, u32[]{:S(2)}, u32[]{:S(2)}) collective-permute-start(bf16[512,512]{1,0:T(8,128)(2,1)S(1)} %pad_maximum_fusion.refs_2_), channel_id=1, source_target_pairs={{0,4},{4,0},{8,12},{12,8},{16,20},{20,16},{24,28},{28,24},{1,5},{5... | collective-permute-start | bytes 1572872 | tf_op jit(solution)/shard_map/ppermute | solution.py:505
  75.3 0.8 copy-start.4

commit v2 on v1

--- a/solution.py
+++ b/solution.py
@@ -21,12 +21,13 @@
 
 BF = jnp.bfloat16
 F32 = jnp.float32
-VMEM_BYTES = 60 * 1024 * 1024
 COPY_PARTS = 8
-
-
-def params():
-    return pltpu.CompilerParams(vmem_limit_bytes=VMEM_BYTES)
+GRADIENT_PAGES = 3
+QUERY_PAGES = 2
+
+
+def params(mebibytes):
+    return pltpu.CompilerParams(vmem_limit_bytes=mebibytes * 1024 * 1024)
 
 
 def smem():
@@ -99,11 +100,12 @@
 
         def turn(j, carry):
             at = pl.multiple_of(i * piece + j * LANES, LANES)
-            low = part_ref[:, pl.ds(at, LANES)].astype(F32)
-            high = part_ref[:, pl.ds(middle + at, LANES)].astype(F32)
-            turned = jnp.concatenate([low, high], axis=0).T
-            rows_ref[pl.ds(at, LANES), :] = turned
-            rows_ref[pl.ds(middle + at, LANES), :] = swap_halves(turned)
+            low = part_ref[:, pl.ds(at, LANES)]
+            high = part_ref[:, pl.ds(middle + at, LANES)]
+            rows_ref[pl.ds(at, LANES), :] = jnp.concatenate([low, high], axis=0).T.astype(F32)
+            rows_ref[pl.ds(middle + at, LANES), :] = jnp.concatenate([high, low], axis=0).T.astype(
+                F32
+            )
             return carry
 
         lax.fori_loop(0, piece // LANES, turn, 0, unroll=4)
@@ -189,7 +191,7 @@
             pltpu.SMEM((tables,), jnp.int32),
             pltpu.SemaphoreType.DMA((2, COPY_PARTS)),
         ],
-        compiler_params=params(),
+        compiler_params=params(32),
         name="gather_rows",
     )(item_table.T, event_ids, negative_ids, seq_lengths, seq_owner)
     return outs[: len(chunks)], outs[len(chunks) :]
@@ -227,7 +229,7 @@
         out_shape=[shape] * chips,
         in_specs=[vmem(), vmem()],
         out_specs=[vmem()] * chips,
-        compiler_params=params(),
+        compiler_params=params(12),
         name="merge_columns",
     )(keep, got)
 
@@ -257,7 +259,7 @@
         in_specs=[spec] * chips,
         out_specs=pl.BlockSpec((neg_rows, chips * lanes), lambda i: (0, 0)),
         scratch_shapes=[spare_blocks(chips, neg_rows, lanes)],
-        compiler_params=params(),
+        compiler_params=params(8),
         name="unit_negatives",
     )(*blocks)
 
@@ -340,20 +342,21 @@
     scale = 1.0 / math.sqrt(head_width)
     row_at = lax.broadcasted_iota(jnp.int32, (PAGE, PAGE), 0)
     causal = lane_ids((PAGE, PAGE)) <= row_at
-    for p in range(pages):
-        whole = first + p
-        part = slice(p * PAGE, (p + 1) * PAGE)
-        inverse = jnp.where(
-            segment[whole] >= 0, 1.0 / jnp.full((1, PAGE), length[whole], jnp.int32).astype(F32), 0.0
+    inverses = [
+        jnp.where(
+            segment[p] >= 0, 1.0 / jnp.full((1, PAGE), length[p], jnp.int32).astype(F32), 0.0
         )
-        factors = [
-            jnp.where(segment[c] == segment[whole], inverse, 0.0) for c in range(whole)
-        ]
+        for p in range(first + pages)
+    ]
+    for group in range(0, pages, QUERY_PAGES):
+        inside = range(group, min(group + QUERY_PAGES, pages))
+        part = slice(group * PAGE, (inside[-1] + 1) * PAGE)
+        upto = (inside[-1] + 1) * PAGE
         for h in range(HEADS):
             low = h * head_width
             query = proj_ref[part, 2 * width + low : 2 * width + low + head_width]
-            keys = proj_ref[0 : (p + 1) * PAGE, 3 * width + low : 3 * width + low + head_width]
-            values = proj_ref[0 : (p + 1) * PAGE, width + low : width + low + head_width]
+            keys = proj_ref[0:upto, 3 * width + low : 3 * width + low + head_width]
+            values = proj_ref[0:upto, width + low : width + low + head_width]
             if first:
                 keys = jnp.concatenate(
                     [prior_ref[:, width + low : width + low + head_width], keys], axis=0
@@ -362,14 +365,24 @@
             scores = lax.dot_general(
                 query, keys, (((1,), (1,)), ((), ())), preferred_element_type=F32
             )
-            weights = []
-            for c in range(whole + 1):
-                score = silu(scores[:, c * PAGE : (c + 1) * PAGE] * scale)
-                if c < whole:
-                    weights.append((score * factors[c]).astype(BF))
-                else:
-                    weights.append(jnp.where(causal, score * inverse, 0.0).astype(BF))
-            weights = weights[0] if whole == 0 else jnp.concatenate(weights, axis=1)
+            rows = []
+            for i, p in enumerate(inside):
+                whole = first + p
+                row = []
+                for c in range(first + inside[-1] + 1):
+                    if c > whole:
+                        row.append(jnp.zeros((PAGE, PAGE), BF))
+                        continue
+                    score = silu(
+                        scores[i * PAGE : (i + 1) * PAGE, c * PAGE : (c + 1) * PAGE] * scale
+                    )
+                    if c < whole:
+                        factor = jnp.where(segment[c] == segment[whole], inverses[whole], 0.0)
+                        row.append((score * factor).astype(BF))
+                    else:
+                        row.append(jnp.where(causal, score * inverses[whole], 0.0).astype(BF))
+                rows.append(row[0] if len(row) == 1 else jnp.concatenate(row, axis=1))
+            weights = rows[0] if len(rows) == 1 else jnp.concatenate(rows, axis=0)
             att_ref[part, low : low + head_width] = jnp.dot(
                 weights, values, preferred_element_type=F32
             )
@@ -413,7 +426,7 @@
             spare_blocks(chips, rows, lanes),
             pltpu.SemaphoreType.DMA((4,)),
         ],
-        compiler_params=params(),
+        compiler_params=params(32),
         name="layer",
     )(*operands)
 
@@ -439,17 +452,21 @@
     row_at = lax.broadcasted_iota(jnp.int32, (PAGE, 1), 0)
     at = 0
     for ref in unit_refs:
-        for low in range(0, ref.shape[0], PAGE):
-            page = at // PAGE
-            unit = ref[low : low + PAGE, :]
+        size = GRADIENT_PAGES * PAGE
+        for low in range(0, ref.shape[0], size):
+            count_pages = min(size, ref.shape[0] - low) // PAGE
+            block = count_pages * PAGE
+            unit = ref[low : low + block, :]
             scores = lax.dot_general(
                 unit, negatives, (((1,), (1,)), ((), ())), preferred_element_type=F32
             )
-            targets = next_ref[at + 1 : at + 1 + PAGE, :]
-            last_row = jnp.where(segment[page + 1] == segment[page], PAGE, PAGE - 1)
-            limit = jnp.where(segment[page] >= 0, last_row, 0)
-            has_next = row_at < limit
-            targets = jnp.where(has_next, targets, 0.0)
+            limits = []
+            for page in range(at // PAGE, at // PAGE + count_pages):
+                last_row = jnp.where(segment[page + 1] == segment[page], PAGE, PAGE - 1)
+                limit = jnp.where(segment[page] >= 0, last_row, 0)
+                limits.append((row_at < limit).astype(F32))
+            has_next = (limits[0] if count_pages == 1 else jnp.concatenate(limits, axis=0)) > 0.5
+            targets = jnp.where(has_next, next_ref[at + 1 : at + 1 + block, :], 0.0)
             positive = jnp.exp(
                 jnp.sum(unit.astype(F32) * targets, axis=1, keepdims=True) * sharp
             )
@@ -459,8 +476,8 @@
             probs = (powers * inverse).astype(BF)
             grad = jnp.dot(probs, negatives, preferred_element_type=F32)
             grad = (grad + (positive * inverse - 1.0) * targets) * sharp
-            out_ref[at : at + PAGE, :] = jnp.where(has_next, grad, 0.0)
-            at += PAGE
+            out_ref[at : at + block, :] = jnp.where(has_next, grad, 0.0)
+            at += block
 
 
 def gradient(seq_lengths, seq_owner, near, far, units, items):
@@ -472,7 +489,7 @@
         in_specs=[smem(), smem()] + [vmem()] * (2 + 2 * len(units)),
         out_specs=vmem(),
         scratch_shapes=[pltpu.VMEM((2 * half, width), BF), pltpu.VMEM((rows + 8, width), F32)],
-        compiler_params=params(),
+        compiler_params=params(28),
         name="gradient",
     )(seq_lengths, seq_owner, near, far, *units, *items)
 

time: 83.7 us -> 69.3 us (0.83)
  Pallas kernels: 44.4 us -> 28.8 us
  local copies, waits for them, and re-layouts: 2.26 us -> 4.91 us
  other arithmetic: 0.94 us -> 0.03 us
    pallas_call x1, Pallas kernels: 18.2 us -> 12.9 us  [gather_rows(): pl.pallas_call(functools.partial(gather_kernel, tables, chunks), out_shap...]
    pallas_call x1, Pallas kernels: 15.1 us -> 11.2 us  [layer(): pl.pallas_call(functools.partial(layer_kernel, chips, first, pages, last)...]
    pallas_call x1, Pallas kernels: 7.2 us -> 4.22 us  [gradient(): pl.pallas_call(functools.partial(gradient_kernel, len(units)), out_shape=...]
    unnamed x12 -> x18, local copies, waits for them, and re-layouts: 2.26 us -> 4.91 us
    pallas_call x1, Pallas kernels: 2.25 us -> 0.25 us  [merge_columns(): pl.pallas_call(functools.partial(merge_kernel, chips, pages, neg_half), o...]
    pallas_call x1, Pallas kernels: 1.62 us -> 0.16 us  [unit_negatives(): pl.pallas_call(functools.partial(unit_negatives_kernel, chips), grid=(1,)...]
    concatenate x1, other arithmetic: 0.94 us -> 0.03 us  [on_device(): near = jnp.concatenate(parts, axis=0)]
  transfers between devices with their start and end apart: 8 -> 8, of which waited for: 6 -> 6; matrix products, arithmetic and copies ran while one was open for 0% -> 0% of each run, Pallas kernels for 18% -> 16%
where the time goes in v2:
time: 69.3 us; the launch traced here: 69 us
  Pallas kernels  28.8 us (42%)
  waiting for transfers between devices  27.2 us (39%)
  starting transfers between devices  7.95 us (11%)
  local copies, waits for them, and re-layouts  4.91 us (7%)
    ppermute x3, waiting for transfers between devices, on_device(): blocks[s] = lax.ppermute(blocks[s], 'table', moves)  19.4 us
    pallas_call x1, Pallas kernels, gather_rows(): pl.pallas_call(functools.partial(gather_kernel, tables, chunks), out_shap...  12.9 us
    pallas_call x1, Pallas kernels, layer(): pl.pallas_call(functools.partial(layer_kernel, chips, first, pages, last)...  11.2 us
    ppermute x3, waiting for transfers between devices, on_device(): parts.append(lax.ppermute(own, 'user', [(u, u ^ s) for u in range(users)]))  6.48 us
    unnamed x18, local copies, waits for them, and re-layouts  4.91 us
    pallas_call x1, Pallas kernels, gradient(): pl.pallas_call(functools.partial(gradient_kernel, len(units)), out_shape=...  4.22 us
    ppermute x3, starting transfers between devices, on_device(): blocks[s] = lax.ppermute(blocks[s], 'table', moves)  3.83 us
    ppermute x3, starting transfers between devices, on_device(): parts.append(lax.ppermute(own, 'user', [(u, u ^ s) for u in range(users)]))  2.71 us
  transfers between devices with their start and end apart: 8, of which 6 were waited for; matrix products, arithmetic and copies ran while one was open for 0% of the time, Pallas kernels for 16%

profile of v2, /device:TPU:11, one launch (start us, length us, event | category | flops | bytes accessed | tf_op | source)
XLA Modules:
  0.0 69.0 jit_solution(13131441005737351311)
XLA Ops:
  0.0 0.0 copy-start
  0.0 2.2 %copy-done = bf16[32768,64]{0,1:T(8,128)(2,1)S(1)} copy-done((bf16[32768,64]{0,1:T(8,128)(2,1)S(1)}, bf16[32768,64]{0,1:T(8,128)(2,1)}, u32[]{:S(2)}) %copy-start) | copy-done | bytes 4194328
  2.2 0.0 copy-start.5
  2.2 0.7 %copy-done.5 = s32[4096]{0:T(1024)S(1)} copy-done((s32[4096]{0:T(1024)S(1)}, s32[4096]{0:T(1024)}, u32[]{:S(2)}) %copy-start.5) | copy-done | bytes 16408
  2.9 0.0 copy-start.6
  2.9 0.7 copy-done.6
  3.6 0.0 copy-start.7
  3.6 0.7 copy-done.7
  4.2 0.0 copy-start.8
  4.2 0.7 copy-done.8
  4.9 0.0 copy-start.2
  4.9 0.0 copy-start.3
  4.9 12.9 %gather_rows.1 = (bf16[1600,128]{1,0:T(8,128)(2,1)S(1)}, bf16[1600,128]{1,0:T(8,128)(2,1)S(1)}) custom-call(bf16[64,32768]{1,0:T(8,128)(2,1)S(1)} %bitcast.1, s32[4096]{0:T(1024)S(1)} %copy-done.5, s32[256]{0:T(256)S(1)} %copy-done.8, s32[1,16]{1,0:T(1,128)S(1)} %copy-done.6, s32[1,16]{1,0:T(1,128)S(1)} %copy-done.7), custom_call_target="tpu_custom_call" | custom-call | tf_op jit(solution)/shard_map/gather_rows/pallas_call | solution.py:182
  17.8 0.0 copy-start.1
  17.8 0.0 copy-start.4
  17.9 0.7 %collective-permute-start = (bf16[1600,128]{1,0:T(8,128)(2,1)S(1)}, bf16[1600,128]{1,0:T(8,128)(2,1)S(1)}, u32[]{:S(2)}, u32[]{:S(2)}) collective-permute-start(bf16[1600,128]{1,0:T(8,128)(2,1)S(1)} %get-tuple-element.14), channel_id=1, source_target_pairs={{0,4},{4,0},{8,12},{12,8},{16,20},{20,16},{24,28},{28,24},{1,5},{5... | collective-permute-start | bytes 1228808 | tf_op jit(solution)/shard_map/ppermute | solution.py:510
  18.6 1.4 %collective-permute-done.got_ref = bf16[1600,128]{1,0:T(8,128)(2,1)S(1)} collective-permute-done((bf16[1600,128]{1,0:T(8,128)(2,1)S(1)}, bf16[1600,128]{1,0:T(8,128)(2,1)S(1)}, u32[]{:S(2)}, u32[]{:S(2)}) %collective-permute-start) | collective-permute-done | bytes 409632 | tf_op jit(solution)/shard_map/ppermute | solution.py:510
  20.0 0.3 merge_columns.1
  20.2 1.3 %collective-permute-start.1 = (bf16[896,128]{1,0:T(8,128)(2,1)S(1)}, bf16[896,128]{1,0:T(8,128)(2,1)S(1)}, u32[]{:S(2)}, u32[]{:S(2)}) collective-permute-start(bf16[896,128]{1,0:T(8,128)(2,1)S(1)} %get-tuple-element.16), channel_id=1, source_target_pairs={{0,8},{4,12},{8,16},{12,20},{16,24},{20,28},{24,0},{28,4},{1,9},{5... | collective-permute-start | bytes 688136 | tf_op jit(solution)/shard_map/ppermute | solution.py:514
  21.6 1.1 %collective-permute-start.2 = (bf16[896,128]{1,0:T(8,128)(2,1)S(1)}, bf16[896,128]{1,0:T(8,128)(2,1)S(1)}, u32[]{:S(2)}, u32[]{:S(2)}) collective-permute-start(bf16[896,128]{1,0:T(8,128)(2,1)S(1)} %get-tuple-element.17), channel_id=1, source_target_pairs={{0,16},{4,20},{8,24},{12,28},{16,0},{20,4},{24,8},{28,12},{1,17},{... | collective-permute-start | bytes 688136 | tf_op jit(solution)/shard_map/ppermute | solution.py:514
  22.7 1.4 %collective-permute-start.3 = (bf16[896,128]{1,0:T(8,128)(2,1)S(1)}, bf16[896,128]{1,0:T(8,128)(2,1)S(1)}, u32[]{:S(2)}, u32[]{:S(2)}) collective-permute-start(bf16[896,128]{1,0:T(8,128)(2,1)S(1)} %get-tuple-element.18), channel_id=1, source_target_pairs={{0,24},{4,28},{8,0},{12,4},{16,8},{20,12},{24,16},{28,20},{1,25},{... | collective-permute-start | bytes 688136 | tf_op jit(solution)/shard_map/ppermute | solution.py:514
  24.1 3.0 %collective-permute-done.1.refs_1_.refs_3_ = bf16[896,128]{1,0:T(8,128)(2,1)S(1)} collective-permute-done((bf16[896,128]{1,0:T(8,128)(2,1)S(1)}, bf16[896,128]{1,0:T(8,128)(2,1)S(1)}, u32[]{:S(2)}, u32[]{:S(2)}) %collective-permute-start.1) | collective-permute-done | bytes 229408 | tf_op jit(solution)/shard_map/ppermute | solution.py:514
  27.1 13.8 %collective-permute-done.2.refs_2_.refs_4_ = bf16[896,128]{1,0:T(8,128)(2,1)S(1)} collective-permute-done((bf16[896,128]{1,0:T(8,128)(2,1)S(1)}, bf16[896,128]{1,0:T(8,128)(2,1)S(1)}, u32[]{:S(2)}, u32[]{:S(2)}) %collective-permute-start.2) | collective-permute-done | bytes 229408 | tf_op jit(solution)/shard_map/ppermute | solution.py:514
  40.9 2.5 %collective-permute-done.3.refs_3_.refs_5_ = bf16[896,128]{1,0:T(8,128)(2,1)S(1)} collective-permute-done((bf16[896,128]{1,0:T(8,128)(2,1)S(1)}, bf16[896,128]{1,0:T(8,128)(2,1)S(1)}, u32[]{:S(2)}, u32[]{:S(2)}) %collective-permute-start.3) | collective-permute-done | bytes 229408 | tf_op jit(solution)/shard_map/ppermute | solution.py:514
  43.4 0.2 unit_negatives.1
  43.6 1.3 %collective-permute-start.6 = (bf16[128,512]{1,0:T(8,128)(2,1)S(1)}, bf16[128,512]{1,0:T(8,128)(2,1)S(1)}, u32[]{:S(2)}, u32[]{:S(2)}) collective-permute-start(bf16[128,512]{1,0:T(8,128)(2,1)S(1)} %unit_negatives.1), channel_id=1, source_target_pairs={{0,3},{1,2},{2,1},{3,0},{4,7},{5,6},{6,5},{7,4},{8,11},{9,10},{10,... | collective-permute-start | bytes 393224 | tf_op jit(solution)/shard_map/ppermute | solution.py:520
  44.9 0.2 collective-permute-start.5
  45.1 1.2 %collective-permute-start.4 = (bf16[128,512]{1,0:T(8,128)(2,1)S(1)}, bf16[128,512]{1,0:T(8,128)(2,1)S(1)}, u32[]{:S(2)}, u32[]{:S(2)}) collective-permute-start(bf16[128,512]{1,0:T(8,128)(2,1)S(1)} %unit_negatives.1), channel_id=1, source_target_pairs={{0,1},{1,0},{2,3},{3,2},{4,5},{5,4},{6,7},{7,6},{8,9},{9,8},{10,11... | collective-permute-start | bytes 393224 | tf_op jit(solution)/shard_map/ppermute | solution.py:520
  46.3 2.8 %collective-permute-done.6 = bf16[128,512]{1,0:T(8,128)(2,1)S(1)} collective-permute-done((bf16[128,512]{1,0:T(8,128)(2,1)S(1)}, bf16[128,512]{1,0:T(8,128)(2,1)S(1)}, u32[]{:S(2)}, u32[]{:S(2)}) %collective-permute-start.6) | collective-permute-done | bytes 131104 | tf_op jit(solution)/shard_map/ppermute | solution.py:520
  49.1 3.6 %collective-permute-done.5 = bf16[128,512]{1,0:T(8,128)(2,1)S(1)} collective-permute-done((bf16[128,512]{1,0:T(8,128)(2,1)S(1)}, bf16[128,512]{1,0:T(8,128)(2,1)S(1)}, u32[]{:S(2)}, u32[]{:S(2)}) %collective-permute-start.5) | collective-permute-done | bytes 131104 | tf_op jit(solution)/shard_map/ppermute | solution.py:520
  52.8 0.0 collective-permute-done.4
  52.8 0.7 collective-permute-start.7
  53.5 0.0 copy-done.2
  53.5 0.0 copy-done.3
  53.5 0.0 copy-done.1
  53.5 0.0 copy-done.4
  53.5 11.2 %layer.1 = (bf16[768,512]{1,0:T(8,128)(2,1)S(1)}, bf16[768,512]{1,0:T(8,128)(2,1)S(1)}) custom-call(s32[1,16]{1,0:T(1,128)S(1)} %copy-done.6, s32[1,16]{1,0:T(1,128)S(1)} %copy-done.7, bf16[896,128]{1,0:T(8,128)(2,1)S(1)} %get-tuple-element.15.refs_0_.refs_2_, bf16[896,128]{1,0:T(8,128)(2,1)S(1)} %collective-permute-done.1.refs_1_.refs_3_, ...), custom_call_target="tpu_custom_call" | custom-call | tf_op jit(solution)/shard_map/layer/pallas_call | solution.py:416
  64.8 0.0 collective-permute-done.7.refs_3_
  64.8 4.2 %gradient.1 = f32[768,512]{1,0:T(8,128)} custom-call(s32[1,16]{1,0:T(1,128)S(1)} %copy-done.6, s32[1,16]{1,0:T(1,128)S(1)} %copy-done.7, bf16[512,512]{1,0:T(8,128)(2,1)S(1)} %pad_maximum_fusion.refs_2_, bf16[512,512]{1,0:T(8,128)(2,1)S(1)} %collective-permute-done.7.refs_3_, bf16[768,512]{1,0:T(8,128)(2,1)S(1)} %get-tuple-element.19.refs_4_, ...), custom_call_target="tpu_custom_call" | custom-call | tf_op jit(solution)/shard_map/gradient/pallas_call | solution.py:486
  (1 shorter events, 0.0 us)
Async XLA Ops:
  0.0 2.2 %copy-start = (bf16[32768,64]{0,1:T(8,128)(2,1)S(1)}, bf16[32768,64]{0,1:T(8,128)(2,1)}, u32[]{:S(2)}) copy-start(bf16[32768,64]{0,1:T(8,128)(2,1)} %param.9) | copy-start | bytes 12582916
  2.2 0.7 %copy-start.5 = (s32[4096]{0:T(1024)S(1)}, s32[4096]{0:T(1024)}, u32[]{:S(2)}) copy-start(s32[4096]{0:T(1024)} %refs_1_.3) | copy-start | bytes 49156
  2.9 0.7 copy-start.6
  3.6 0.7 copy-start.7
  4.2 0.7 copy-start.8
  4.9 48.6 %copy-start.2 = (bf16[2048,512]{1,0:T(8,128)(2,1)S(1)}, bf16[2048,512]{1,0:T(8,128)(2,1)}, u32[]{:S(2)}) copy-start(bf16[2048,512]{1,0:T(8,128)(2,1)} %refs_7_.1) | copy-start | bytes 6291460
  4.9 48.6 %copy-start.3 = (bf16[512,2048]{1,0:T(8,128)(2,1)S(1)}, bf16[512,2048]{1,0:T(8,128)(2,1)}, u32[]{:S(2)}) copy-start(bf16[512,2048]{1,0:T(8,128)(2,1)} %refs_8_.1) | copy-start | bytes 6291460
  17.8 35.7 %copy-start.1 = (bf16[512,2048]{1,0:T(8,128)(2,1)S(1)}, bf16[512,2048]{1,0:T(8,128)(2,1)}, u32[]{:S(2)}) copy-start(bf16[512,2048]{1,0:T(8,128)(2,1)} %refs_6_.1) | copy-start | bytes 6291460
  17.8 35.7 %copy-start.4 = (bf16[512,512]{1,0:T(8,128)(2,1)S(1)}, bf16[512,512]{1,0:T(8,128)(2,1)}, u32[]{:S(2)}) copy-start(bf16[512,512]{1,0:T(8,128)(2,1)} %refs_9_.1) | copy-start | bytes 1572868
  17.9 2.1 %collective-permute-start = (bf16[1600,128]{1,0:T(8,128)(2,1)S(1)}, bf16[1600,128]{1,0:T(8,128)(2,1)S(1)}, u32[]{:S(2)}, u32[]{:S(2)}) collective-permute-start(bf16[1600,128]{1,0:T(8,128)(2,1)S(1)} %get-tuple-element.14), channel_id=1, source_target_pairs={{0,4},{4,0},{8,12},{12,8},{16,20},{20,16},{24,28},{28,24},{1,5},{5... | collective-permute-start | bytes 1228808 | tf_op jit(solution)/shard_map/ppermute | solution.py:510
  20.2 6.9 %collective-permute-start.1 = (bf16[896,128]{1,0:T(8,128)(2,1)S(1)}, bf16[896,128]{1,0:T(8,128)(2,1)S(1)}, u32[]{:S(2)}, u32[]{:S(2)}) collective-permute-start(bf16[896,128]{1,0:T(8,128)(2,1)S(1)} %get-tuple-element.16), channel_id=1, source_target_pairs={{0,8},{4,12},{8,16},{12,20},{16,24},{20,28},{24,0},{28,4},{1,9},{5... | collective-permute-start | bytes 688136 | tf_op jit(solution)/shard_map/ppermute | solution.py:514
  21.6 19.4 %collective-permute-start.2 = (bf16[896,128]{1,0:T(8,128)(2,1)S(1)}, bf16[896,128]{1,0:T(8,128)(2,1)S(1)}, u32[]{:S(2)}, u32[]{:S(2)}) collective-permute-start(bf16[896,128]{1,0:T(8,128)(2,1)S(1)} %get-tuple-element.17), channel_id=1, source_target_pairs={{0,16},{4,20},{8,24},{12,28},{16,0},{20,4},{24,8},{28,12},{1,17},{... | collective-permute-start | bytes 688136 | tf_op jit(solution)/shard_map/ppermute | solution.py:514
  22.7 20.8 %collective-permute-start.3 = (bf16[896,128]{1,0:T(8,128)(2,1)S(1)}, bf16[896,128]{1,0:T(8,128)(2,1)S(1)}, u32[]{:S(2)}, u32[]{:S(2)}) collective-permute-start(bf16[896,128]{1,0:T(8,128)(2,1)S(1)} %get-tuple-element.18), channel_id=1, source_target_pairs={{0,24},{4,28},{8,0},{12,4},{16,8},{20,12},{24,16},{28,20},{1,25},{... | collective-permute-start | bytes 688136 | tf_op jit(solution)/shard_map/ppermute | solution.py:514
  43.6 5.5 %collective-permute-start.6 = (bf16[128,512]{1,0:T(8,128)(2,1)S(1)}, bf16[128,512]{1,0:T(8,128)(2,1)S(1)}, u32[]{:S(2)}, u32[]{:S(2)}) collective-permute-start(bf16[128,512]{1,0:T(8,128)(2,1)S(1)} %unit_negatives.1), channel_id=1, source_target_pairs={{0,3},{1,2},{2,1},{3,0},{4,7},{5,6},{6,5},{7,4},{8,11},{9,10},{10,... | collective-permute-start | bytes 393224 | tf_op jit(solution)/shard_map/ppermute | solution.py:520
  44.9 7.9 %collective-permute-start.5 = (bf16[128,512]{1,0:T(8,128)(2,1)S(1)}, bf16[128,512]{1,0:T(8,128)(2,1)S(1)}, u32[]{:S(2)}, u32[]{:S(2)}) collective-permute-start(bf16[128,512]{1,0:T(8,128)(2,1)S(1)} %unit_negatives.1), channel_id=1, source_target_pairs={{0,2},{1,3},{2,0},{3,1},{4,6},{5,7},{6,4},{7,5},{8,10},{9,11},{10,... | collective-permute-start | bytes 393224 | tf_op jit(solution)/shard_map/ppermute | solution.py:520
  45.1 7.7 %collective-permute-start.4 = (bf16[128,512]{1,0:T(8,128)(2,1)S(1)}, bf16[128,512]{1,0:T(8,128)(2,1)S(1)}, u32[]{:S(2)}, u32[]{:S(2)}) collective-permute-start(bf16[128,512]{1,0:T(8,128)(2,1)S(1)} %unit_negatives.1), channel_id=1, source_target_pairs={{0,1},{1,0},{2,3},{3,2},{4,5},{5,4},{6,7},{7,6},{8,9},{9,8},{10,11... | collective-permute-start | bytes 393224 | tf_op jit(solution)/shard_map/ppermute | solution.py:520
  52.8 11.9 %collective-permute-start.7 = (bf16[512,512]{1,0:T(8,128)(2,1)S(1)}, bf16[512,512]{1,0:T(8,128)(2,1)S(1)}, u32[]{:S(2)}, u32[]{:S(2)}) collective-permute-start(bf16[512,512]{1,0:T(8,128)(2,1)S(1)} %pad_maximum_fusion.refs_2_), channel_id=1, source_target_pairs={{0,4},{4,0},{8,12},{12,8},{16,20},{20,16},{24,28},{28,24},{1,5},{5... | collective-permute-start | bytes 1572872 | tf_op jit(solution)/shard_map/ppermute | solution.py:522

commit v3 on v2

--- a/solution.py
+++ b/solution.py
@@ -12,7 +12,7 @@
 PAGE = 128
 HALF = PAGE // 2
 CAP_PAGES = 6
-CHUNKS = (6,)
+CHUNKS = (3, 3)
 LANES = 128
 
 SCORE_SHARPNESS = 0.02
@@ -23,6 +23,7 @@
 F32 = jnp.float32
 COPY_PARTS = 8
 GRADIENT_PAGES = 3
+LAYER_COST = 24
 QUERY_PAGES = 2
 
 
@@ -30,6 +31,28 @@
     return pltpu.CompilerParams(vmem_limit_bytes=mebibytes * 1024 * 1024)
 
 
+def run(kernel, operands, in_specs, out_shape, scratch, mebibytes, name, after=(), flops=0):
+    count = len(operands)
+
+    def body(*refs):
+        kernel(*refs[:count], *refs[count + len(after) :])
+
+    return pl.pallas_call(
+        body,
+        out_shape=out_shape,
+        in_specs=in_specs + [anywhere()] * len(after),
+        out_specs=[vmem()] * len(out_shape),
+        scratch_shapes=scratch,
+        compiler_params=params(mebibytes),
+        name=name,
+        cost_estimate=pl.CostEstimate(flops=flops, transcendentals=0, bytes_accessed=flops // 300),
+    )(*operands, *after)
+
+
+def stay(array):
+    return pltpu.with_memory_space_constraint(array, pltpu.HBM)
+
+
 def smem():
     return pl.BlockSpec(memory_space=pltpu.SMEM)
 
@@ -39,6 +62,10 @@
 
 
 def hbm():
+    return pl.BlockSpec(memory_space=pltpu.HBM)
+
+
+def anywhere():
     return pl.BlockSpec(memory_space=pl.ANY)
 
 
@@ -73,18 +100,8 @@
     return lax.broadcasted_iota(jnp.int32, shape, len(shape) - 1)
 
 
-def gather_kernel(tables, chunks, *refs):
-    table_ref, ids_ref, neg_ref, len_ref, own_ref = refs[:5]
-    count = len(chunks)
-    keep_refs = refs[5 : 5 + count]
-    give_refs = refs[5 + count : 5 + 2 * count]
-    part_ref, rows_ref, stage_ref, next_ref, sem = refs[5 + 2 * count :]
-    me = lax.axis_index("table")
-    core = me % 2
-    chip = me // 2
-    chips = tables // 2
-    width, vocab = table_ref.shape
-    middle = vocab // 2
+def turn_table(table_ref, part_ref, rows_ref, sem):
+    middle = table_ref.shape[1] // 2
     piece = middle // COPY_PARTS
 
     def copy(side, i):
@@ -110,9 +127,33 @@
 
         lax.fori_loop(0, piece // LANES, turn, 0, unroll=4)
 
+
+def gather_kernel(tables, start, size, negatives, *refs):
+    ids_in, len_in, own_in = refs[:3]
+    if negatives:
+        neg_in, table_ref, rows_ref, keep_ref, give_ref = refs[3:8]
+    else:
+        rows_ref, keep_ref, give_ref = refs[3:6]
+    ids_ref, len_ref, own_ref, neg_ref, stage_ref, next_ref, small_sem = refs[-7:]
+    smalls = [(ids_in, ids_ref), (len_in, len_ref), (own_in, own_ref)]
+    if negatives:
+        smalls.append((neg_in, neg_ref))
+    copies = [pltpu.make_async_copy(a, b, small_sem.at[i]) for i, (a, b) in enumerate(smalls)]
+    for c in copies:
+        c.start()
+    if negatives:
+        turn_table(table_ref, refs[-9], rows_ref, refs[-8])
+    for c in copies:
+        c.wait()
+    me = lax.axis_index("table")
+    core = me % 2
+    chip = me // 2
+    chips = tables // 2
+    vocab, lanes = rows_ref.shape
+    middle = vocab // 2
     first_xor = core * middle
     second_xor = middle - first_xor
-    own_lanes = (lane_ids((1, 2 * width)) < width) == (core == 0)
+    own_lanes = (lane_ids((1, lanes)) < lanes // 2) == (core == 0)
 
     def fetch(source, base, half):
         def step(j, carry):
@@ -126,14 +167,15 @@
                 stage_ref[pl.ds(at + k, 1), :] = picked
             return carry
 
-        lax.fori_loop(0, half // 8, step, 0)
+        lax.fori_loop(0, half // 8, step, 0, unroll=2)
         return stage_ref[0:half, :].astype(BF)
 
-    neg_rows = neg_ref.shape[0] // 2
-    neg_half = neg_rows // 2
-    neg_at = chips * chunks[0] * HALF
-    keep_refs[0][neg_at : neg_at + neg_half, :] = fetch(neg_ref, core * neg_rows, neg_half)
-    give_refs[0][neg_at : neg_at + neg_half, :] = fetch(neg_ref, (1 - core) * neg_rows, neg_half)
+    if negatives:
+        neg_rows = neg_ref.shape[0] // 2
+        neg_half = neg_rows // 2
+        neg_at = chips * size * HALF
+        keep_ref[neg_at : neg_at + neg_half, :] = fetch(neg_ref, core * neg_rows, neg_half)
+        give_ref[neg_at : neg_at + neg_half, :] = fetch(neg_ref, (1 - core) * neg_rows, neg_half)
 
     for t in range(tables):
         next_ref[t] = 0
@@ -146,55 +188,60 @@
         shift = lax.rem(owner // 2 - chip + chips, chips)
         mine = owner % 2 == core
 
-        def one_page(j, carry):
-            block = fetch(ids_ref, (page + j) * PAGE, HALF)
-            slot = slot0 + j
-            start = 0
-            for c, size in enumerate(chunks):
-                inside = (slot >= start) & (slot < start + size)
-                at = pl.multiple_of((shift * size + slot - start) * HALF, HALF)
-
-                @pl.when(inside & mine)
-                def _():
-                    keep_refs[c][pl.ds(at, HALF), :] = block
-
-                @pl.when(inside & jnp.logical_not(mine))
-                def _():
-                    give_refs[c][pl.ds(at, HALF), :] = block
-
-                start += size
+        def one_page(slot, carry):
+            block = fetch(ids_ref, (page + slot - slot0) * PAGE, HALF)
+            at = pl.multiple_of((shift * size + slot - start) * HALF, HALF)
+
+            @pl.when(mine)
+            def _():
+                keep_ref[pl.ds(at, HALF), :] = block
+
+            @pl.when(jnp.logical_not(mine))
+            def _():
+                give_ref[pl.ds(at, HALF), :] = block
+
             return carry
 
-        lax.fori_loop(0, pages, one_page, 0)
+        low = jnp.maximum(slot0, start)
+        high = jnp.minimum(slot0 + pages, start + size)
+        lax.fori_loop(low, high, one_page, 0)
         return page + pages
 
     lax.fori_loop(0, len_ref.shape[1], sequence, 0)
 
 
-def gather_rows(item_table, event_ids, negative_ids, seq_lengths, seq_owner, tables, chunks):
-    vocab, width = item_table.shape
+def gather_rows(event_ids, seq_lengths, seq_owner, negative_ids, table, rows, tables, start, size):
     chips = tables // 2
+    negatives = rows is None
     neg_half = negative_ids.shape[0] // 4
-    shapes = [
-        jax.ShapeDtypeStruct((chips * size * HALF + (neg_half if c == 0 else 0), 2 * width), BF)
-        for c, size in enumerate(chunks)
+    columns, vocab = table.shape
+    lanes = 2 * columns
+    block = jax.ShapeDtypeStruct((chips * size * HALF + (neg_half if negatives else 0), lanes), BF)
+    operands = [event_ids, seq_lengths, seq_owner]
+    in_specs = [hbm()] * 3
+    out_shape = [block, block]
+    scratch = [
+        pltpu.SMEM(event_ids.shape, jnp.int32),
+        pltpu.SMEM(seq_lengths.shape, jnp.int32),
+        pltpu.SMEM(seq_owner.shape, jnp.int32),
+        pltpu.SMEM(negative_ids.shape, jnp.int32),
+        pltpu.VMEM((max(HALF, neg_half), lanes), F32),
+        pltpu.SMEM((tables,), jnp.int32),
+        pltpu.SemaphoreType.DMA((4,)),
     ]
-    outs = pl.pallas_call(
-        functools.partial(gather_kernel, tables, chunks),
-        out_shape=shapes + shapes,
-        in_specs=[hbm(), smem(), smem(), smem(), smem()],
-        out_specs=[vmem()] * (2 * len(chunks)),
-        scratch_shapes=[
-            pltpu.VMEM((width, vocab), BF),
-            pltpu.VMEM((vocab, 2 * width), F32),
-            pltpu.VMEM((max(HALF, neg_half), 2 * width), F32),
-            pltpu.SMEM((tables,), jnp.int32),
+    if negatives:
+        operands += [negative_ids, table]
+        in_specs += [hbm(), hbm()]
+        out_shape = [jax.ShapeDtypeStruct((vocab, lanes), F32)] + out_shape
+        scratch = [
+            pltpu.VMEM((columns, vocab), BF),
             pltpu.SemaphoreType.DMA((2, COPY_PARTS)),
-        ],
-        compiler_params=params(32),
-        name="gather_rows",
-    )(item_table.T, event_ids, negative_ids, seq_lengths, seq_owner)
-    return outs[: len(chunks)], outs[len(chunks) :]
+        ] + scratch
+    else:
+        operands.append(rows)
+        in_specs.append(vmem())
+    kernel = functools.partial(gather_kernel, tables, start, size, negatives)
+    return run(kernel, operands, in_specs, out_shape, scratch, 28, "gather_rows")
 
 
 def merge_kernel(chips, pages, neg_half, keep_ref, got_ref, *out_refs):
@@ -222,16 +269,11 @@
             out_refs[s][k * PAGE + HALF : (k + 1) * PAGE, :] = low
 
 
-def merge_columns(keep, got, chips, pages, neg_half):
+def merge_columns(keep, got, chips, pages, neg_half, after):
     shape = jax.ShapeDtypeStruct((pages * PAGE + 2 * neg_half, keep.shape[1]), BF)
-    return pl.pallas_call(
-        functools.partial(merge_kernel, chips, pages, neg_half),
-        out_shape=[shape] * chips,
-        in_specs=[vmem(), vmem()],
-        out_specs=[vmem()] * chips,
-        compiler_params=params(12),
-        name="merge_columns",
-    )(keep, got)
+    kernel = functools.partial(merge_kernel, chips, pages, neg_half)
+    specs = [vmem(), vmem()]
+    return run(kernel, [keep, got], specs, [shape] * chips, [], 12, "merge_columns", after)
 
 
 def source_chip(s, chips):
@@ -239,29 +281,27 @@
     return lax.rem(chip - s + chips, chips)
 
 
-def unit_negatives_kernel(chips, *refs):
+def unit_negatives_kernel(chips, neg_rows, *refs):
     block_refs, out_ref, spare_ref = refs[:chips], refs[chips], refs[chips + 1]
-    blocks = [ref[...].astype(F32) for ref in block_refs]
+    blocks = [ref[ref.shape[0] - neg_rows :, :].astype(F32) for ref in block_refs]
     squares = sum(jnp.sum(b * b, axis=1, keepdims=True) for b in blocks)
     scale = lax.rsqrt(squares + NORM_EPSILON)
     place_columns(out_ref, spare_ref, [(b * scale).astype(BF) for b in blocks], chips)
 
 
-def unit_negatives(blocks, neg_rows):
+def unit_negatives(blocks, neg_rows, after):
     chips = len(blocks)
-    tail = (blocks[0].shape[0] - neg_rows) // neg_rows
     lanes = blocks[0].shape[1]
-    spec = pl.BlockSpec((neg_rows, lanes), lambda i: (tail, 0))
-    return pl.pallas_call(
-        functools.partial(unit_negatives_kernel, chips),
-        grid=(1,),
-        out_shape=jax.ShapeDtypeStruct((neg_rows, chips * lanes), BF),
-        in_specs=[spec] * chips,
-        out_specs=pl.BlockSpec((neg_rows, chips * lanes), lambda i: (0, 0)),
-        scratch_shapes=[spare_blocks(chips, neg_rows, lanes)],
-        compiler_params=params(8),
-        name="unit_negatives",
-    )(*blocks)
+    return run(
+        functools.partial(unit_negatives_kernel, chips, neg_rows),
+        blocks,
+        [vmem()] * chips,
+        [jax.ShapeDtypeStruct((neg_rows, chips * lanes), BF)],
+        [spare_blocks(chips, neg_rows, lanes)],
+        8,
+        "unit_negatives",
+        after,
+    )[0]
 
 
 def own_plan(len_ref, own_ref):
@@ -399,46 +439,89 @@
     ).astype(BF)
 
 
-def layer(seq_lengths, seq_owner, blocks, weights, prior, first, pages, last):
+def layer(seq_lengths, seq_owner, blocks, weights, prior, first, pages, last, after):
     chips = len(blocks)
     lanes = blocks[0].shape[1]
     width = chips * lanes
     rows = pages * PAGE
     wide = 4 * width
     operands = [seq_lengths, seq_owner, *blocks, *weights]
-    in_specs = [smem(), smem()] + [vmem()] * chips + [hbm()] * 4
+    in_specs = [smem(), smem()] + [vmem()] * chips + [anywhere()] * 4
     if first:
         operands.append(prior)
         in_specs.append(vmem())
     out_shape = [jax.ShapeDtypeStruct((rows, width), BF)] * 2
     if not last:
         out_shape.append(jax.ShapeDtypeStruct((first * PAGE + rows, 2 * width), BF))
-    return pl.pallas_call(
-        functools.partial(layer_kernel, chips, first, pages, last),
-        out_shape=out_shape,
-        in_specs=in_specs,
-        out_specs=[vmem()] * len(out_shape),
-        scratch_shapes=[pltpu.VMEM(w.shape, BF) for w in weights]
-        + [
-            pltpu.VMEM((rows, width), BF),
-            pltpu.VMEM((rows, wide), BF),
-            pltpu.VMEM((rows, width), F32),
-            spare_blocks(chips, rows, lanes),
-            pltpu.SemaphoreType.DMA((4,)),
-        ],
-        compiler_params=params(32),
-        name="layer",
-    )(*operands)
-
-
-def gradient_kernel(count, *refs):
-    len_ref, own_ref, near_ref, far_ref = refs[:4]
-    unit_refs = refs[4 : 4 + count]
-    item_refs = refs[4 + count : 4 + 2 * count]
-    out_ref, neg_ref, next_ref = refs[4 + 2 * count :]
-    half = near_ref.shape[0]
-    neg_ref[:half, :] = near_ref[...]
-    neg_ref[half:, :] = far_ref[...]
+    scratch = [pltpu.VMEM(w.shape, BF) for w in weights] + [
+        pltpu.VMEM((rows, width), BF),
+        pltpu.VMEM((rows, wide), BF),
+        pltpu.VMEM((rows, width), F32),
+        spare_blocks(chips, rows, lanes),
+        pltpu.SemaphoreType.DMA((4,)),
+    ]
+    kernel = functools.partial(layer_kernel, chips, first, pages, last)
+    return run(kernel, operands, in_specs, out_shape, scratch, 28, "layer", after, LAYER_COST * rows * width * width)
+
+
+def join_kernel(*refs):
+    rows = refs[0].shape[0]
+    for i, ref in enumerate(refs[:-1]):
+        refs[-1][i * rows : (i + 1) * rows, :] = ref[...]
+
+
+def join(parts, after):
+    rows, width = parts[0].shape
+    shape = [jax.ShapeDtypeStruct((len(parts) * rows, width), BF)]
+    return run(join_kernel, parts, [vmem()] * len(parts), shape, [], 8, "join", after)[0]
+
+
+def score_part(unit, negatives):
+    scores = lax.dot_general(
+        unit, negatives, (((1,), (1,)), ((), ())), preferred_element_type=F32
+    )
+    powers = jnp.exp(scores * (1.0 / SCORE_SHARPNESS))
+    total = jnp.sum(powers, axis=1, keepdims=True)
+    return total, jnp.dot(powers.astype(BF), negatives, preferred_element_type=F32)
+
+
+def row_blocks(refs):
+    at = 0
+    for ref in refs:
+        size = GRADIENT_PAGES * PAGE
+        for low in range(0, ref.shape[0], size):
+            block = min(size, ref.shape[0] - low)
+            yield ref, low, at, block
+            at += block
+
+
+def near_kernel(count, *refs):
+    negatives = refs[0][...]
+    unit_refs, (sum_ref, total_ref) = refs[1 : 1 + count], refs[1 + count :]
+    for ref, low, at, block in row_blocks(unit_refs):
+        total, part = score_part(ref[low : low + block, :], negatives)
+        sum_ref[at : at + block, :] = part
+        total_ref[at : at + block, :] = total
+
+
+def near_gradient(near, units):
+    rows = sum(u.shape[0] for u in units)
+    half, width = near.shape
+    shapes = [
+        jax.ShapeDtypeStruct((rows, width), F32),
+        jax.ShapeDtypeStruct((rows, 1), F32),
+    ]
+    kernel = functools.partial(near_kernel, len(units))
+    specs = [vmem()] * (1 + len(units))
+    flops = LAYER_COST * rows * width * width // 4
+    return run(kernel, [near, *units], specs, shapes, [], 20, "near_gradient", (), flops)
+
+
+def far_kernel(count, *refs):
+    len_ref, own_ref, far_ref, sum_ref, total_ref = refs[:5]
+    unit_refs = refs[5 : 5 + count]
+    item_refs = refs[5 + count : 5 + 2 * count]
+    out_ref, next_ref = refs[5 + 2 * count :]
     rows = out_ref.shape[0]
     at = 0
     for ref in item_refs:
@@ -447,51 +530,38 @@
     next_ref[rows:, :] = jnp.zeros_like(next_ref[rows:, :])
     segment, _ = own_plan(len_ref, own_ref)
     segment = segment + [jnp.int32(-1)]
-    negatives = neg_ref[...]
+    negatives = far_ref[...]
     sharp = 1.0 / SCORE_SHARPNESS
     row_at = lax.broadcasted_iota(jnp.int32, (PAGE, 1), 0)
-    at = 0
-    for ref in unit_refs:
-        size = GRADIENT_PAGES * PAGE
-        for low in range(0, ref.shape[0], size):
-            count_pages = min(size, ref.shape[0] - low) // PAGE
-            block = count_pages * PAGE
-            unit = ref[low : low + block, :]
-            scores = lax.dot_general(
-                unit, negatives, (((1,), (1,)), ((), ())), preferred_element_type=F32
-            )
-            limits = []
-            for page in range(at // PAGE, at // PAGE + count_pages):
-                last_row = jnp.where(segment[page + 1] == segment[page], PAGE, PAGE - 1)
-                limit = jnp.where(segment[page] >= 0, last_row, 0)
-                limits.append((row_at < limit).astype(F32))
-            has_next = (limits[0] if count_pages == 1 else jnp.concatenate(limits, axis=0)) > 0.5
-            targets = jnp.where(has_next, next_ref[at + 1 : at + 1 + block, :], 0.0)
-            positive = jnp.exp(
-                jnp.sum(unit.astype(F32) * targets, axis=1, keepdims=True) * sharp
-            )
-            powers = jnp.exp(scores * sharp)
-            total = jnp.sum(powers, axis=1, keepdims=True) + positive
-            inverse = 1.0 / total
-            probs = (powers * inverse).astype(BF)
-            grad = jnp.dot(probs, negatives, preferred_element_type=F32)
-            grad = (grad + (positive * inverse - 1.0) * targets) * sharp
-            out_ref[at : at + block, :] = jnp.where(has_next, grad, 0.0)
-            at += block
-
-
-def gradient(seq_lengths, seq_owner, near, far, units, items):
-    rows = sum(u.shape[0] for u in units)
-    half, width = near.shape
-    return pl.pallas_call(
-        functools.partial(gradient_kernel, len(units)),
-        out_shape=jax.ShapeDtypeStruct((rows, width), F32),
-        in_specs=[smem(), smem()] + [vmem()] * (2 + 2 * len(units)),
-        out_specs=vmem(),
-        scratch_shapes=[pltpu.VMEM((2 * half, width), BF), pltpu.VMEM((rows + 8, width), F32)],
-        compiler_params=params(28),
-        name="gradient",
-    )(seq_lengths, seq_owner, near, far, *units, *items)
+    for ref, low, at, block in row_blocks(unit_refs):
+        unit = ref[low : low + block, :]
+        limits = []
+        for page in range(at // PAGE, (at + block) // PAGE):
+            last_row = jnp.where(segment[page + 1] == segment[page], PAGE, PAGE - 1)
+            limit = jnp.where(segment[page] >= 0, last_row, 0)
+            limits.append((row_at < limit).astype(F32))
+        has_next = (limits[0] if len(limits) == 1 else jnp.concatenate(limits, axis=0)) > 0.5
+        targets = jnp.where(has_next, next_ref[at + 1 : at + 1 + block, :], 0.0)
+        positive = jnp.exp(jnp.sum(unit.astype(F32) * targets, axis=1, keepdims=True) * sharp)
+        total, part = score_part(unit, negatives)
+        total = total + total_ref[at : at + block, :] + positive
+        inverse = 1.0 / total
+        grad = (part + sum_ref[at : at + block, :]) * inverse
+        grad = (grad + (positive * inverse - 1.0) * targets) * sharp
+        out_ref[at : at + block, :] = jnp.where(has_next, grad, 0.0)
+
+
+def far_gradient(seq_lengths, seq_owner, far, sums, totals, units, items):
+    rows, width = sums.shape
+    return run(
+        functools.partial(far_kernel, len(units)),
+        [seq_lengths, seq_owner, far, sums, totals, *units, *items],
+        [smem(), smem()] + [vmem()] * (3 + 2 * len(units)),
+        [jax.ShapeDtypeStruct((rows, width), F32)],
+        [pltpu.VMEM((rows + 8, width), F32)],
+        20,
+        "far_gradient",
+    )[0]
 
 
 def on_device(
@@ -502,37 +572,53 @@
     chips = tables // 2
     neg_half = negative_ids.shape[0] // 4
     cores = [(t, t ^ 1) for t in range(tables)]
-    keeps, gives = gather_rows(
-        item_table, event_ids, negative_ids, seq_lengths, seq_owner, tables, CHUNKS
-    )
+    table = stay(item_table.T)
+    event_ids, negative_ids = stay(event_ids), stay(negative_ids)
+    lengths, owners = stay(seq_lengths), stay(seq_owner)
+    rows, first = None, 0
+    packed = []
+    for size in CHUNKS:
+        outs = gather_rows(
+            event_ids, lengths, owners, negative_ids, table, rows, tables, first, size
+        )
+        if rows is None:
+            rows = outs[0]
+        packed.append(outs[-2:])
+        first += size
+    packed.append(())
     arrived = []
     for c, size in enumerate(CHUNKS):
-        got = lax.ppermute(gives[c], "table", cores)
-        blocks = list(merge_columns(keeps[c], got, chips, size, neg_half if c == 0 else 0))
+        keep, give = packed[c]
+        got = lax.ppermute(give, "table", cores)
+        own_neg = neg_half if c == 0 else 0
+        blocks = list(merge_columns(keep, got, chips, size, own_neg, packed[c + 1][-1:]))
         for s in range(1, chips):
             moves = [(t, (t // 2 + s) % chips * 2 + t % 2) for t in range(tables)]
             blocks[s] = lax.ppermute(blocks[s], "table", moves)
         arrived.append(blocks)
-
-    own = unit_negatives(arrived[0], 2 * neg_half)
-    parts = [own]
-    for s in range(1, users):
-        parts.append(lax.ppermute(own, "user", [(u, u ^ s) for u in range(users)]))
-    near = jnp.concatenate(parts, axis=0)
-    far = lax.ppermute(near, "table", cores)
+    arrived.append(())
 
     weights = (w_in, w_mid, w_uvqk, w_proj)
     units, items = [], []
     prior, first = None, 0
     for c, size in enumerate(CHUNKS):
         last = c == len(CHUNKS) - 1
-        outs = layer(seq_lengths, seq_owner, arrived[c], weights, prior, first, size, last)
+        after = list(arrived[c + 1][:1])
+        outs = layer(seq_lengths, seq_owner, arrived[c], weights, prior, first, size, last, after)
         units.append(outs[0])
         items.append(outs[1])
         if not last:
             prior = outs[2]
+        if c == 0:
+            own = unit_negatives(arrived[0], 2 * neg_half, units + list(arrived[1]))
+            parts = [own]
+            for s in range(1, users):
+                parts.append(lax.ppermute(own, "user", [(u, u ^ s) for u in range(users)]))
         first += size
-    return gradient(seq_lengths, seq_owner, near, far, units, items)
+    near = join(parts, units[1:])
+    far = lax.ppermute(near, "table", cores)
+    sums, totals = near_gradient(near, units)
+    return far_gradient(seq_lengths, seq_owner, far, sums, totals, units, items)
 
 
 def solution(mesh):

time: 69.3 us -> 57.8 us (0.83)
  the two profiles are of different devices: /device:TPU:11 before, /device:TPU:15 now
where the time goes in v3:
time: 57.8 us; the launch traced here: 57.7 us
  Pallas kernels  33.2 us (57%)
  waiting for transfers between devices  12.2 us (21%)
  starting transfers between devices  12.1 us (21%)
    pallas_call x10, Pallas kernels, run(): pl.pallas_call(body, out_shape=out_shape, in_specs=in_specs + [anywhere()...  33.2 us
    ppermute x6, waiting for transfers between devices, on_device(): blocks[s] = lax.ppermute(blocks[s], 'table', moves)  11.8 us
    ppermute x6, starting transfers between devices, on_device(): blocks[s] = lax.ppermute(blocks[s], 'table', moves)  7.03 us
    ppermute x3, starting transfers between devices, on_device(): parts.append(lax.ppermute(own, 'user', [(u, u ^ s) for u in range(users)]))  2.71 us
    ppermute x1, starting transfers between devices, on_device(): far = lax.ppermute(near, 'table', cores)  1.51 us
  transfers between devices with their start and end apart: 12, of which 3 were waited for; matrix products, arithmetic and copies ran while one was open for 0% of the time, Pallas kernels for 34%

profile of v3, /device:TPU:15, one launch (start us, length us, event | category | flops | bytes accessed | tf_op | source)
XLA Modules:
  0.0 57.7 jit_solution(4358996453995862516)
XLA Ops:
  0.0 10.1 %gather_rows.2 = (f32[32768,128]{1,0:T(8,128)S(1)}, bf16[832,128]{1,0:T(8,128)(2,1)S(1)}, bf16[832,128]{1,0:T(8,128)(2,1)S(1)}) custom-call(s32[4096]{0:T(1024)} %refs_0_.6, s32[1,16]{1,0:T(1,128)} %refs_0_.9, s32[1,16]{1,0:T(1,128)} %refs_1_.9, s32[256]{0:T(256)} %refs_3_.1, bf16[64,32768]{1,0:T(8,128)(2,1)} %bitcast.1), custom_call_target="tpu_custom_call" | custom-call | tf_op jit(solution)/shard_map/gather_rows/pallas_call | solution.py:40
  10.2 0.7 %collective-permute-start = (bf16[832,128]{1,0:T(8,128)(2,1)S(1)}, bf16[832,128]{1,0:T(8,128)(2,1)S(1)}, u32[]{:S(2)}, u32[]{:S(2)}) collective-permute-start(bf16[832,128]{1,0:T(8,128)(2,1)S(1)} %get-tuple-element.26), channel_id=1, source_target_pairs={{0,4},{4,0},{8,12},{12,8},{16,20},{20,16},{24,28},{28,24},{1,5},{5... | collective-permute-start | bytes 638984 | tf_op jit(solution)/shard_map/ppermute | solution.py:592
  10.9 0.0 copy-start
  10.9 0.0 copy-start.1
  10.9 0.0 copy-start.2
  10.9 0.0 copy-start.3
  10.9 0.0 copy-start.4
  10.9 0.0 copy-start.5
  10.9 3.2 %gather_rows.3 = (bf16[768,128]{1,0:T(8,128)(2,1)S(1)}, bf16[768,128]{1,0:T(8,128)(2,1)S(1)}) custom-call(s32[4096]{0:T(1024)} %refs_0_.6, s32[1,16]{1,0:T(1,128)} %refs_0_.9, s32[1,16]{1,0:T(1,128)} %refs_1_.9, f32[32768,128]{1,0:T(8,128)S(1)} %get-tuple-element.27.refs_3_), custom_call_target="tpu_custom_call" | custom-call | tf_op jit(solution)/shard_map/gather_rows/pallas_call | solution.py:40
  14.1 0.1 collective-permute-start.4
  14.3 0.0 collective-permute-done.refs_1_
  14.3 0.2 merge_columns.2
  14.4 1.3 %collective-permute-start.1 = (bf16[512,128]{1,0:T(8,128)(2,1)S(1)}, bf16[512,128]{1,0:T(8,128)(2,1)S(1)}, u32[]{:S(2)}, u32[]{:S(2)}) collective-permute-start(bf16[512,128]{1,0:T(8,128)(2,1)S(1)} %get-tuple-element.30), channel_id=1, source_target_pairs={{0,8},{4,12},{8,16},{12,20},{16,24},{20,28},{24,0},{28,4},{1,9},{5... | collective-permute-start | bytes 393224 | tf_op jit(solution)/shard_map/ppermute | solution.py:597
  15.8 1.1 %collective-permute-start.2 = (bf16[512,128]{1,0:T(8,128)(2,1)S(1)}, bf16[512,128]{1,0:T(8,128)(2,1)S(1)}, u32[]{:S(2)}, u32[]{:S(2)}) collective-permute-start(bf16[512,128]{1,0:T(8,128)(2,1)S(1)} %get-tuple-element.31), channel_id=1, source_target_pairs={{0,16},{4,20},{8,24},{12,28},{16,0},{20,4},{24,8},{28,12},{1,17},{... | collective-permute-start | bytes 393224 | tf_op jit(solution)/shard_map/ppermute | solution.py:597
  16.9 1.4 %collective-permute-start.3 = (bf16[512,128]{1,0:T(8,128)(2,1)S(1)}, bf16[512,128]{1,0:T(8,128)(2,1)S(1)}, u32[]{:S(2)}, u32[]{:S(2)}) collective-permute-start(bf16[512,128]{1,0:T(8,128)(2,1)S(1)} %get-tuple-element.32), channel_id=1, source_target_pairs={{0,24},{4,28},{8,0},{12,4},{16,8},{20,12},{24,16},{28,20},{1,25},{... | collective-permute-start | bytes 393224 | tf_op jit(solution)/shard_map/ppermute | solution.py:597
  18.3 0.0 collective-permute-done.4.refs_1_
  18.3 0.2 merge_columns.3
  18.4 0.1 collective-permute-start.5
  18.6 3.1 %collective-permute-start.6 = (bf16[384,128]{1,0:T(8,128)(2,1)S(1)}, bf16[384,128]{1,0:T(8,128)(2,1)S(1)}, u32[]{:S(2)}, u32[]{:S(2)}) collective-permute-start(bf16[384,128]{1,0:T(8,128)(2,1)S(1)} %get-tuple-element.37), channel_id=1, source_target_pairs={{0,16},{4,20},{8,24},{12,28},{16,0},{20,4},{24,8},{28,12},{1,17},{... | collective-permute-start | bytes 294920 | tf_op jit(solution)/shard_map/ppermute | solution.py:597
  21.6 0.0 collective-permute-done.1.refs_3_.refs_1_
  21.6 0.0 collective-permute-start.7
  21.6 5.1 %collective-permute-done.2.refs_4_.refs_2_ = bf16[512,128]{1,0:T(8,128)(2,1)S(1)} collective-permute-done((bf16[512,128]{1,0:T(8,128)(2,1)S(1)}, bf16[512,128]{1,0:T(8,128)(2,1)S(1)}, u32[]{:S(2)}, u32[]{:S(2)}) %collective-permute-start.2) | collective-permute-done | bytes 131104 | tf_op jit(solution)/shard_map/ppermute | solution.py:597
  26.7 6.7 %collective-permute-done.3.refs_5_.refs_3_ = bf16[512,128]{1,0:T(8,128)(2,1)S(1)} collective-permute-done((bf16[512,128]{1,0:T(8,128)(2,1)S(1)}, bf16[512,128]{1,0:T(8,128)(2,1)S(1)}, u32[]{:S(2)}, u32[]{:S(2)}) %collective-permute-start.3) | collective-permute-done | bytes 131104 | tf_op jit(solution)/shard_map/ppermute | solution.py:597
  33.4 0.0 copy-done
  33.4 0.0 copy-done.1
  33.4 0.0 copy-done.2
  33.5 0.0 copy-done.3
  33.5 0.0 copy-done.4
  33.5 0.0 copy-done.5
  33.5 6.6 %layer.2 = (bf16[384,512]{1,0:T(8,128)(2,1)S(1)}, bf16[384,512]{1,0:T(8,128)(2,1)S(1)}, bf16[384,1024]{1,0:T(8,128)(2,1)S(1)}) custom-call(s32[1,16]{1,0:T(1,128)S(1)} %copy-done, s32[1,16]{1,0:T(1,128)S(1)} %copy-done.1, bf16[512,128]{1,0:T(8,128)(2,1)S(1)} %get-tuple-element.29.refs_2_.refs_0_, ...), custom_call_target="tpu_custom_call" | custom-call | flops 2415919104 | bytes 8053063 | tf_op jit(solution)/shard_map/layer/pallas_call | solution.py:40
  40.1 0.0 collective-permute-done.5.refs_6_.refs_3_
  40.1 0.0 collective-permute-done.6.refs_7_.refs_4_
  40.1 0.0 collective-permute-done.7.refs_8_.refs_5_
  40.1 0.2 unit_negatives.1.refs_0_
  40.3 0.2 collective-permute-start.10
  40.6 1.2 %collective-permute-start.9 = (bf16[128,512]{1,0:T(8,128)(2,1)S(1)}, bf16[128,512]{1,0:T(8,128)(2,1)S(1)}, u32[]{:S(2)}, u32[]{:S(2)}) collective-permute-start(bf16[128,512]{1,0:T(8,128)(2,1)S(1)} %unit_negatives.1.refs_0_), channel_id=1, source_target_pairs={{0,2},{1,3},{2,0},{3,1},{4,6},{5,7},{6,4},{7,5},{8,10},{9,11},{10,... | collective-permute-start | bytes 393224 | tf_op jit(solution)/shard_map/ppermute | solution.py:616
  41.8 1.2 %collective-permute-start.8 = (bf16[128,512]{1,0:T(8,128)(2,1)S(1)}, bf16[128,512]{1,0:T(8,128)(2,1)S(1)}, u32[]{:S(2)}, u32[]{:S(2)}) collective-permute-start(bf16[128,512]{1,0:T(8,128)(2,1)S(1)} %unit_negatives.1.refs_0_), channel_id=1, source_target_pairs={{0,1},{1,0},{2,3},{3,2},{4,5},{5,4},{6,7},{7,6},{8,9},{9,8},{10,11... | collective-permute-start | bytes 393224 | tf_op jit(solution)/shard_map/ppermute | solution.py:616
  43.0 8.1 %layer.3 = (bf16[384,512]{1,0:T(8,128)(2,1)S(1)}, bf16[384,512]{1,0:T(8,128)(2,1)S(1)}) custom-call(s32[1,16]{1,0:T(1,128)S(1)} %copy-done, s32[1,16]{1,0:T(1,128)S(1)} %copy-done.1, bf16[384,128]{1,0:T(8,128)(2,1)S(1)} %get-tuple-element.34.refs_10_.refs_5_.refs_2_, bf16[384,128]{1,0:T(8,128)(2,1)S(1)} %collective-permute-done.5.refs_6_.refs_3_, ...), custom_call_target="tpu_custom_call" | custom-call | flops 2415919104 | bytes 8053063 | tf_op jit(solution)/shard_map/layer/pallas_call | solution.py:40
  51.1 0.0 collective-permute-done.10.refs_3_
  51.1 0.0 collective-permute-done.9.refs_2_
  51.2 0.0 collective-permute-done.8.refs_1_
  51.2 1.5 %collective-permute-start.11 = (bf16[512,512]{1,0:T(8,128)(2,1)S(1)}, bf16[512,512]{1,0:T(8,128)(2,1)S(1)}, u32[]{:S(2)}, u32[]{:S(2)}) collective-permute-start(bf16[512,512]{1,0:T(8,128)(2,1)S(1)} %join.1.refs_0_), channel_id=1, source_target_pairs={{0,4},{4,0},{8,12},{12,8},{16,20},{20,16},{24,28},{28,24},{1,5},{5... | collective-permute-start | bytes 1572872 | tf_op jit(solution)/shard_map/ppermute | solution.py:619
  52.7 1.1 %near_gradient.1 = (f32[768,512]{1,0:T(8,128)S(1)}, f32[768,1]{1,0:T(8,128)S(1)}) custom-call(bf16[512,512]{1,0:T(8,128)(2,1)S(1)} %join.1.refs_0_, bf16[384,512]{1,0:T(8,128)(2,1)S(1)} %get-tuple-element.35.refs_4_.refs_1_.refs_5_, bf16[384,512]{1,0:T(8,128)(2,1)S(1)} %get-tuple-element.40.refs_4_.refs_2_.refs_6_), custom_call_target="tpu_custom_call" | custom-call | flops 1207959552 | bytes 4026531 | tf_op jit(solution)/shard_map/near_gradient/pallas_call | solution.py:40
  53.8 0.4 collective-permute-done.11.refs_2_
  54.3 3.4 %far_gradient.1 = f32[768,512]{1,0:T(8,128)} custom-call(s32[1,16]{1,0:T(1,128)S(1)} %copy-done, s32[1,16]{1,0:T(1,128)S(1)} %copy-done.1, bf16[512,512]{1,0:T(8,128)(2,1)S(1)} %collective-permute-done.11.refs_2_, f32[768,512]{1,0:T(8,128)S(1)} %get-tuple-element.41.refs_3_, f32[768,1]{1,0:T(8,128)S(1)} %get-tuple-element.42.refs_4_, ...), custom_call_target="tpu_custom_call" | custom-call | tf_op jit(solution)/shard_map/far_gradient/pallas_call | solution.py:40
  (1 shorter events, 0.0 us)
Async XLA Ops:
  10.2 4.1 %collective-permute-start = (bf16[832,128]{1,0:T(8,128)(2,1)S(1)}, bf16[832,128]{1,0:T(8,128)(2,1)S(1)}, u32[]{:S(2)}, u32[]{:S(2)}) collective-permute-start(bf16[832,128]{1,0:T(8,128)(2,1)S(1)} %get-tuple-element.26), channel_id=1, source_target_pairs={{0,4},{4,0},{8,12},{12,8},{16,20},{20,16},{24,28},{28,24},{1,5},{5... | collective-permute-start | bytes 638984 | tf_op jit(solution)/shard_map/ppermute | solution.py:592
  10.9 22.5 %copy-start = (s32[1,16]{1,0:T(1,128)S(1)}, s32[1,16]{1,0:T(1,128)}, u32[]{:S(2)}) copy-start(s32[1,16]{1,0:T(1,128)} %refs_0_.9) | copy-start | bytes 196
  10.9 22.5 %copy-start.1 = (s32[1,16]{1,0:T(1,128)S(1)}, s32[1,16]{1,0:T(1,128)}, u32[]{:S(2)}) copy-start(s32[1,16]{1,0:T(1,128)} %refs_1_.9) | copy-start | bytes 196
  10.9 22.5 %copy-start.2 = (bf16[512,2048]{1,0:T(8,128)(2,1)S(1)}, bf16[512,2048]{1,0:T(8,128)(2,1)}, u32[]{:S(2)}) copy-start(bf16[512,2048]{1,0:T(8,128)(2,1)} %refs_6_.3) | copy-start | bytes 6291460
  10.9 22.6 %copy-start.3 = (bf16[2048,512]{1,0:T(8,128)(2,1)S(1)}, bf16[2048,512]{1,0:T(8,128)(2,1)}, u32[]{:S(2)}) copy-start(bf16[2048,512]{1,0:T(8,128)(2,1)} %refs_7_.3) | copy-start | bytes 6291460
  10.9 22.6 %copy-start.4 = (bf16[512,2048]{1,0:T(8,128)(2,1)S(1)}, bf16[512,2048]{1,0:T(8,128)(2,1)}, u32[]{:S(2)}) copy-start(bf16[512,2048]{1,0:T(8,128)(2,1)} %refs_8_.3) | copy-start | bytes 6291460
  10.9 22.6 %copy-start.5 = (bf16[512,512]{1,0:T(8,128)(2,1)S(1)}, bf16[512,512]{1,0:T(8,128)(2,1)}, u32[]{:S(2)}) copy-start(bf16[512,512]{1,0:T(8,128)(2,1)} %refs_9_.3) | copy-start | bytes 1572868
  14.1 4.1 %collective-permute-start.4 = (bf16[768,128]{1,0:T(8,128)(2,1)S(1)}, bf16[768,128]{1,0:T(8,128)(2,1)S(1)}, u32[]{:S(2)}, u32[]{:S(2)}) collective-permute-start(bf16[768,128]{1,0:T(8,128)(2,1)S(1)} %get-tuple-element.28.refs_2_), channel_id=1, source_target_pairs={{0,4},{4,0},{8,12},{12,8},{16,20},{20,16},{24,28},{28,24},{1,5},{5... | collective-permute-start | bytes 589832 | tf_op jit(solution)/shard_map/ppermute | solution.py:592
  14.4 7.2 %collective-permute-start.1 = (bf16[512,128]{1,0:T(8,128)(2,1)S(1)}, bf16[512,128]{1,0:T(8,128)(2,1)S(1)}, u32[]{:S(2)}, u32[]{:S(2)}) collective-permute-start(bf16[512,128]{1,0:T(8,128)(2,1)S(1)} %get-tuple-element.30), channel_id=1, source_target_pairs={{0,8},{4,12},{8,16},{12,20},{16,24},{20,28},{24,0},{28,4},{1,9},{5... | collective-permute-start | bytes 393224 | tf_op jit(solution)/shard_map/ppermute | solution.py:597
  15.8 10.9 %collective-permute-start.2 = (bf16[512,128]{1,0:T(8,128)(2,1)S(1)}, bf16[512,128]{1,0:T(8,128)(2,1)S(1)}, u32[]{:S(2)}, u32[]{:S(2)}) collective-permute-start(bf16[512,128]{1,0:T(8,128)(2,1)S(1)} %get-tuple-element.31), channel_id=1, source_target_pairs={{0,16},{4,20},{8,24},{12,28},{16,0},{20,4},{24,8},{28,12},{1,17},{... | collective-permute-start | bytes 393224 | tf_op jit(solution)/shard_map/ppermute | solution.py:597
  16.9 16.6 %collective-permute-start.3 = (bf16[512,128]{1,0:T(8,128)(2,1)S(1)}, bf16[512,128]{1,0:T(8,128)(2,1)S(1)}, u32[]{:S(2)}, u32[]{:S(2)}) collective-permute-start(bf16[512,128]{1,0:T(8,128)(2,1)S(1)} %get-tuple-element.32), channel_id=1, source_target_pairs={{0,24},{4,28},{8,0},{12,4},{16,8},{20,12},{24,16},{28,20},{1,25},{... | collective-permute-start | bytes 393224 | tf_op jit(solution)/shard_map/ppermute | solution.py:597
  18.4 21.7 %collective-permute-start.5 = (bf16[384,128]{1,0:T(8,128)(2,1)S(1)}, bf16[384,128]{1,0:T(8,128)(2,1)S(1)}, u32[]{:S(2)}, u32[]{:S(2)}) collective-permute-start(bf16[384,128]{1,0:T(8,128)(2,1)S(1)} %get-tuple-element.36), channel_id=1, source_target_pairs={{0,8},{4,12},{8,16},{12,20},{16,24},{20,28},{24,0},{28,4},{1,9},{5... | collective-permute-start | bytes 294920 | tf_op jit(solution)/shard_map/ppermute | solution.py:597
  18.6 21.5 %collective-permute-start.6 = (bf16[384,128]{1,0:T(8,128)(2,1)S(1)}, bf16[384,128]{1,0:T(8,128)(2,1)S(1)}, u32[]{:S(2)}, u32[]{:S(2)}) collective-permute-start(bf16[384,128]{1,0:T(8,128)(2,1)S(1)} %get-tuple-element.37), channel_id=1, source_target_pairs={{0,16},{4,20},{8,24},{12,28},{16,0},{20,4},{24,8},{28,12},{1,17},{... | collective-permute-start | bytes 294920 | tf_op jit(solution)/shard_map/ppermute | solution.py:597
  21.6 18.5 %collective-permute-start.7 = (bf16[384,128]{1,0:T(8,128)(2,1)S(1)}, bf16[384,128]{1,0:T(8,128)(2,1)S(1)}, u32[]{:S(2)}, u32[]{:S(2)}) collective-permute-start(bf16[384,128]{1,0:T(8,128)(2,1)S(1)} %get-tuple-element.38), channel_id=1, source_target_pairs={{0,24},{4,28},{8,0},{12,4},{16,8},{20,12},{24,16},{28,20},{1,25},{... | collective-permute-start | bytes 294920 | tf_op jit(solution)/shard_map/ppermute | solution.py:597
  40.3 10.8 %collective-permute-start.10 = (bf16[128,512]{1,0:T(8,128)(2,1)S(1)}, bf16[128,512]{1,0:T(8,128)(2,1)S(1)}, u32[]{:S(2)}, u32[]{:S(2)}) collective-permute-start(bf16[128,512]{1,0:T(8,128)(2,1)S(1)} %unit_negatives.1.refs_0_), channel_id=1, source_target_pairs={{0,3},{1,2},{2,1},{3,0},{4,7},{5,6},{6,5},{7,4},{8,11},{9,10},{10,... | collective-permute-start | bytes 393224 | tf_op jit(solution)/shard_map/ppermute | solution.py:616
  40.6 10.6 %collective-permute-start.9 = (bf16[128,512]{1,0:T(8,128)(2,1)S(1)}, bf16[128,512]{1,0:T(8,128)(2,1)S(1)}, u32[]{:S(2)}, u32[]{:S(2)}) collective-permute-start(bf16[128,512]{1,0:T(8,128)(2,1)S(1)} %unit_negatives.1.refs_0_), channel_id=1, source_target_pairs={{0,2},{1,3},{2,0},{3,1},{4,6},{5,7},{6,4},{7,5},{8,10},{9,11},{10,... | collective-permute-start | bytes 393224 | tf_op jit(solution)/shard_map/ppermute | solution.py:616
  41.8 9.4 %collective-permute-start.8 = (bf16[128,512]{1,0:T(8,128)(2,1)S(1)}, bf16[128,512]{1,0:T(8,128)(2,1)S(1)}, u32[]{:S(2)}, u32[]{:S(2)}) collective-permute-start(bf16[128,512]{1,0:T(8,128)(2,1)S(1)} %unit_negatives.1.refs_0_), channel_id=1, source_target_pairs={{0,1},{1,0},{2,3},{3,2},{4,5},{5,4},{6,7},{7,6},{8,9},{9,8},{10,11... | collective-permute-start | bytes 393224 | tf_op jit(solution)/shard_map/ppermute | solution.py:616
  51.2 3.0 %collective-permute-start.11 = (bf16[512,512]{1,0:T(8,128)(2,1)S(1)}, bf16[512,512]{1,0:T(8,128)(2,1)S(1)}, u32[]{:S(2)}, u32[]{:S(2)}) collective-permute-start(bf16[512,512]{1,0:T(8,128)(2,1)S(1)} %join.1.refs_0_), channel_id=1, source_target_pairs={{0,4},{4,0},{8,12},{12,8},{16,20},{20,16},{24,28},{28,24},{1,5},{5... | collective-permute-start | bytes 1572872 | tf_op jit(solution)/shard_map/ppermute | solution.py:619

commit v4 on v3

--- a/solution.py
+++ b/solution.py
@@ -24,6 +24,7 @@
 COPY_PARTS = 8
 GRADIENT_PAGES = 3
 LAYER_COST = 24
+FAR_PAGES = 3
 QUERY_PAGES = 2
 
 
@@ -125,7 +126,7 @@
             )
             return carry
 
-        lax.fori_loop(0, piece // LANES, turn, 0, unroll=4)
+        lax.fori_loop(0, piece // LANES, turn, 0, unroll=16)
 
 
 def gather_kernel(tables, start, size, negatives, *refs):
@@ -167,7 +168,7 @@
                 stage_ref[pl.ds(at + k, 1), :] = picked
             return carry
 
-        lax.fori_loop(0, half // 8, step, 0, unroll=2)
+        lax.fori_loop(0, half // 8, step, 0, unroll=8)
         return stage_ref[0:half, :].astype(BF)
 
     if negatives:
@@ -333,15 +334,7 @@
     refs = refs[2:]
     if not last:
         kv_out, refs = refs[0], refs[1:]
-    w_in_v, w_mid_v, w_uvqk_v, w_proj_v, x_ref, proj_ref, att_ref, spare_ref, sem = refs
-    copies = [
-        pltpu.make_async_copy(a, b, sem.at[i])
-        for i, (a, b) in enumerate(
-            ((w_in, w_in_v), (w_mid, w_mid_v), (w_uvqk, w_uvqk_v), (w_proj, w_proj_v))
-        )
-    ]
-    for c in copies:
-        c.start()
+    x_ref, proj_ref, att_ref, spare_ref = refs
     width = w_in.shape[0]
     segment, length = own_plan(len_ref, own_ref)
     place_columns(x_ref, spare_ref, [ref[0 : pages * PAGE, :] for ref in block_refs], chips)
@@ -358,21 +351,17 @@
     x = x_ref[...]
     hidden_width = w_in.shape[1]
     step = 512
-    copies[0].wait()
     mixed = None
     for f in range(0, hidden_width, step):
         hidden = silu(
-            jnp.dot(x, w_in_v[:, f : f + step], preferred_element_type=F32)
+            jnp.dot(x, w_in[:, f : f + step], preferred_element_type=F32)
         ).astype(BF)
-        if f == 0:
-            copies[1].wait()
-        part = jnp.dot(hidden, w_mid_v[f : f + step, :], preferred_element_type=F32)
+        part = jnp.dot(hidden, w_mid[f : f + step, :], preferred_element_type=F32)
         mixed = part if mixed is None else mixed + part
     mixed = mixed.astype(BF)
-    copies[2].wait()
     for f in range(0, 4 * width, step):
         proj_ref[:, f : f + step] = silu(
-            jnp.dot(mixed, w_uvqk_v[:, f : f + step], preferred_element_type=F32)
+            jnp.dot(mixed, w_uvqk[:, f : f + step], preferred_element_type=F32)
         ).astype(BF)
     if not last:
         kv_out[:, :width] = proj_ref[:, width : 2 * width]
@@ -432,8 +421,7 @@
     gated = (
         centered * lax.rsqrt(variance + LAYER_EPSILON) * proj_ref[:, :width].astype(F32)
     ).astype(BF)
-    copies[3].wait()
-    state = mixed.astype(F32) + jnp.dot(gated, w_proj_v[...], preferred_element_type=F32)
+    state = mixed.astype(F32) + jnp.dot(gated, w_proj[...], preferred_element_type=F32)
     unit_ref[...] = (
         state * lax.rsqrt(jnp.sum(state * state, axis=1, keepdims=True) + NORM_EPSILON)
     ).astype(BF)
@@ -446,19 +434,18 @@
     rows = pages * PAGE
     wide = 4 * width
     operands = [seq_lengths, seq_owner, *blocks, *weights]
-    in_specs = [smem(), smem()] + [vmem()] * chips + [anywhere()] * 4
+    in_specs = [smem(), smem()] + [vmem()] * (chips + 4)
     if first:
         operands.append(prior)
         in_specs.append(vmem())
     out_shape = [jax.ShapeDtypeStruct((rows, width), BF)] * 2
     if not last:
         out_shape.append(jax.ShapeDtypeStruct((first * PAGE + rows, 2 * width), BF))
-    scratch = [pltpu.VMEM(w.shape, BF) for w in weights] + [
+    scratch = [
         pltpu.VMEM((rows, width), BF),
         pltpu.VMEM((rows, wide), BF),
         pltpu.VMEM((rows, width), F32),
         spare_blocks(chips, rows, lanes),
-        pltpu.SemaphoreType.DMA((4,)),
     ]
     kernel = functools.partial(layer_kernel, chips, first, pages, last)
     return run(kernel, operands, in_specs, out_shape, scratch, 28, "layer", after, LAYER_COST * rows * width * width)
@@ -495,73 +482,94 @@
             at += block
 
 
+def next_limits(segment, first, pages):
+    row_at = lax.broadcasted_iota(jnp.int32, (PAGE, 1), 0)
+    limits = []
+    for page in range(first, first + pages):
+        last_row = jnp.where(segment[page + 1] == segment[page], PAGE, PAGE - 1)
+        limit = jnp.where(segment[page] >= 0, last_row, 0)
+        limits.append((row_at < limit).astype(F32))
+    return (limits[0] if pages == 1 else jnp.concatenate(limits, axis=0)) > 0.5
+
+
 def near_kernel(count, *refs):
-    negatives = refs[0][...]
-    unit_refs, (sum_ref, total_ref) = refs[1 : 1 + count], refs[1 + count :]
+    len_ref, own_ref, near_ref = refs[:3]
+    unit_refs = refs[3 : 3 + count]
+    item_refs = refs[3 + count : 3 + 2 * count]
+    sum_ref, total_ref, positive_ref, all_unit_ref, target_ref, next_ref = refs[3 + 2 * count :]
+    negatives = near_ref[...]
+    at = 0
+    for unit, item in zip(unit_refs, item_refs):
+        size = item.shape[0]
+        next_ref[at : at + size, :] = item[...].astype(F32)
+        all_unit_ref[at : at + size, :] = unit[...]
+        at += size
+    next_ref[at:, :] = jnp.zeros_like(next_ref[at:, :])
+    segment, _ = own_plan(len_ref, own_ref)
+    segment = segment + [jnp.int32(-1)]
+    sharp = 1.0 / SCORE_SHARPNESS
     for ref, low, at, block in row_blocks(unit_refs):
-        total, part = score_part(ref[low : low + block, :], negatives)
+        unit = ref[low : low + block, :]
+        has_next = next_limits(segment, at // PAGE, block // PAGE)
+        targets = jnp.where(has_next, next_ref[at + 1 : at + 1 + block, :], 0.0)
+        target_ref[at : at + block, :] = targets.astype(BF)
+        positive = jnp.exp(jnp.sum(unit.astype(F32) * targets, axis=1, keepdims=True) * sharp)
+        total, part = score_part(unit, negatives)
         sum_ref[at : at + block, :] = part
-        total_ref[at : at + block, :] = total
-
-
-def near_gradient(near, units):
+        total_ref[at : at + block, :] = total + positive
+        positive_ref[at : at + block, :] = jnp.where(has_next, positive, -1.0)
+
+
+def near_gradient(seq_lengths, seq_owner, near, units, items):
     rows = sum(u.shape[0] for u in units)
-    half, width = near.shape
+    width = near.shape[1]
     shapes = [
         jax.ShapeDtypeStruct((rows, width), F32),
         jax.ShapeDtypeStruct((rows, 1), F32),
+        jax.ShapeDtypeStruct((rows, 1), F32),
+        jax.ShapeDtypeStruct((rows, width), BF),
+        jax.ShapeDtypeStruct((rows, width), BF),
     ]
-    kernel = functools.partial(near_kernel, len(units))
-    specs = [vmem()] * (1 + len(units))
-    flops = LAYER_COST * rows * width * width // 4
-    return run(kernel, [near, *units], specs, shapes, [], 20, "near_gradient", (), flops)
-
-
-def far_kernel(count, *refs):
-    len_ref, own_ref, far_ref, sum_ref, total_ref = refs[:5]
-    unit_refs = refs[5 : 5 + count]
-    item_refs = refs[5 + count : 5 + 2 * count]
-    out_ref, next_ref = refs[5 + 2 * count :]
-    rows = out_ref.shape[0]
-    at = 0
-    for ref in item_refs:
-        next_ref[at : at + ref.shape[0], :] = ref[...].astype(F32)
-        at += ref.shape[0]
-    next_ref[rows:, :] = jnp.zeros_like(next_ref[rows:, :])
-    segment, _ = own_plan(len_ref, own_ref)
-    segment = segment + [jnp.int32(-1)]
-    negatives = far_ref[...]
-    sharp = 1.0 / SCORE_SHARPNESS
-    row_at = lax.broadcasted_iota(jnp.int32, (PAGE, 1), 0)
-    for ref, low, at, block in row_blocks(unit_refs):
-        unit = ref[low : low + block, :]
-        limits = []
-        for page in range(at // PAGE, (at + block) // PAGE):
-            last_row = jnp.where(segment[page + 1] == segment[page], PAGE, PAGE - 1)
-            limit = jnp.where(segment[page] >= 0, last_row, 0)
-            limits.append((row_at < limit).astype(F32))
-        has_next = (limits[0] if len(limits) == 1 else jnp.concatenate(limits, axis=0)) > 0.5
-        targets = jnp.where(has_next, next_ref[at + 1 : at + 1 + block, :], 0.0)
-        positive = jnp.exp(jnp.sum(unit.astype(F32) * targets, axis=1, keepdims=True) * sharp)
-        total, part = score_part(unit, negatives)
-        total = total + total_ref[at : at + block, :] + positive
-        inverse = 1.0 / total
-        grad = (part + sum_ref[at : at + block, :]) * inverse
-        grad = (grad + (positive * inverse - 1.0) * targets) * sharp
-        out_ref[at : at + block, :] = jnp.where(has_next, grad, 0.0)
-
-
-def far_gradient(seq_lengths, seq_owner, far, sums, totals, units, items):
-    rows, width = sums.shape
     return run(
-        functools.partial(far_kernel, len(units)),
-        [seq_lengths, seq_owner, far, sums, totals, *units, *items],
-        [smem(), smem()] + [vmem()] * (3 + 2 * len(units)),
-        [jax.ShapeDtypeStruct((rows, width), F32)],
+        functools.partial(near_kernel, len(units)),
+        [seq_lengths, seq_owner, near, *units, *items],
+        [smem(), smem()] + [vmem()] * (1 + 2 * len(units)),
+        shapes,
         [pltpu.VMEM((rows + 8, width), F32)],
         20,
-        "far_gradient",
-    )[0]
+        "near_gradient",
+        (),
+        LAYER_COST * rows * width * width // 4,
+    )
+
+
+def far_kernel(far_ref, sum_ref, total_ref, positive_ref, unit_ref, target_ref, out_ref):
+    sharp = 1.0 / SCORE_SHARPNESS
+    total, part = score_part(unit_ref[...], far_ref[...])
+    positive = positive_ref[...]
+    inverse = 1.0 / (total + total_ref[...])
+    grad = (part + sum_ref[...]) * inverse
+    grad = (grad + (positive * inverse - 1.0) * target_ref[...].astype(F32)) * sharp
+    out_ref[...] = jnp.where(positive >= 0.0, grad, 0.0)
+
+
+def far_gradient(far, sums, totals, positives, unit, targets):
+    rows, width = sums.shape
+    block = FAR_PAGES * PAGE
+
+    def spec(shape):
+        return pl.BlockSpec((block, shape[1]), lambda i: (i, 0))
+
+    operands = [sums, totals, positives, unit, targets]
+    return pl.pallas_call(
+        far_kernel,
+        grid=(rows // block,),
+        out_shape=jax.ShapeDtypeStruct((rows, width), F32),
+        in_specs=[pl.BlockSpec(far.shape, lambda i: (0, 0))] + [spec(x.shape) for x in operands],
+        out_specs=pl.BlockSpec((block, width), lambda i: (i, 0)),
+        compiler_params=params(20),
+        name="far_gradient",
+    )(far, *operands)
 
 
 def on_device(
@@ -617,8 +625,7 @@
         first += size
     near = join(parts, units[1:])
     far = lax.ppermute(near, "table", cores)
-    sums, totals = near_gradient(near, units)
-    return far_gradient(seq_lengths, seq_owner, far, sums, totals, units, items)
+    return far_gradient(far, *near_gradient(seq_lengths, seq_owner, near, units, items))
 
 
 def solution(mesh):

time: 57.8 us -> 53 us (0.917)
  the two profiles are of different devices: /device:TPU:15 before, /device:TPU:13 now
where the time goes in v4:
time: 53 us; the launch traced here: 52.8 us
  Pallas kernels  28.7 us (54%)
  starting transfers between devices  12.1 us (23%)
  waiting for transfers between devices  11.8 us (22%)
    pallas_call x9, Pallas kernels, run(): pl.pallas_call(body, out_shape=out_shape, in_specs=in_specs + [anywhere()...  26.2 us
    ppermute x6, waiting for transfers between devices, on_device(): blocks[s] = lax.ppermute(blocks[s], 'table', moves)  11.8 us
    ppermute x6, starting transfers between devices, on_device(): blocks[s] = lax.ppermute(blocks[s], 'table', moves)  7.03 us
    ppermute x3, starting transfers between devices, on_device(): parts.append(lax.ppermute(own, 'user', [(u, u ^ s) for u in range(users)]))  2.71 us
    pallas_call x1, Pallas kernels, far_gradient(): pl.pallas_call(far_kernel, grid=(rows // block,), out_shape=jax.ShapeDtyp...  2.52 us
    ppermute x1, starting transfers between devices, on_device(): far = lax.ppermute(near, 'table', cores)  1.48 us
  transfers between devices with their start and end apart: 12, of which 2 were waited for; matrix products, arithmetic and copies ran while one was open for 0% of the time, Pallas kernels for 34%

profile of v4, /device:TPU:13, one launch (start us, length us, event | category | flops | bytes accessed | tf_op | source)
XLA Modules:
  0.0 52.8 jit_solution(442666505369058723)
XLA Ops:
  0.0 8.0 %gather_rows.2 = (f32[32768,128]{1,0:T(8,128)S(1)}, bf16[832,128]{1,0:T(8,128)(2,1)S(1)}, bf16[832,128]{1,0:T(8,128)(2,1)S(1)}) custom-call(s32[4096]{0:T(1024)} %refs_0_.6, s32[1,16]{1,0:T(1,128)} %refs_0_.9, s32[1,16]{1,0:T(1,128)} %refs_1_.9, s32[256]{0:T(256)} %refs_3_.1, bf16[64,32768]{1,0:T(8,128)(2,1)} %bitcast.1), custom_call_target="tpu_custom_call" | custom-call | tf_op jit(solution)/shard_map/gather_rows/pallas_call | solution.py:41
  8.0 0.7 %collective-permute-start = (bf16[832,128]{1,0:T(8,128)(2,1)S(1)}, bf16[832,128]{1,0:T(8,128)(2,1)S(1)}, u32[]{:S(2)}, u32[]{:S(2)}) collective-permute-start(bf16[832,128]{1,0:T(8,128)(2,1)S(1)} %get-tuple-element.29), channel_id=1, source_target_pairs={{0,4},{4,0},{8,12},{12,8},{16,20},{20,16},{24,28},{28,24},{1,5},{5... | collective-permute-start | bytes 638984 | tf_op jit(solution)/shard_map/ppermute | solution.py:600
  8.7 0.0 copy-start
  8.7 0.0 copy-start.1
  8.7 0.0 copy-start.2
  8.7 0.0 copy-start.3
  8.7 0.0 copy-start.4
  8.8 0.0 copy-start.5
  8.8 3.4 %gather_rows.3 = (bf16[768,128]{1,0:T(8,128)(2,1)S(1)}, bf16[768,128]{1,0:T(8,128)(2,1)S(1)}) custom-call(s32[4096]{0:T(1024)} %refs_0_.6, s32[1,16]{1,0:T(1,128)} %refs_0_.9, s32[1,16]{1,0:T(1,128)} %refs_1_.9, f32[32768,128]{1,0:T(8,128)S(1)} %get-tuple-element.30.refs_3_), custom_call_target="tpu_custom_call" | custom-call | tf_op jit(solution)/shard_map/gather_rows/pallas_call | solution.py:41
  12.1 0.1 collective-permute-start.4
  12.3 0.0 collective-permute-done.refs_1_
  12.3 0.2 merge_columns.2
  12.4 1.3 %collective-permute-start.1 = (bf16[512,128]{1,0:T(8,128)(2,1)S(1)}, bf16[512,128]{1,0:T(8,128)(2,1)S(1)}, u32[]{:S(2)}, u32[]{:S(2)}) collective-permute-start(bf16[512,128]{1,0:T(8,128)(2,1)S(1)} %get-tuple-element.33), channel_id=1, source_target_pairs={{0,8},{4,12},{8,16},{12,20},{16,24},{20,28},{24,0},{28,4},{1,9},{5... | collective-permute-start | bytes 393224 | tf_op jit(solution)/shard_map/ppermute | solution.py:605
  13.8 1.1 %collective-permute-start.2 = (bf16[512,128]{1,0:T(8,128)(2,1)S(1)}, bf16[512,128]{1,0:T(8,128)(2,1)S(1)}, u32[]{:S(2)}, u32[]{:S(2)}) collective-permute-start(bf16[512,128]{1,0:T(8,128)(2,1)S(1)} %get-tuple-element.34), channel_id=1, source_target_pairs={{0,16},{4,20},{8,24},{12,28},{16,0},{20,4},{24,8},{28,12},{1,17},{... | collective-permute-start | bytes 393224 | tf_op jit(solution)/shard_map/ppermute | solution.py:605
  14.9 1.4 %collective-permute-start.3 = (bf16[512,128]{1,0:T(8,128)(2,1)S(1)}, bf16[512,128]{1,0:T(8,128)(2,1)S(1)}, u32[]{:S(2)}, u32[]{:S(2)}) collective-permute-start(bf16[512,128]{1,0:T(8,128)(2,1)S(1)} %get-tuple-element.35), channel_id=1, source_target_pairs={{0,24},{4,28},{8,0},{12,4},{16,8},{20,12},{24,16},{28,20},{1,25},{... | collective-permute-start | bytes 393224 | tf_op jit(solution)/shard_map/ppermute | solution.py:605
  16.3 0.0 collective-permute-done.4.refs_1_
  16.3 0.2 merge_columns.3
  16.4 0.1 collective-permute-start.5
  16.6 3.1 %collective-permute-start.6 = (bf16[384,128]{1,0:T(8,128)(2,1)S(1)}, bf16[384,128]{1,0:T(8,128)(2,1)S(1)}, u32[]{:S(2)}, u32[]{:S(2)}) collective-permute-start(bf16[384,128]{1,0:T(8,128)(2,1)S(1)} %get-tuple-element.40), channel_id=1, source_target_pairs={{0,16},{4,20},{8,24},{12,28},{16,0},{20,4},{24,8},{28,12},{1,17},{... | collective-permute-start | bytes 294920 | tf_op jit(solution)/shard_map/ppermute | solution.py:605
  19.6 0.0 collective-permute-done.1.refs_3_.refs_1_
  19.6 0.0 collective-permute-start.7
  19.6 5.1 %collective-permute-done.2.refs_4_.refs_2_ = bf16[512,128]{1,0:T(8,128)(2,1)S(1)} collective-permute-done((bf16[512,128]{1,0:T(8,128)(2,1)S(1)}, bf16[512,128]{1,0:T(8,128)(2,1)S(1)}, u32[]{:S(2)}, u32[]{:S(2)}) %collective-permute-start.2) | collective-permute-done | bytes 131104 | tf_op jit(solution)/shard_map/ppermute | solution.py:605
  24.7 6.7 %collective-permute-done.3.refs_5_.refs_3_ = bf16[512,128]{1,0:T(8,128)(2,1)S(1)} collective-permute-done((bf16[512,128]{1,0:T(8,128)(2,1)S(1)}, bf16[512,128]{1,0:T(8,128)(2,1)S(1)}, u32[]{:S(2)}, u32[]{:S(2)}) %collective-permute-start.3) | collective-permute-done | bytes 131104 | tf_op jit(solution)/shard_map/ppermute | solution.py:605
  31.4 0.0 copy-done
  31.4 0.0 copy-done.1
  31.4 0.0 copy-done.2
  31.4 0.0 copy-done.3
  31.5 0.0 copy-done.4
  31.5 0.0 copy-done.5
  31.5 5.6 %layer.2 = (bf16[384,512]{1,0:T(8,128)(2,1)S(1)}, bf16[384,512]{1,0:T(8,128)(2,1)S(1)}, bf16[384,1024]{1,0:T(8,128)(2,1)S(1)}) custom-call(s32[1,16]{1,0:T(1,128)S(1)} %copy-done, s32[1,16]{1,0:T(1,128)S(1)} %copy-done.1, bf16[512,128]{1,0:T(8,128)(2,1)S(1)} %get-tuple-element.32.refs_2_.refs_0_, ...), custom_call_target="tpu_custom_call" | custom-call | flops 2415919104 | bytes 8053063 | tf_op jit(solution)/shard_map/layer/pallas_call | solution.py:41
  37.1 0.0 collective-permute-done.5.refs_6_.refs_3_
  37.1 0.0 collective-permute-done.6.refs_7_.refs_4_
  37.1 0.0 collective-permute-done.7.refs_8_.refs_5_
  37.1 0.2 unit_negatives.1.refs_0_
  37.3 1.2 %collective-permute-start.10 = (bf16[128,512]{1,0:T(8,128)(2,1)S(1)}, bf16[128,512]{1,0:T(8,128)(2,1)S(1)}, u32[]{:S(2)}, u32[]{:S(2)}) collective-permute-start(bf16[128,512]{1,0:T(8,128)(2,1)S(1)} %unit_negatives.1.refs_0_), channel_id=1, source_target_pairs={{0,3},{1,2},{2,1},{3,0},{4,7},{5,6},{6,5},{7,4},{8,11},{9,10},{10,... | collective-permute-start | bytes 393224 | tf_op jit(solution)/shard_map/ppermute | solution.py:624
  38.5 1.2 %collective-permute-start.9 = (bf16[128,512]{1,0:T(8,128)(2,1)S(1)}, bf16[128,512]{1,0:T(8,128)(2,1)S(1)}, u32[]{:S(2)}, u32[]{:S(2)}) collective-permute-start(bf16[128,512]{1,0:T(8,128)(2,1)S(1)} %unit_negatives.1.refs_0_), channel_id=1, source_target_pairs={{0,2},{1,3},{2,0},{3,1},{4,6},{5,7},{6,4},{7,5},{8,10},{9,11},{10,... | collective-permute-start | bytes 393224 | tf_op jit(solution)/shard_map/ppermute | solution.py:624
  39.7 0.3 collective-permute-start.8
  40.0 6.7 %layer.3 = (bf16[384,512]{1,0:T(8,128)(2,1)S(1)}, bf16[384,512]{1,0:T(8,128)(2,1)S(1)}) custom-call(s32[1,16]{1,0:T(1,128)S(1)} %copy-done, s32[1,16]{1,0:T(1,128)S(1)} %copy-done.1, bf16[384,128]{1,0:T(8,128)(2,1)S(1)} %get-tuple-element.37.refs_10_.refs_5_.refs_2_, bf16[384,128]{1,0:T(8,128)(2,1)S(1)} %collective-permute-done.5.refs_6_.refs_3_, ...), custom_call_target="tpu_custom_call" | custom-call | flops 2415919104 | bytes 8053063 | tf_op jit(solution)/shard_map/layer/pallas_call | solution.py:41
  46.6 0.0 collective-permute-done.10.refs_3_
  46.6 0.0 collective-permute-done.9.refs_2_
  46.7 0.0 collective-permute-done.8.refs_1_
  46.7 1.5 %collective-permute-start.11 = (bf16[512,512]{1,0:T(8,128)(2,1)S(1)}, bf16[512,512]{1,0:T(8,128)(2,1)S(1)}, u32[]{:S(2)}, u32[]{:S(2)}) collective-permute-start(bf16[512,512]{1,0:T(8,128)(2,1)S(1)} %join.1.refs_2_), channel_id=1, source_target_pairs={{0,4},{4,0},{8,12},{12,8},{16,20},{20,16},{24,28},{28,24},{1,5},{5... | collective-permute-start | bytes 1572872 | tf_op jit(solution)/shard_map/ppermute | solution.py:627
  48.2 2.1 %near_gradient.1 = (f32[768,512]{1,0:T(8,128)S(1)}, f32[768,1]{1,0:T(8,128)S(1)}, f32[768,1]{1,0:T(8,128)S(1)}, bf16[768,512]{1,0:T(8,128)(2,1)S(1)}, bf16[768,512]{1,0:T(8,128)(2,1)S(1)}) custom-call(s32[1,16]{1,0:T(1,128)S(1)} %copy-done, s32[1,16]{1,0:T(1,128)S(1)} %copy-done.1, bf16[512,512]{1,0:T(8,128)(2,1)S(1)} %join.1.refs_2_, ...), custom_call_target="tpu_custom_call" | custom-call | flops 1207959552 | bytes 4026531 | tf_op jit(solution)/shard_map/near_gradient/pallas_call | solution.py:41
  50.3 0.0 collective-permute-done.11.far_ref
  50.3 2.5 %far_gradient.1 = f32[768,512]{1,0:T(8,128)} custom-call(bf16[512,512]{1,0:T(8,128)(2,1)S(1)} %collective-permute-done.11.far_ref, f32[768,512]{1,0:T(8,128)S(1)} %get-tuple-element.46.sum_ref, f32[768,1]{1,0:T(8,128)S(1)} %get-tuple-element.47.total_ref, f32[768,1]{1,0:T(8,128)S(1)} %get-tuple-element.48.positive_ref, ...), custom_call_target="tpu_custom_call" | custom-call | tf_op jit(solution)/shard_map/far_gradient/pallas_call | solution.py:564
  (1 shorter events, 0.0 us)
Async XLA Ops:
  8.0 4.3 %collective-permute-start = (bf16[832,128]{1,0:T(8,128)(2,1)S(1)}, bf16[832,128]{1,0:T(8,128)(2,1)S(1)}, u32[]{:S(2)}, u32[]{:S(2)}) collective-permute-start(bf16[832,128]{1,0:T(8,128)(2,1)S(1)} %get-tuple-element.29), channel_id=1, source_target_pairs={{0,4},{4,0},{8,12},{12,8},{16,20},{20,16},{24,28},{28,24},{1,5},{5... | collective-permute-start | bytes 638984 | tf_op jit(solution)/shard_map/ppermute | solution.py:600
  8.7 22.7 %copy-start = (s32[1,16]{1,0:T(1,128)S(1)}, s32[1,16]{1,0:T(1,128)}, u32[]{:S(2)}) copy-start(s32[1,16]{1,0:T(1,128)} %refs_0_.9) | copy-start | bytes 196
  8.7 22.7 %copy-start.1 = (s32[1,16]{1,0:T(1,128)S(1)}, s32[1,16]{1,0:T(1,128)}, u32[]{:S(2)}) copy-start(s32[1,16]{1,0:T(1,128)} %refs_1_.9) | copy-start | bytes 196
  8.7 22.7 %copy-start.2 = (bf16[512,2048]{1,0:T(8,128)(2,1)S(1)}, bf16[512,2048]{1,0:T(8,128)(2,1)}, u32[]{:S(2)}) copy-start(bf16[512,2048]{1,0:T(8,128)(2,1)} %refs_6_.3) | copy-start | bytes 6291460
  8.7 22.7 %copy-start.3 = (bf16[2048,512]{1,0:T(8,128)(2,1)S(1)}, bf16[2048,512]{1,0:T(8,128)(2,1)}, u32[]{:S(2)}) copy-start(bf16[2048,512]{1,0:T(8,128)(2,1)} %refs_7_.3) | copy-start | bytes 6291460
  8.7 22.7 %copy-start.4 = (bf16[512,2048]{1,0:T(8,128)(2,1)S(1)}, bf16[512,2048]{1,0:T(8,128)(2,1)}, u32[]{:S(2)}) copy-start(bf16[512,2048]{1,0:T(8,128)(2,1)} %refs_8_.3) | copy-start | bytes 6291460
  8.8 22.7 %copy-start.5 = (bf16[512,512]{1,0:T(8,128)(2,1)S(1)}, bf16[512,512]{1,0:T(8,128)(2,1)}, u32[]{:S(2)}) copy-start(bf16[512,512]{1,0:T(8,128)(2,1)} %refs_9_.3) | copy-start | bytes 1572868
  12.1 4.1 %collective-permute-start.4 = (bf16[768,128]{1,0:T(8,128)(2,1)S(1)}, bf16[768,128]{1,0:T(8,128)(2,1)S(1)}, u32[]{:S(2)}, u32[]{:S(2)}) collective-permute-start(bf16[768,128]{1,0:T(8,128)(2,1)S(1)} %get-tuple-element.31.refs_2_), channel_id=1, source_target_pairs={{0,4},{4,0},{8,12},{12,8},{16,20},{20,16},{24,28},{28,24},{1,5},{5... | collective-permute-start | bytes 589832 | tf_op jit(solution)/shard_map/ppermute | solution.py:600
  12.4 7.2 %collective-permute-start.1 = (bf16[512,128]{1,0:T(8,128)(2,1)S(1)}, bf16[512,128]{1,0:T(8,128)(2,1)S(1)}, u32[]{:S(2)}, u32[]{:S(2)}) collective-permute-start(bf16[512,128]{1,0:T(8,128)(2,1)S(1)} %get-tuple-element.33), channel_id=1, source_target_pairs={{0,8},{4,12},{8,16},{12,20},{16,24},{20,28},{24,0},{28,4},{1,9},{5... | collective-permute-start | bytes 393224 | tf_op jit(solution)/shard_map/ppermute | solution.py:605
  13.8 10.9 %collective-permute-start.2 = (bf16[512,128]{1,0:T(8,128)(2,1)S(1)}, bf16[512,128]{1,0:T(8,128)(2,1)S(1)}, u32[]{:S(2)}, u32[]{:S(2)}) collective-permute-start(bf16[512,128]{1,0:T(8,128)(2,1)S(1)} %get-tuple-element.34), channel_id=1, source_target_pairs={{0,16},{4,20},{8,24},{12,28},{16,0},{20,4},{24,8},{28,12},{1,17},{... | collective-permute-start | bytes 393224 | tf_op jit(solution)/shard_map/ppermute | solution.py:605
  14.9 16.6 %collective-permute-start.3 = (bf16[512,128]{1,0:T(8,128)(2,1)S(1)}, bf16[512,128]{1,0:T(8,128)(2,1)S(1)}, u32[]{:S(2)}, u32[]{:S(2)}) collective-permute-start(bf16[512,128]{1,0:T(8,128)(2,1)S(1)} %get-tuple-element.35), channel_id=1, source_target_pairs={{0,24},{4,28},{8,0},{12,4},{16,8},{20,12},{24,16},{28,20},{1,25},{... | collective-permute-start | bytes 393224 | tf_op jit(solution)/shard_map/ppermute | solution.py:605
  16.4 20.6 %collective-permute-start.5 = (bf16[384,128]{1,0:T(8,128)(2,1)S(1)}, bf16[384,128]{1,0:T(8,128)(2,1)S(1)}, u32[]{:S(2)}, u32[]{:S(2)}) collective-permute-start(bf16[384,128]{1,0:T(8,128)(2,1)S(1)} %get-tuple-element.39), channel_id=1, source_target_pairs={{0,8},{4,12},{8,16},{12,20},{16,24},{20,28},{24,0},{28,4},{1,9},{5... | collective-permute-start | bytes 294920 | tf_op jit(solution)/shard_map/ppermute | solution.py:605
  16.6 20.5 %collective-permute-start.6 = (bf16[384,128]{1,0:T(8,128)(2,1)S(1)}, bf16[384,128]{1,0:T(8,128)(2,1)S(1)}, u32[]{:S(2)}, u32[]{:S(2)}) collective-permute-start(bf16[384,128]{1,0:T(8,128)(2,1)S(1)} %get-tuple-element.40), channel_id=1, source_target_pairs={{0,16},{4,20},{8,24},{12,28},{16,0},{20,4},{24,8},{28,12},{1,17},{... | collective-permute-start | bytes 294920 | tf_op jit(solution)/shard_map/ppermute | solution.py:605
  19.6 17.4 %collective-permute-start.7 = (bf16[384,128]{1,0:T(8,128)(2,1)S(1)}, bf16[384,128]{1,0:T(8,128)(2,1)S(1)}, u32[]{:S(2)}, u32[]{:S(2)}) collective-permute-start(bf16[384,128]{1,0:T(8,128)(2,1)S(1)} %get-tuple-element.41), channel_id=1, source_target_pairs={{0,24},{4,28},{8,0},{12,4},{16,8},{20,12},{24,16},{28,20},{1,25},{... | collective-permute-start | bytes 294920 | tf_op jit(solution)/shard_map/ppermute | solution.py:605
  37.3 9.4 %collective-permute-start.10 = (bf16[128,512]{1,0:T(8,128)(2,1)S(1)}, bf16[128,512]{1,0:T(8,128)(2,1)S(1)}, u32[]{:S(2)}, u32[]{:S(2)}) collective-permute-start(bf16[128,512]{1,0:T(8,128)(2,1)S(1)} %unit_negatives.1.refs_0_), channel_id=1, source_target_pairs={{0,3},{1,2},{2,1},{3,0},{4,7},{5,6},{6,5},{7,4},{8,11},{9,10},{10,... | collective-permute-start | bytes 393224 | tf_op jit(solution)/shard_map/ppermute | solution.py:624
  38.5 8.2 %collective-permute-start.9 = (bf16[128,512]{1,0:T(8,128)(2,1)S(1)}, bf16[128,512]{1,0:T(8,128)(2,1)S(1)}, u32[]{:S(2)}, u32[]{:S(2)}) collective-permute-start(bf16[128,512]{1,0:T(8,128)(2,1)S(1)} %unit_negatives.1.refs_0_), channel_id=1, source_target_pairs={{0,2},{1,3},{2,0},{3,1},{4,6},{5,7},{6,4},{7,5},{8,10},{9,11},{10,... | collective-permute-start | bytes 393224 | tf_op jit(solution)/shard_map/ppermute | solution.py:624
  39.7 7.0 %collective-permute-start.8 = (bf16[128,512]{1,0:T(8,128)(2,1)S(1)}, bf16[128,512]{1,0:T(8,128)(2,1)S(1)}, u32[]{:S(2)}, u32[]{:S(2)}) collective-permute-start(bf16[128,512]{1,0:T(8,128)(2,1)S(1)} %unit_negatives.1.refs_0_), channel_id=1, source_target_pairs={{0,1},{1,0},{2,3},{3,2},{4,5},{5,4},{6,7},{7,6},{8,9},{9,8},{10,11... | collective-permute-start | bytes 393224 | tf_op jit(solution)/shard_map/ppermute | solution.py:624
  46.7 3.6 %collective-permute-start.11 = (bf16[512,512]{1,0:T(8,128)(2,1)S(1)}, bf16[512,512]{1,0:T(8,128)(2,1)S(1)}, u32[]{:S(2)}, u32[]{:S(2)}) collective-permute-start(bf16[512,512]{1,0:T(8,128)(2,1)S(1)} %join.1.refs_2_), channel_id=1, source_target_pairs={{0,4},{4,0},{8,12},{12,8},{16,20},{20,16},{24,28},{28,24},{1,5},{5... | collective-permute-start | bytes 1572872 | tf_op jit(solution)/shard_map/ppermute | solution.py:627

commit v5 on v4

--- a/solution.py
+++ b/solution.py
@@ -25,7 +25,8 @@
 GRADIENT_PAGES = 3
 LAYER_COST = 24
 FAR_PAGES = 3
-QUERY_PAGES = 2
+EARLIER = slice(2, 3)
+QUERY_PAGES = 3
 
 
 def params(mebibytes):
@@ -350,7 +351,7 @@
 
     x = x_ref[...]
     hidden_width = w_in.shape[1]
-    step = 512
+    step = 1024
     mixed = None
     for f in range(0, hidden_width, step):
         hidden = silu(
@@ -599,7 +600,8 @@
         keep, give = packed[c]
         got = lax.ppermute(give, "table", cores)
         own_neg = neg_half if c == 0 else 0
-        blocks = list(merge_columns(keep, got, chips, size, own_neg, packed[c + 1][-1:]))
+        after = list(packed[c + 1][-1:]) + (arrived[0][EARLIER] if c else [])
+        blocks = list(merge_columns(keep, got, chips, size, own_neg, after))
         for s in range(1, chips):
             moves = [(t, (t // 2 + s) % chips * 2 + t % 2) for t in range(tables)]
             blocks[s] = lax.ppermute(blocks[s], "table", moves)
@@ -618,7 +620,7 @@
         if not last:
             prior = outs[2]
         if c == 0:
-            own = unit_negatives(arrived[0], 2 * neg_half, units + list(arrived[1]))
+            own = unit_negatives(arrived[0], 2 * neg_half, units + list(arrived[1][1:2]))
             parts = [own]
             for s in range(1, users):
                 parts.append(lax.ppermute(own, "user", [(u, u ^ s) for u in range(users)]))

time: 53 us -> 50.4 us (0.951)
  the two profiles are of different devices: /device:TPU:13 before, /device:TPU:1 now
where the time goes in v5:
time: 50.4 us; the launch traced here: 50.3 us
  Pallas kernels  27.8 us (55%)
  starting transfers between devices  16.4 us (33%)
  waiting for transfers between devices  5.9 us (12%)
    pallas_call x9, Pallas kernels, run(): pl.pallas_call(body, out_shape=out_shape, in_specs=in_specs + [anywhere()...  25.3 us
    ppermute x6, starting transfers between devices, on_device(): blocks[s] = lax.ppermute(blocks[s], 'table', moves)  10 us
    ppermute x6, waiting for transfers between devices, on_device(): blocks[s] = lax.ppermute(blocks[s], 'table', moves)  5.88 us
    ppermute x1, starting transfers between devices, on_device(): far = lax.ppermute(near, 'table', cores)  3.03 us
    ppermute x3, starting transfers between devices, on_device(): parts.append(lax.ppermute(own, 'user', [(u, u ^ s) for u in range(users)]))  2.71 us
    pallas_call x1, Pallas kernels, far_gradient(): pl.pallas_call(far_kernel, grid=(rows // block,), out_shape=jax.ShapeDtyp...  2.53 us
  transfers between devices with their start and end apart: 12, of which 1 were waited for; matrix products, arithmetic and copies ran while one was open for 0% of the time, Pallas kernels for 34%

profile of v5, /device:TPU:1, one launch (start us, length us, event | category | flops | bytes accessed | tf_op | source)
XLA Modules:
  0.0 50.3 jit_solution(3711970375444375233)
XLA Ops:
  0.0 8.1 %gather_rows.2 = (f32[32768,128]{1,0:T(8,128)S(1)}, bf16[832,128]{1,0:T(8,128)(2,1)S(1)}, bf16[832,128]{1,0:T(8,128)(2,1)S(1)}) custom-call(s32[4096]{0:T(1024)} %refs_0_.6, s32[1,16]{1,0:T(1,128)} %refs_0_.9, s32[1,16]{1,0:T(1,128)} %refs_1_.9, s32[256]{0:T(256)} %refs_3_.1, bf16[64,32768]{1,0:T(8,128)(2,1)} %bitcast.1), custom_call_target="tpu_custom_call" | custom-call | tf_op jit(solution)/shard_map/gather_rows/pallas_call | solution.py:42
  8.2 0.1 collective-permute-start
  8.3 0.0 copy-start
  8.3 0.0 copy-start.1
  8.3 0.0 copy-start.2
  8.3 0.0 copy-start.3
  8.3 0.0 copy-start.4
  8.3 0.0 copy-start.5
  8.3 3.2 %gather_rows.3 = (bf16[768,128]{1,0:T(8,128)(2,1)S(1)}, bf16[768,128]{1,0:T(8,128)(2,1)S(1)}) custom-call(s32[4096]{0:T(1024)} %refs_0_.6, s32[1,16]{1,0:T(1,128)} %refs_0_.9, s32[1,16]{1,0:T(1,128)} %refs_1_.9, f32[32768,128]{1,0:T(8,128)S(1)} %get-tuple-element.30.refs_3_), custom_call_target="tpu_custom_call" | custom-call | tf_op jit(solution)/shard_map/gather_rows/pallas_call | solution.py:42
  11.5 0.5 %collective-permute-start.4 = (bf16[768,128]{1,0:T(8,128)(2,1)S(1)}, bf16[768,128]{1,0:T(8,128)(2,1)S(1)}, u32[]{:S(2)}, u32[]{:S(2)}) collective-permute-start(bf16[768,128]{1,0:T(8,128)(2,1)S(1)} %get-tuple-element.31.refs_2_), channel_id=1, source_target_pairs={{0,4},{4,0},{8,12},{12,8},{16,20},{20,16},{24,28},{28,24},{1,5},{5... | collective-permute-start | bytes 589832 | tf_op jit(solution)/shard_map/ppermute | solution.py:601
  12.0 0.0 collective-permute-done.refs_1_
  12.0 0.2 merge_columns.2
  12.2 3.4 %collective-permute-start.2 = (bf16[512,128]{1,0:T(8,128)(2,1)S(1)}, bf16[512,128]{1,0:T(8,128)(2,1)S(1)}, u32[]{:S(2)}, u32[]{:S(2)}) collective-permute-start(bf16[512,128]{1,0:T(8,128)(2,1)S(1)} %get-tuple-element.34), channel_id=1, source_target_pairs={{0,16},{4,20},{8,24},{12,28},{16,0},{20,4},{24,8},{28,12},{1,17},{... | collective-permute-start | bytes 393224 | tf_op jit(solution)/shard_map/ppermute | solution.py:607
  15.6 1.3 %collective-permute-start.1 = (bf16[512,128]{1,0:T(8,128)(2,1)S(1)}, bf16[512,128]{1,0:T(8,128)(2,1)S(1)}, u32[]{:S(2)}, u32[]{:S(2)}) collective-permute-start(bf16[512,128]{1,0:T(8,128)(2,1)S(1)} %get-tuple-element.33), channel_id=1, source_target_pairs={{0,8},{4,12},{8,16},{12,20},{16,24},{20,28},{24,0},{28,4},{1,9},{5... | collective-permute-start | bytes 393224 | tf_op jit(solution)/shard_map/ppermute | solution.py:607
  16.9 2.0 %collective-permute-start.3 = (bf16[512,128]{1,0:T(8,128)(2,1)S(1)}, bf16[512,128]{1,0:T(8,128)(2,1)S(1)}, u32[]{:S(2)}, u32[]{:S(2)}) collective-permute-start(bf16[512,128]{1,0:T(8,128)(2,1)S(1)} %get-tuple-element.35), channel_id=1, source_target_pairs={{0,24},{4,28},{8,0},{12,4},{16,8},{20,12},{24,16},{28,20},{1,25},{... | collective-permute-start | bytes 393224 | tf_op jit(solution)/shard_map/ppermute | solution.py:607
  18.9 0.0 collective-permute-done.4.refs_1_
  18.9 5.9 %collective-permute-done.2.refs_2_.refs_4_ = bf16[512,128]{1,0:T(8,128)(2,1)S(1)} collective-permute-done((bf16[512,128]{1,0:T(8,128)(2,1)S(1)}, bf16[512,128]{1,0:T(8,128)(2,1)S(1)}, u32[]{:S(2)}, u32[]{:S(2)}) %collective-permute-start.2) | collective-permute-done | bytes 131104 | tf_op jit(solution)/shard_map/ppermute | solution.py:607
  24.8 0.2 merge_columns.3
  24.9 0.1 collective-permute-start.5
  25.0 2.0 %collective-permute-start.9 = (bf16[384,128]{1,0:T(8,128)(2,1)S(1)}, bf16[384,128]{1,0:T(8,128)(2,1)S(1)}, u32[]{:S(2)}, u32[]{:S(2)}) collective-permute-start(bf16[384,128]{1,0:T(8,128)(2,1)S(1)} %get-tuple-element.40), channel_id=1, source_target_pairs={{0,16},{4,20},{8,24},{12,28},{16,0},{20,4},{24,8},{28,12},{1,17},{... | collective-permute-start | bytes 294920 | tf_op jit(solution)/shard_map/ppermute | solution.py:607
  27.0 1.3 %collective-permute-start.10 = (bf16[384,128]{1,0:T(8,128)(2,1)S(1)}, bf16[384,128]{1,0:T(8,128)(2,1)S(1)}, u32[]{:S(2)}, u32[]{:S(2)}) collective-permute-start(bf16[384,128]{1,0:T(8,128)(2,1)S(1)} %get-tuple-element.41), channel_id=1, source_target_pairs={{0,24},{4,28},{8,0},{12,4},{16,8},{20,12},{24,16},{28,20},{1,25},{... | collective-permute-start | bytes 294920 | tf_op jit(solution)/shard_map/ppermute | solution.py:607
  28.3 0.0 collective-permute-done.1.refs_3_.refs_1_
  28.3 0.0 collective-permute-done.3.refs_5_.refs_3_
  28.3 0.0 copy-done
  28.3 0.0 copy-done.1
  28.3 0.0 copy-done.2
  28.3 0.0 copy-done.3
  28.3 0.0 copy-done.4
  28.3 0.0 copy-done.5
  28.3 5.4 %layer.2 = (bf16[384,512]{1,0:T(8,128)(2,1)S(1)}, bf16[384,512]{1,0:T(8,128)(2,1)S(1)}, bf16[384,1024]{1,0:T(8,128)(2,1)S(1)}) custom-call(s32[1,16]{1,0:T(1,128)S(1)} %copy-done, s32[1,16]{1,0:T(1,128)S(1)} %copy-done.1, bf16[512,128]{1,0:T(8,128)(2,1)S(1)} %get-tuple-element.32.refs_2_.refs_0_, ...), custom_call_target="tpu_custom_call" | custom-call | flops 2415919104 | bytes 8053063 | tf_op jit(solution)/shard_map/layer/pallas_call | solution.py:42
  33.7 0.0 collective-permute-done.5.refs_5_.refs_3_
  33.8 0.2 unit_negatives.1.refs_0_
  33.9 2.0 %collective-permute-start.8 = (bf16[128,512]{1,0:T(8,128)(2,1)S(1)}, bf16[128,512]{1,0:T(8,128)(2,1)S(1)}, u32[]{:S(2)}, u32[]{:S(2)}) collective-permute-start(bf16[128,512]{1,0:T(8,128)(2,1)S(1)} %unit_negatives.1.refs_0_), channel_id=1, source_target_pairs={{0,3},{1,2},{2,1},{3,0},{4,7},{5,6},{6,5},{7,4},{8,11},{9,10},{10,... | collective-permute-start | bytes 393224 | tf_op jit(solution)/shard_map/ppermute | solution.py:626
  35.9 0.2 collective-permute-start.7
  36.1 0.5 %collective-permute-start.6 = (bf16[128,512]{1,0:T(8,128)(2,1)S(1)}, bf16[128,512]{1,0:T(8,128)(2,1)S(1)}, u32[]{:S(2)}, u32[]{:S(2)}) collective-permute-start(bf16[128,512]{1,0:T(8,128)(2,1)S(1)} %unit_negatives.1.refs_0_), channel_id=1, source_target_pairs={{0,1},{1,0},{2,3},{3,2},{4,5},{5,4},{6,7},{7,6},{8,9},{9,8},{10,11... | collective-permute-start | bytes 393224 | tf_op jit(solution)/shard_map/ppermute | solution.py:626
  36.6 0.0 collective-permute-done.9.refs_4_
  36.6 0.0 collective-permute-done.10.refs_5_
  36.6 5.9 %layer.3 = (bf16[384,512]{1,0:T(8,128)(2,1)S(1)}, bf16[384,512]{1,0:T(8,128)(2,1)S(1)}) custom-call(s32[1,16]{1,0:T(1,128)S(1)} %copy-done, s32[1,16]{1,0:T(1,128)S(1)} %copy-done.1, bf16[384,128]{1,0:T(8,128)(2,1)S(1)} %get-tuple-element.37.refs_10_.refs_2_, bf16[384,128]{1,0:T(8,128)(2,1)S(1)} %collective-permute-done.5.refs_5_.refs_3_, ...), custom_call_target="tpu_custom_call" | custom-call | flops 2415919104 | bytes 8053063 | tf_op jit(solution)/shard_map/layer/pallas_call | solution.py:42
  42.6 0.0 collective-permute-done.8.refs_3_
  42.6 0.0 collective-permute-done.7.refs_2_
  42.6 0.0 collective-permute-done.6.refs_1_
  42.6 3.0 %collective-permute-start.11 = (bf16[512,512]{1,0:T(8,128)(2,1)S(1)}, bf16[512,512]{1,0:T(8,128)(2,1)S(1)}, u32[]{:S(2)}, u32[]{:S(2)}) collective-permute-start(bf16[512,512]{1,0:T(8,128)(2,1)S(1)} %join.1.refs_2_), channel_id=1, source_target_pairs={{0,4},{4,0},{8,12},{12,8},{16,20},{20,16},{24,28},{28,24},{1,5},{5... | collective-permute-start | bytes 1572872 | tf_op jit(solution)/shard_map/ppermute | solution.py:629
  45.7 2.1 %near_gradient.1 = (f32[768,512]{1,0:T(8,128)S(1)}, f32[768,1]{1,0:T(8,128)S(1)}, f32[768,1]{1,0:T(8,128)S(1)}, bf16[768,512]{1,0:T(8,128)(2,1)S(1)}, bf16[768,512]{1,0:T(8,128)(2,1)S(1)}) custom-call(s32[1,16]{1,0:T(1,128)S(1)} %copy-done, s32[1,16]{1,0:T(1,128)S(1)} %copy-done.1, bf16[512,512]{1,0:T(8,128)(2,1)S(1)} %join.1.refs_2_, ...), custom_call_target="tpu_custom_call" | custom-call | flops 1207959552 | bytes 4026531 | tf_op jit(solution)/shard_map/near_gradient/pallas_call | solution.py:42
  47.7 0.0 collective-permute-done.11.far_ref
  47.8 2.5 %far_gradient.1 = f32[768,512]{1,0:T(8,128)} custom-call(bf16[512,512]{1,0:T(8,128)(2,1)S(1)} %collective-permute-done.11.far_ref, f32[768,512]{1,0:T(8,128)S(1)} %get-tuple-element.46.sum_ref, f32[768,1]{1,0:T(8,128)S(1)} %get-tuple-element.47.total_ref, f32[768,1]{1,0:T(8,128)S(1)} %get-tuple-element.48.positive_ref, ...), custom_call_target="tpu_custom_call" | custom-call | tf_op jit(solution)/shard_map/far_gradient/pallas_call | solution.py:565
  (1 shorter events, 0.0 us)
Async XLA Ops:
  8.2 3.9 %collective-permute-start = (bf16[832,128]{1,0:T(8,128)(2,1)S(1)}, bf16[832,128]{1,0:T(8,128)(2,1)S(1)}, u32[]{:S(2)}, u32[]{:S(2)}) collective-permute-start(bf16[832,128]{1,0:T(8,128)(2,1)S(1)} %get-tuple-element.29), channel_id=1, source_target_pairs={{0,4},{4,0},{8,12},{12,8},{16,20},{20,16},{24,28},{28,24},{1,5},{5... | collective-permute-start | bytes 638984 | tf_op jit(solution)/shard_map/ppermute | solution.py:601
  8.3 20.0 %copy-start = (s32[1,16]{1,0:T(1,128)S(1)}, s32[1,16]{1,0:T(1,128)}, u32[]{:S(2)}) copy-start(s32[1,16]{1,0:T(1,128)} %refs_0_.9) | copy-start | bytes 196
  8.3 20.0 %copy-start.1 = (s32[1,16]{1,0:T(1,128)S(1)}, s32[1,16]{1,0:T(1,128)}, u32[]{:S(2)}) copy-start(s32[1,16]{1,0:T(1,128)} %refs_1_.9) | copy-start | bytes 196
  8.3 20.0 %copy-start.2 = (bf16[512,2048]{1,0:T(8,128)(2,1)S(1)}, bf16[512,2048]{1,0:T(8,128)(2,1)}, u32[]{:S(2)}) copy-start(bf16[512,2048]{1,0:T(8,128)(2,1)} %refs_6_.3) | copy-start | bytes 6291460
  8.3 20.0 %copy-start.3 = (bf16[2048,512]{1,0:T(8,128)(2,1)S(1)}, bf16[2048,512]{1,0:T(8,128)(2,1)}, u32[]{:S(2)}) copy-start(bf16[2048,512]{1,0:T(8,128)(2,1)} %refs_7_.3) | copy-start | bytes 6291460
  8.3 20.0 %copy-start.4 = (bf16[512,2048]{1,0:T(8,128)(2,1)S(1)}, bf16[512,2048]{1,0:T(8,128)(2,1)}, u32[]{:S(2)}) copy-start(bf16[512,2048]{1,0:T(8,128)(2,1)} %refs_8_.3) | copy-start | bytes 6291460
  8.3 20.0 %copy-start.5 = (bf16[512,512]{1,0:T(8,128)(2,1)S(1)}, bf16[512,512]{1,0:T(8,128)(2,1)}, u32[]{:S(2)}) copy-start(bf16[512,512]{1,0:T(8,128)(2,1)} %refs_9_.3) | copy-start | bytes 1572868
  11.5 7.4 %collective-permute-start.4 = (bf16[768,128]{1,0:T(8,128)(2,1)S(1)}, bf16[768,128]{1,0:T(8,128)(2,1)S(1)}, u32[]{:S(2)}, u32[]{:S(2)}) collective-permute-start(bf16[768,128]{1,0:T(8,128)(2,1)S(1)} %get-tuple-element.31.refs_2_), channel_id=1, source_target_pairs={{0,4},{4,0},{8,12},{12,8},{16,20},{20,16},{24,28},{28,24},{1,5},{5... | collective-permute-start | bytes 589832 | tf_op jit(solution)/shard_map/ppermute | solution.py:601
  12.2 12.6 %collective-permute-start.2 = (bf16[512,128]{1,0:T(8,128)(2,1)S(1)}, bf16[512,128]{1,0:T(8,128)(2,1)S(1)}, u32[]{:S(2)}, u32[]{:S(2)}) collective-permute-start(bf16[512,128]{1,0:T(8,128)(2,1)S(1)} %get-tuple-element.34), channel_id=1, source_target_pairs={{0,16},{4,20},{8,24},{12,28},{16,0},{20,4},{24,8},{28,12},{1,17},{... | collective-permute-start | bytes 393224 | tf_op jit(solution)/shard_map/ppermute | solution.py:607
  15.6 12.6 %collective-permute-start.1 = (bf16[512,128]{1,0:T(8,128)(2,1)S(1)}, bf16[512,128]{1,0:T(8,128)(2,1)S(1)}, u32[]{:S(2)}, u32[]{:S(2)}) collective-permute-start(bf16[512,128]{1,0:T(8,128)(2,1)S(1)} %get-tuple-element.33), channel_id=1, source_target_pairs={{0,8},{4,12},{8,16},{12,20},{16,24},{20,28},{24,0},{28,4},{1,9},{5... | collective-permute-start | bytes 393224 | tf_op jit(solution)/shard_map/ppermute | solution.py:607
  16.9 11.3 %collective-permute-start.3 = (bf16[512,128]{1,0:T(8,128)(2,1)S(1)}, bf16[512,128]{1,0:T(8,128)(2,1)S(1)}, u32[]{:S(2)}, u32[]{:S(2)}) collective-permute-start(bf16[512,128]{1,0:T(8,128)(2,1)S(1)} %get-tuple-element.35), channel_id=1, source_target_pairs={{0,24},{4,28},{8,0},{12,4},{16,8},{20,12},{24,16},{28,20},{1,25},{... | collective-permute-start | bytes 393224 | tf_op jit(solution)/shard_map/ppermute | solution.py:607
  24.9 8.8 %collective-permute-start.5 = (bf16[384,128]{1,0:T(8,128)(2,1)S(1)}, bf16[384,128]{1,0:T(8,128)(2,1)S(1)}, u32[]{:S(2)}, u32[]{:S(2)}) collective-permute-start(bf16[384,128]{1,0:T(8,128)(2,1)S(1)} %get-tuple-element.39), channel_id=1, source_target_pairs={{0,8},{4,12},{8,16},{12,20},{16,24},{20,28},{24,0},{28,4},{1,9},{5... | collective-permute-start | bytes 294920 | tf_op jit(solution)/shard_map/ppermute | solution.py:607
  25.0 11.6 %collective-permute-start.9 = (bf16[384,128]{1,0:T(8,128)(2,1)S(1)}, bf16[384,128]{1,0:T(8,128)(2,1)S(1)}, u32[]{:S(2)}, u32[]{:S(2)}) collective-permute-start(bf16[384,128]{1,0:T(8,128)(2,1)S(1)} %get-tuple-element.40), channel_id=1, source_target_pairs={{0,16},{4,20},{8,24},{12,28},{16,0},{20,4},{24,8},{28,12},{1,17},{... | collective-permute-start | bytes 294920 | tf_op jit(solution)/shard_map/ppermute | solution.py:607
  27.0 9.7 %collective-permute-start.10 = (bf16[384,128]{1,0:T(8,128)(2,1)S(1)}, bf16[384,128]{1,0:T(8,128)(2,1)S(1)}, u32[]{:S(2)}, u32[]{:S(2)}) collective-permute-start(bf16[384,128]{1,0:T(8,128)(2,1)S(1)} %get-tuple-element.41), channel_id=1, source_target_pairs={{0,24},{4,28},{8,0},{12,4},{16,8},{20,12},{24,16},{28,20},{1,25},{... | collective-permute-start | bytes 294920 | tf_op jit(solution)/shard_map/ppermute | solution.py:607
  33.9 8.6 %collective-permute-start.8 = (bf16[128,512]{1,0:T(8,128)(2,1)S(1)}, bf16[128,512]{1,0:T(8,128)(2,1)S(1)}, u32[]{:S(2)}, u32[]{:S(2)}) collective-permute-start(bf16[128,512]{1,0:T(8,128)(2,1)S(1)} %unit_negatives.1.refs_0_), channel_id=1, source_target_pairs={{0,3},{1,2},{2,1},{3,0},{4,7},{5,6},{6,5},{7,4},{8,11},{9,10},{10,... | collective-permute-start | bytes 393224 | tf_op jit(solution)/shard_map/ppermute | solution.py:626
  35.9 6.7 %collective-permute-start.7 = (bf16[128,512]{1,0:T(8,128)(2,1)S(1)}, bf16[128,512]{1,0:T(8,128)(2,1)S(1)}, u32[]{:S(2)}, u32[]{:S(2)}) collective-permute-start(bf16[128,512]{1,0:T(8,128)(2,1)S(1)} %unit_negatives.1.refs_0_), channel_id=1, source_target_pairs={{0,2},{1,3},{2,0},{3,1},{4,6},{5,7},{6,4},{7,5},{8,10},{9,11},{10,... | collective-permute-start | bytes 393224 | tf_op jit(solution)/shard_map/ppermute | solution.py:626
  36.1 6.5 %collective-permute-start.6 = (bf16[128,512]{1,0:T(8,128)(2,1)S(1)}, bf16[128,512]{1,0:T(8,128)(2,1)S(1)}, u32[]{:S(2)}, u32[]{:S(2)}) collective-permute-start(bf16[128,512]{1,0:T(8,128)(2,1)S(1)} %unit_negatives.1.refs_0_), channel_id=1, source_target_pairs={{0,1},{1,0},{2,3},{3,2},{4,5},{5,4},{6,7},{7,6},{8,9},{9,8},{10,11... | collective-permute-start | bytes 393224 | tf_op jit(solution)/shard_map/ppermute | solution.py:626
  42.6 5.1 %collective-permute-start.11 = (bf16[512,512]{1,0:T(8,128)(2,1)S(1)}, bf16[512,512]{1,0:T(8,128)(2,1)S(1)}, u32[]{:S(2)}, u32[]{:S(2)}) collective-permute-start(bf16[512,512]{1,0:T(8,128)(2,1)S(1)} %join.1.refs_2_), channel_id=1, source_target_pairs={{0,4},{4,0},{8,12},{12,8},{16,20},{20,16},{24,28},{28,24},{1,5},{5... | collective-permute-start | bytes 1572872 | tf_op jit(solution)/shard_map/ppermute | solution.py:629

commit v6 on v5

--- a/solution.py
+++ b/solution.py
@@ -135,7 +135,7 @@
     if negatives:
         neg_in, table_ref, rows_ref, keep_ref, give_ref = refs[3:8]
     else:
-        rows_ref, keep_ref, give_ref = refs[3:6]
+        rows_ref, keep_ref, give_ref, second_ref = refs[3:7]
     ids_ref, len_ref, own_ref, neg_ref, stage_ref, next_ref, small_sem = refs[-7:]
     smalls = [(ids_in, ids_ref), (len_in, len_ref), (own_in, own_ref)]
     if negatives:
@@ -198,9 +198,23 @@
             def _():
                 keep_ref[pl.ds(at, HALF), :] = block
 
-            @pl.when(jnp.logical_not(mine))
-            def _():
-                give_ref[pl.ds(at, HALF), :] = block
+            if negatives:
+
+                @pl.when(jnp.logical_not(mine))
+                def _():
+                    give_ref[pl.ds(at, HALF), :] = block
+
+            else:
+                late = shift >= chips // 2
+                border = chips // 2 * size * HALF
+
+                @pl.when(jnp.logical_not(mine) & jnp.logical_not(late))
+                def _():
+                    give_ref[pl.ds(at, HALF), :] = block
+
+                @pl.when(jnp.logical_not(mine) & late)
+                def _():
+                    second_ref[pl.ds(pl.multiple_of(at - border, HALF), HALF), :] = block
 
             return carry
 
@@ -212,7 +226,9 @@
     lax.fori_loop(0, len_ref.shape[1], sequence, 0)
 
 
-def gather_rows(event_ids, seq_lengths, seq_owner, negative_ids, table, rows, tables, start, size):
+def gather_rows(
+    event_ids, seq_lengths, seq_owner, negative_ids, table, rows, tables, start, size, after
+):
     chips = tables // 2
     negatives = rows is None
     neg_half = negative_ids.shape[0] // 4
@@ -240,20 +256,26 @@
             pltpu.SemaphoreType.DMA((2, COPY_PARTS)),
         ] + scratch
     else:
+        part = jax.ShapeDtypeStruct((chips // 2 * size * HALF, lanes), BF)
+        out_shape = [block, part, part]
         operands.append(rows)
         in_specs.append(vmem())
     kernel = functools.partial(gather_kernel, tables, start, size, negatives)
-    return run(kernel, operands, in_specs, out_shape, scratch, 28, "gather_rows")
-
-
-def merge_kernel(chips, pages, neg_half, keep_ref, got_ref, *out_refs):
+    return run(kernel, operands, in_specs, out_shape, scratch, 28, "gather_rows", after)
+
+
+def merge_kernel(chips, pages, neg_half, keep_ref, *refs):
+    got_refs, out_refs = refs[:-chips], refs[-chips:]
     core = lax.axis_index("table") % 2
     width = keep_ref.shape[1] // 2
     own_lanes = (lane_ids((1, 2 * width)) < width) == (core == 0)
 
     def merged(at, half):
         own = keep_ref[at : at + half, :].astype(F32)
-        other = got_ref[at : at + half, :].astype(F32)
+        got_ref, low_at = got_refs[0], at
+        if len(got_refs) > 1 and at >= got_ref.shape[0]:
+            got_ref, low_at = got_refs[1], at - got_ref.shape[0]
+        other = got_ref[low_at : low_at + half, :].astype(F32)
         top = jnp.where(own_lanes, own, other)
         low = swap_halves(jnp.where(own_lanes, other, own))
         return top.astype(BF), low.astype(BF)
@@ -274,8 +296,8 @@
 def merge_columns(keep, got, chips, pages, neg_half, after):
     shape = jax.ShapeDtypeStruct((pages * PAGE + 2 * neg_half, keep.shape[1]), BF)
     kernel = functools.partial(merge_kernel, chips, pages, neg_half)
-    specs = [vmem(), vmem()]
-    return run(kernel, [keep, got], specs, [shape] * chips, [], 12, "merge_columns", after)
+    specs = [vmem()] * (1 + len(got))
+    return run(kernel, [keep, *got], specs, [shape] * chips, [], 12, "merge_columns", after)
 
 
 def source_chip(s, chips):
@@ -585,27 +607,23 @@
     event_ids, negative_ids = stay(event_ids), stay(negative_ids)
     lengths, owners = stay(seq_lengths), stay(seq_owner)
     rows, first = None, 0
-    packed = []
-    for size in CHUNKS:
+    arrived, after, gate = [], [], []
+    for c, size in enumerate(CHUNKS):
         outs = gather_rows(
-            event_ids, lengths, owners, negative_ids, table, rows, tables, first, size
+            event_ids, lengths, owners, negative_ids, table, rows, tables, first, size, after
         )
         if rows is None:
             rows = outs[0]
-        packed.append(outs[-2:])
-        first += size
-    packed.append(())
-    arrived = []
-    for c, size in enumerate(CHUNKS):
-        keep, give = packed[c]
-        got = lax.ppermute(give, "table", cores)
-        own_neg = neg_half if c == 0 else 0
-        after = list(packed[c + 1][-1:]) + (arrived[0][EARLIER] if c else [])
-        blocks = list(merge_columns(keep, got, chips, size, own_neg, after))
+        keep, *gives = outs[1:] if c == 0 else outs
+        got = [lax.ppermute(give, "table", cores) for give in gives]
+        blocks = list(merge_columns(keep, got, chips, size, neg_half if c == 0 else 0, gate))
+        after = blocks[:1]
         for s in range(1, chips):
             moves = [(t, (t // 2 + s) % chips * 2 + t % 2) for t in range(tables)]
             blocks[s] = lax.ppermute(blocks[s], "table", moves)
+        gate = blocks[EARLIER]
         arrived.append(blocks)
+        first += size
     arrived.append(())
 
     weights = (w_in, w_mid, w_uvqk, w_proj)

time: 50.4 us -> 48.2 us (0.956)
  waiting for transfers between devices: 5.9 us -> 2.66 us
  starting transfers between devices: 16.4 us -> 17.3 us
    ppermute x6, waiting for transfers between devices: 5.88 us -> 0.02 us  [on_device(): blocks[s] = lax.ppermute(blocks[s], 'table', moves)]
    ppermute x2 -> x3, waiting for transfers between devices: 0.01 us -> 2.63 us  [on_device(): got = [lax.ppermute(give, 'table', cores) for give in gives]]
    ppermute x2 -> x3, starting transfers between devices: 0.64 us -> 1.48 us  [on_device(): got = [lax.ppermute(give, 'table', cores) for give in gives]]
  transfers between devices with their start and end apart: 12 -> 13, of which waited for: 1 -> 3; matrix products, arithmetic and copies ran while one was open for 0% -> 0% of each run, Pallas kernels for 34% -> 36%
where the time goes in v6:
time: 48.2 us; the launch traced here: 48.1 us
  Pallas kernels  27.9 us (58%)
  starting transfers between devices  17.3 us (36%)
  waiting for transfers between devices  2.66 us (6%)
    pallas_call x9, Pallas kernels, run(): pl.pallas_call(body, out_shape=out_shape, in_specs=in_specs + [anywhere()...  25.4 us
    ppermute x6, starting transfers between devices, on_device(): blocks[s] = lax.ppermute(blocks[s], 'table', moves)  10.1 us
    ppermute x1, starting transfers between devices, on_device(): far = lax.ppermute(near, 'table', cores)  3.02 us
    ppermute x3, starting transfers between devices, on_device(): parts.append(lax.ppermute(own, 'user', [(u, u ^ s) for u in range(users)]))  2.71 us
    ppermute x3, waiting for transfers between devices, on_device(): got = [lax.ppermute(give, 'table', cores) for give in gives]  2.63 us
    pallas_call x1, Pallas kernels, far_gradient(): pl.pallas_call(far_kernel, grid=(rows // block,), out_shape=jax.ShapeDtyp...  2.53 us
    ppermute x3, starting transfers between devices, on_device(): got = [lax.ppermute(give, 'table', cores) for give in gives]  1.48 us
  transfers between devices with their start and end apart: 13, of which 3 were waited for; matrix products, arithmetic and copies ran while one was open for 0% of the time, Pallas kernels for 36%

profile of v6, /device:TPU:1, one launch (start us, length us, event | category | flops | bytes accessed | tf_op | source)
XLA Modules:
  0.0 48.1 jit_solution(12578742201835732133)
XLA Ops:
  0.0 8.0 %gather_rows.2 = (f32[32768,128]{1,0:T(8,128)S(1)}, bf16[832,128]{1,0:T(8,128)(2,1)S(1)}, bf16[832,128]{1,0:T(8,128)(2,1)S(1)}) custom-call(s32[4096]{0:T(1024)} %refs_0_.6, s32[1,16]{1,0:T(1,128)} %refs_0_.9, s32[1,16]{1,0:T(1,128)} %refs_1_.9, s32[256]{0:T(256)} %refs_3_.1, bf16[64,32768]{1,0:T(8,128)(2,1)} %bitcast.1), custom_call_target="tpu_custom_call" | custom-call | tf_op jit(solution)/shard_map/gather_rows/pallas_call | solution.py:42
  8.0 0.1 collective-permute-start
  8.1 1.4 %collective-permute-done.refs_1_ = bf16[832,128]{1,0:T(8,128)(2,1)S(1)} collective-permute-done((bf16[832,128]{1,0:T(8,128)(2,1)S(1)}, bf16[832,128]{1,0:T(8,128)(2,1)S(1)}, u32[]{:S(2)}, u32[]{:S(2)}) %collective-permute-start) | collective-permute-done | bytes 213024 | tf_op jit(solution)/shard_map/ppermute | solution.py:618
  9.5 0.2 merge_columns.2
  9.7 3.5 %collective-permute-start.2 = (bf16[512,128]{1,0:T(8,128)(2,1)S(1)}, bf16[512,128]{1,0:T(8,128)(2,1)S(1)}, u32[]{:S(2)}, u32[]{:S(2)}) collective-permute-start(bf16[512,128]{1,0:T(8,128)(2,1)S(1)} %get-tuple-element.33), channel_id=1, source_target_pairs={{0,16},{4,20},{8,24},{12,28},{16,0},{20,4},{24,8},{28,12},{1,17},{... | collective-permute-start | bytes 393224 | tf_op jit(solution)/shard_map/ppermute | solution.py:623
  13.2 1.3 %collective-permute-start.1 = (bf16[512,128]{1,0:T(8,128)(2,1)S(1)}, bf16[512,128]{1,0:T(8,128)(2,1)S(1)}, u32[]{:S(2)}, u32[]{:S(2)}) collective-permute-start(bf16[512,128]{1,0:T(8,128)(2,1)S(1)} %get-tuple-element.32), channel_id=1, source_target_pairs={{0,8},{4,12},{8,16},{12,20},{16,24},{20,28},{24,0},{28,4},{1,9},{5... | collective-permute-start | bytes 393224 | tf_op jit(solution)/shard_map/ppermute | solution.py:623
  14.5 2.0 %collective-permute-start.3 = (bf16[512,128]{1,0:T(8,128)(2,1)S(1)}, bf16[512,128]{1,0:T(8,128)(2,1)S(1)}, u32[]{:S(2)}, u32[]{:S(2)}) collective-permute-start(bf16[512,128]{1,0:T(8,128)(2,1)S(1)} %get-tuple-element.34), channel_id=1, source_target_pairs={{0,24},{4,28},{8,0},{12,4},{16,8},{20,12},{24,16},{28,20},{1,25},{... | collective-permute-start | bytes 393224 | tf_op jit(solution)/shard_map/ppermute | solution.py:623
  16.5 0.0 copy-start
  16.5 0.0 copy-start.1
  16.5 0.0 copy-start.2
  16.5 0.0 copy-start.3
  16.5 0.0 copy-start.4
  16.5 0.0 copy-start.5
  16.5 3.4 %gather_rows.3 = (bf16[768,128]{1,0:T(8,128)(2,1)S(1)}, bf16[384,128]{1,0:T(8,128)(2,1)S(1)}, bf16[384,128]{1,0:T(8,128)(2,1)S(1)}) custom-call(s32[4096]{0:T(1024)} %refs_0_.6, s32[1,16]{1,0:T(1,128)} %refs_0_.9, s32[1,16]{1,0:T(1,128)} %refs_1_.9, f32[32768,128]{1,0:T(8,128)S(1)} %get-tuple-element.35.refs_3_, ...), custom_call_target="tpu_custom_call" | custom-call | tf_op jit(solution)/shard_map/gather_rows/pallas_call | solution.py:42
  19.9 1.3 %collective-permute-start.4 = (bf16[384,128]{1,0:T(8,128)(2,1)S(1)}, bf16[384,128]{1,0:T(8,128)(2,1)S(1)}, u32[]{:S(2)}, u32[]{:S(2)}) collective-permute-start(bf16[384,128]{1,0:T(8,128)(2,1)S(1)} %get-tuple-element.37), channel_id=1, source_target_pairs={{0,4},{4,0},{8,12},{12,8},{16,20},{20,16},{24,28},{28,24},{1,5},{5... | collective-permute-start | bytes 294920 | tf_op jit(solution)/shard_map/ppermute | solution.py:618
  21.2 0.1 collective-permute-start.5
  21.3 0.9 %collective-permute-done.4.refs_1_ = bf16[384,128]{1,0:T(8,128)(2,1)S(1)} collective-permute-done((bf16[384,128]{1,0:T(8,128)(2,1)S(1)}, bf16[384,128]{1,0:T(8,128)(2,1)S(1)}, u32[]{:S(2)}, u32[]{:S(2)}) %collective-permute-start.4) | collective-permute-done | bytes 98336 | tf_op jit(solution)/shard_map/ppermute | solution.py:618
  22.2 0.4 collective-permute-done.5.refs_2_
  22.5 0.0 collective-permute-done.2.refs_3_.refs_4_.refs_2_
  22.5 0.2 merge_columns.3
  22.7 0.1 collective-permute-start.6
  22.8 1.7 %collective-permute-start.10 = (bf16[384,128]{1,0:T(8,128)(2,1)S(1)}, bf16[384,128]{1,0:T(8,128)(2,1)S(1)}, u32[]{:S(2)}, u32[]{:S(2)}) collective-permute-start(bf16[384,128]{1,0:T(8,128)(2,1)S(1)} %get-tuple-element.42), channel_id=1, source_target_pairs={{0,16},{4,20},{8,24},{12,28},{16,0},{20,4},{24,8},{28,12},{1,17},{... | collective-permute-start | bytes 294920 | tf_op jit(solution)/shard_map/ppermute | solution.py:623
  24.4 1.6 %collective-permute-start.11 = (bf16[384,128]{1,0:T(8,128)(2,1)S(1)}, bf16[384,128]{1,0:T(8,128)(2,1)S(1)}, u32[]{:S(2)}, u32[]{:S(2)}) collective-permute-start(bf16[384,128]{1,0:T(8,128)(2,1)S(1)} %get-tuple-element.43), channel_id=1, source_target_pairs={{0,24},{4,28},{8,0},{12,4},{16,8},{20,12},{24,16},{28,20},{1,25},{... | collective-permute-start | bytes 294920 | tf_op jit(solution)/shard_map/ppermute | solution.py:623
  26.0 0.0 collective-permute-done.1.refs_3_.refs_1_
  26.0 0.0 collective-permute-done.3.refs_5_.refs_3_
  26.0 0.0 copy-done
  26.0 0.0 copy-done.1
  26.0 0.0 copy-done.2
  26.1 0.0 copy-done.3
  26.1 0.0 copy-done.4
  26.1 0.0 copy-done.5
  26.1 5.4 %layer.2 = (bf16[384,512]{1,0:T(8,128)(2,1)S(1)}, bf16[384,512]{1,0:T(8,128)(2,1)S(1)}, bf16[384,1024]{1,0:T(8,128)(2,1)S(1)}) custom-call(s32[1,16]{1,0:T(1,128)S(1)} %copy-done, s32[1,16]{1,0:T(1,128)S(1)} %copy-done.1, bf16[512,128]{1,0:T(8,128)(2,1)S(1)} %get-tuple-element.31.refs_4_.refs_2_.refs_0_, ...), custom_call_target="tpu_custom_call" | custom-call | flops 2415919104 | bytes 8053063 | tf_op jit(solution)/shard_map/layer/pallas_call | solution.py:42
  31.5 0.0 collective-permute-done.6.refs_5_.refs_3_
  31.5 0.2 unit_negatives.1.refs_0_
  31.7 2.2 %collective-permute-start.9 = (bf16[128,512]{1,0:T(8,128)(2,1)S(1)}, bf16[128,512]{1,0:T(8,128)(2,1)S(1)}, u32[]{:S(2)}, u32[]{:S(2)}) collective-permute-start(bf16[128,512]{1,0:T(8,128)(2,1)S(1)} %unit_negatives.1.refs_0_), channel_id=1, source_target_pairs={{0,3},{1,2},{2,1},{3,0},{4,7},{5,6},{6,5},{7,4},{8,11},{9,10},{10,... | collective-permute-start | bytes 393224 | tf_op jit(solution)/shard_map/ppermute | solution.py:644
  33.9 0.2 collective-permute-start.8
  34.2 0.3 collective-permute-start.7
  34.4 0.0 collective-permute-done.10.refs_4_
  34.4 0.0 collective-permute-done.11.refs_5_
  34.4 5.9 %layer.3 = (bf16[384,512]{1,0:T(8,128)(2,1)S(1)}, bf16[384,512]{1,0:T(8,128)(2,1)S(1)}) custom-call(s32[1,16]{1,0:T(1,128)S(1)} %copy-done, s32[1,16]{1,0:T(1,128)S(1)} %copy-done.1, bf16[384,128]{1,0:T(8,128)(2,1)S(1)} %get-tuple-element.39.refs_10_.refs_2_, bf16[384,128]{1,0:T(8,128)(2,1)S(1)} %collective-permute-done.6.refs_5_.refs_3_, ...), custom_call_target="tpu_custom_call" | custom-call | flops 2415919104 | bytes 8053063 | tf_op jit(solution)/shard_map/layer/pallas_call | solution.py:42
  40.4 0.0 collective-permute-done.9.refs_3_
  40.4 0.0 collective-permute-done.8.refs_2_
  40.4 0.0 collective-permute-done.7.refs_1_
  40.4 3.0 %collective-permute-start.12 = (bf16[512,512]{1,0:T(8,128)(2,1)S(1)}, bf16[512,512]{1,0:T(8,128)(2,1)S(1)}, u32[]{:S(2)}, u32[]{:S(2)}) collective-permute-start(bf16[512,512]{1,0:T(8,128)(2,1)S(1)} %join.1.refs_2_), channel_id=1, source_target_pairs={{0,4},{4,0},{8,12},{12,8},{16,20},{20,16},{24,28},{28,24},{1,5},{5... | collective-permute-start | bytes 1572872 | tf_op jit(solution)/shard_map/ppermute | solution.py:647
  43.5 2.1 %near_gradient.1 = (f32[768,512]{1,0:T(8,128)S(1)}, f32[768,1]{1,0:T(8,128)S(1)}, f32[768,1]{1,0:T(8,128)S(1)}, bf16[768,512]{1,0:T(8,128)(2,1)S(1)}, bf16[768,512]{1,0:T(8,128)(2,1)S(1)}) custom-call(s32[1,16]{1,0:T(1,128)S(1)} %copy-done, s32[1,16]{1,0:T(1,128)S(1)} %copy-done.1, bf16[512,512]{1,0:T(8,128)(2,1)S(1)} %join.1.refs_2_, ...), custom_call_target="tpu_custom_call" | custom-call | flops 1207959552 | bytes 4026531 | tf_op jit(solution)/shard_map/near_gradient/pallas_call | solution.py:42
  45.5 0.0 collective-permute-done.12.far_ref
  45.6 2.5 %far_gradient.1 = f32[768,512]{1,0:T(8,128)} custom-call(bf16[512,512]{1,0:T(8,128)(2,1)S(1)} %collective-permute-done.12.far_ref, f32[768,512]{1,0:T(8,128)S(1)} %get-tuple-element.48.sum_ref, f32[768,1]{1,0:T(8,128)S(1)} %get-tuple-element.49.total_ref, f32[768,1]{1,0:T(8,128)S(1)} %get-tuple-element.50.positive_ref, ...), custom_call_target="tpu_custom_call" | custom-call | tf_op jit(solution)/shard_map/far_gradient/pallas_call | solution.py:587
  (1 shorter events, 0.0 us)
Async XLA Ops:
  8.0 1.5 %collective-permute-start = (bf16[832,128]{1,0:T(8,128)(2,1)S(1)}, bf16[832,128]{1,0:T(8,128)(2,1)S(1)}, u32[]{:S(2)}, u32[]{:S(2)}) collective-permute-start(bf16[832,128]{1,0:T(8,128)(2,1)S(1)} %get-tuple-element.30), channel_id=1, source_target_pairs={{0,4},{4,0},{8,12},{12,8},{16,20},{20,16},{24,28},{28,24},{1,5},{5... | collective-permute-start | bytes 638984 | tf_op jit(solution)/shard_map/ppermute | solution.py:618
  9.7 12.8 %collective-permute-start.2 = (bf16[512,128]{1,0:T(8,128)(2,1)S(1)}, bf16[512,128]{1,0:T(8,128)(2,1)S(1)}, u32[]{:S(2)}, u32[]{:S(2)}) collective-permute-start(bf16[512,128]{1,0:T(8,128)(2,1)S(1)} %get-tuple-element.33), channel_id=1, source_target_pairs={{0,16},{4,20},{8,24},{12,28},{16,0},{20,4},{24,8},{28,12},{1,17},{... | collective-permute-start | bytes 393224 | tf_op jit(solution)/shard_map/ppermute | solution.py:623
  13.2 12.8 %collective-permute-start.1 = (bf16[512,128]{1,0:T(8,128)(2,1)S(1)}, bf16[512,128]{1,0:T(8,128)(2,1)S(1)}, u32[]{:S(2)}, u32[]{:S(2)}) collective-permute-start(bf16[512,128]{1,0:T(8,128)(2,1)S(1)} %get-tuple-element.32), channel_id=1, source_target_pairs={{0,8},{4,12},{8,16},{12,20},{16,24},{20,28},{24,0},{28,4},{1,9},{5... | collective-permute-start | bytes 393224 | tf_op jit(solution)/shard_map/ppermute | solution.py:623
  14.5 11.5 %collective-permute-start.3 = (bf16[512,128]{1,0:T(8,128)(2,1)S(1)}, bf16[512,128]{1,0:T(8,128)(2,1)S(1)}, u32[]{:S(2)}, u32[]{:S(2)}) collective-permute-start(bf16[512,128]{1,0:T(8,128)(2,1)S(1)} %get-tuple-element.34), channel_id=1, source_target_pairs={{0,24},{4,28},{8,0},{12,4},{16,8},{20,12},{24,16},{28,20},{1,25},{... | collective-permute-start | bytes 393224 | tf_op jit(solution)/shard_map/ppermute | solution.py:623
  16.5 9.6 %copy-start = (s32[1,16]{1,0:T(1,128)S(1)}, s32[1,16]{1,0:T(1,128)}, u32[]{:S(2)}) copy-start(s32[1,16]{1,0:T(1,128)} %refs_0_.9) | copy-start | bytes 196
  16.5 9.6 %copy-start.1 = (s32[1,16]{1,0:T(1,128)S(1)}, s32[1,16]{1,0:T(1,128)}, u32[]{:S(2)}) copy-start(s32[1,16]{1,0:T(1,128)} %refs_1_.9) | copy-start | bytes 196
  16.5 9.6 %copy-start.2 = (bf16[512,2048]{1,0:T(8,128)(2,1)S(1)}, bf16[512,2048]{1,0:T(8,128)(2,1)}, u32[]{:S(2)}) copy-start(bf16[512,2048]{1,0:T(8,128)(2,1)} %refs_6_.3) | copy-start | bytes 6291460
  16.5 9.6 %copy-start.3 = (bf16[2048,512]{1,0:T(8,128)(2,1)S(1)}, bf16[2048,512]{1,0:T(8,128)(2,1)}, u32[]{:S(2)}) copy-start(bf16[2048,512]{1,0:T(8,128)(2,1)} %refs_7_.3) | copy-start | bytes 6291460
  16.5 9.6 %copy-start.4 = (bf16[512,2048]{1,0:T(8,128)(2,1)S(1)}, bf16[512,2048]{1,0:T(8,128)(2,1)}, u32[]{:S(2)}) copy-start(bf16[512,2048]{1,0:T(8,128)(2,1)} %refs_8_.3) | copy-start | bytes 6291460
  16.5 9.6 %copy-start.5 = (bf16[512,512]{1,0:T(8,128)(2,1)S(1)}, bf16[512,512]{1,0:T(8,128)(2,1)}, u32[]{:S(2)}) copy-start(bf16[512,512]{1,0:T(8,128)(2,1)} %refs_9_.3) | copy-start | bytes 1572868
  19.9 2.2 %collective-permute-start.4 = (bf16[384,128]{1,0:T(8,128)(2,1)S(1)}, bf16[384,128]{1,0:T(8,128)(2,1)S(1)}, u32[]{:S(2)}, u32[]{:S(2)}) collective-permute-start(bf16[384,128]{1,0:T(8,128)(2,1)S(1)} %get-tuple-element.37), channel_id=1, source_target_pairs={{0,4},{4,0},{8,12},{12,8},{16,20},{20,16},{24,28},{28,24},{1,5},{5... | collective-permute-start | bytes 294920 | tf_op jit(solution)/shard_map/ppermute | solution.py:618
  21.2 1.3 %collective-permute-start.5 = (bf16[384,128]{1,0:T(8,128)(2,1)S(1)}, bf16[384,128]{1,0:T(8,128)(2,1)S(1)}, u32[]{:S(2)}, u32[]{:S(2)}) collective-permute-start(bf16[384,128]{1,0:T(8,128)(2,1)S(1)} %get-tuple-element.38), channel_id=1, source_target_pairs={{0,4},{4,0},{8,12},{12,8},{16,20},{20,16},{24,28},{28,24},{1,5},{5... | collective-permute-start | bytes 294920 | tf_op jit(solution)/shard_map/ppermute | solution.py:618
  22.7 8.8 %collective-permute-start.6 = (bf16[384,128]{1,0:T(8,128)(2,1)S(1)}, bf16[384,128]{1,0:T(8,128)(2,1)S(1)}, u32[]{:S(2)}, u32[]{:S(2)}) collective-permute-start(bf16[384,128]{1,0:T(8,128)(2,1)S(1)} %get-tuple-element.41), channel_id=1, source_target_pairs={{0,8},{4,12},{8,16},{12,20},{16,24},{20,28},{24,0},{28,4},{1,9},{5... | collective-permute-start | bytes 294920 | tf_op jit(solution)/shard_map/ppermute | solution.py:623
  22.8 11.7 %collective-permute-start.10 = (bf16[384,128]{1,0:T(8,128)(2,1)S(1)}, bf16[384,128]{1,0:T(8,128)(2,1)S(1)}, u32[]{:S(2)}, u32[]{:S(2)}) collective-permute-start(bf16[384,128]{1,0:T(8,128)(2,1)S(1)} %get-tuple-element.42), channel_id=1, source_target_pairs={{0,16},{4,20},{8,24},{12,28},{16,0},{20,4},{24,8},{28,12},{1,17},{... | collective-permute-start | bytes 294920 | tf_op jit(solution)/shard_map/ppermute | solution.py:623
  24.4 10.0 %collective-permute-start.11 = (bf16[384,128]{1,0:T(8,128)(2,1)S(1)}, bf16[384,128]{1,0:T(8,128)(2,1)S(1)}, u32[]{:S(2)}, u32[]{:S(2)}) collective-permute-start(bf16[384,128]{1,0:T(8,128)(2,1)S(1)} %get-tuple-element.43), channel_id=1, source_target_pairs={{0,24},{4,28},{8,0},{12,4},{16,8},{20,12},{24,16},{28,20},{1,25},{... | collective-permute-start | bytes 294920 | tf_op jit(solution)/shard_map/ppermute | solution.py:623
  31.7 8.7 %collective-permute-start.9 = (bf16[128,512]{1,0:T(8,128)(2,1)S(1)}, bf16[128,512]{1,0:T(8,128)(2,1)S(1)}, u32[]{:S(2)}, u32[]{:S(2)}) collective-permute-start(bf16[128,512]{1,0:T(8,128)(2,1)S(1)} %unit_negatives.1.refs_0_), channel_id=1, source_target_pairs={{0,3},{1,2},{2,1},{3,0},{4,7},{5,6},{6,5},{7,4},{8,11},{9,10},{10,... | collective-permute-start | bytes 393224 | tf_op jit(solution)/shard_map/ppermute | solution.py:644
  33.9 6.4 %collective-permute-start.8 = (bf16[128,512]{1,0:T(8,128)(2,1)S(1)}, bf16[128,512]{1,0:T(8,128)(2,1)S(1)}, u32[]{:S(2)}, u32[]{:S(2)}) collective-permute-start(bf16[128,512]{1,0:T(8,128)(2,1)S(1)} %unit_negatives.1.refs_0_), channel_id=1, source_target_pairs={{0,2},{1,3},{2,0},{3,1},{4,6},{5,7},{6,4},{7,5},{8,10},{9,11},{10,... | collective-permute-start | bytes 393224 | tf_op jit(solution)/shard_map/ppermute | solution.py:644
  34.2 6.2 %collective-permute-start.7 = (bf16[128,512]{1,0:T(8,128)(2,1)S(1)}, bf16[128,512]{1,0:T(8,128)(2,1)S(1)}, u32[]{:S(2)}, u32[]{:S(2)}) collective-permute-start(bf16[128,512]{1,0:T(8,128)(2,1)S(1)} %unit_negatives.1.refs_0_), channel_id=1, source_target_pairs={{0,1},{1,0},{2,3},{3,2},{4,5},{5,4},{6,7},{7,6},{8,9},{9,8},{10,11... | collective-permute-start | bytes 393224 | tf_op jit(solution)/shard_map/ppermute | solution.py:644
  40.4 5.1 %collective-permute-start.12 = (bf16[512,512]{1,0:T(8,128)(2,1)S(1)}, bf16[512,512]{1,0:T(8,128)(2,1)S(1)}, u32[]{:S(2)}, u32[]{:S(2)}) collective-permute-start(bf16[512,512]{1,0:T(8,128)(2,1)S(1)} %join.1.refs_2_), channel_id=1, source_target_pairs={{0,4},{4,0},{8,12},{12,8},{16,20},{20,16},{24,28},{28,24},{1,5},{5... | collective-permute-start | bytes 1572872 | tf_op jit(solution)/shard_map/ppermute | solution.py:647

commit v7 on v6

--- a/solution.py
+++ b/solution.py
@@ -495,10 +495,10 @@
     return total, jnp.dot(powers.astype(BF), negatives, preferred_element_type=F32)
 
 
-def row_blocks(refs):
+def row_blocks(refs, pages):
     at = 0
     for ref in refs:
-        size = GRADIENT_PAGES * PAGE
+        size = pages * PAGE
         for low in range(0, ref.shape[0], size):
             block = min(size, ref.shape[0] - low)
             yield ref, low, at, block
@@ -519,19 +519,18 @@
     len_ref, own_ref, near_ref = refs[:3]
     unit_refs = refs[3 : 3 + count]
     item_refs = refs[3 + count : 3 + 2 * count]
-    sum_ref, total_ref, positive_ref, all_unit_ref, target_ref, next_ref = refs[3 + 2 * count :]
+    sum_ref, total_ref, positive_ref, target_ref, next_ref = refs[3 + 2 * count :]
     negatives = near_ref[...]
     at = 0
-    for unit, item in zip(unit_refs, item_refs):
+    for item in item_refs:
         size = item.shape[0]
         next_ref[at : at + size, :] = item[...].astype(F32)
-        all_unit_ref[at : at + size, :] = unit[...]
         at += size
     next_ref[at:, :] = jnp.zeros_like(next_ref[at:, :])
     segment, _ = own_plan(len_ref, own_ref)
     segment = segment + [jnp.int32(-1)]
     sharp = 1.0 / SCORE_SHARPNESS
-    for ref, low, at, block in row_blocks(unit_refs):
+    for ref, low, at, block in row_blocks(unit_refs, GRADIENT_PAGES):
         unit = ref[low : low + block, :]
         has_next = next_limits(segment, at // PAGE, block // PAGE)
         targets = jnp.where(has_next, next_ref[at + 1 : at + 1 + block, :], 0.0)
@@ -550,7 +549,6 @@
         jax.ShapeDtypeStruct((rows, width), F32),
         jax.ShapeDtypeStruct((rows, 1), F32),
         jax.ShapeDtypeStruct((rows, 1), F32),
-        jax.ShapeDtypeStruct((rows, width), BF),
         jax.ShapeDtypeStruct((rows, width), BF),
     ]
     return run(
@@ -566,33 +564,45 @@
     )
 
 
-def far_kernel(far_ref, sum_ref, total_ref, positive_ref, unit_ref, target_ref, out_ref):
+def far_kernel(count, *refs):
+    far_ref, sum_ref, total_ref, positive_ref, target_ref = refs[:5]
+    unit_refs = refs[5 : 5 + count]
+    out_ref, stage_ref, sem = refs[5 + count :]
+    negatives = far_ref[...]
     sharp = 1.0 / SCORE_SHARPNESS
-    total, part = score_part(unit_ref[...], far_ref[...])
-    positive = positive_ref[...]
-    inverse = 1.0 / (total + total_ref[...])
-    grad = (part + sum_ref[...]) * inverse
-    grad = (grad + (positive * inverse - 1.0) * target_ref[...].astype(F32)) * sharp
-    out_ref[...] = jnp.where(positive >= 0.0, grad, 0.0)
-
-
-def far_gradient(far, sums, totals, positives, unit, targets):
+    copies = []
+    for ref, low, at, block in row_blocks(unit_refs, FAR_PAGES):
+        part_rows = slice(at, at + block)
+        total, part = score_part(ref[low : low + block, :], negatives)
+        positive = positive_ref[part_rows, :]
+        inverse = 1.0 / (total + total_ref[part_rows, :])
+        grad = (part + sum_ref[part_rows, :]) * inverse
+        targets = target_ref[part_rows, :].astype(F32)
+        grad = (grad + (positive * inverse - 1.0) * targets) * sharp
+        stage_ref[part_rows, :] = jnp.where(positive >= 0.0, grad, 0.0)
+        rows = pl.ds(at, block)
+        copies.append(
+            pltpu.make_async_copy(stage_ref.at[rows, :], out_ref.at[rows, :], sem.at[len(copies)])
+        )
+        copies[-1].start()
+    for copy in copies:
+        copy.wait()
+
+
+def far_gradient(far, sums, totals, positives, targets, units):
     rows, width = sums.shape
-    block = FAR_PAGES * PAGE
-
-    def spec(shape):
-        return pl.BlockSpec((block, shape[1]), lambda i: (i, 0))
-
-    operands = [sums, totals, positives, unit, targets]
     return pl.pallas_call(
-        far_kernel,
-        grid=(rows // block,),
+        functools.partial(far_kernel, len(units)),
         out_shape=jax.ShapeDtypeStruct((rows, width), F32),
-        in_specs=[pl.BlockSpec(far.shape, lambda i: (0, 0))] + [spec(x.shape) for x in operands],
-        out_specs=pl.BlockSpec((block, width), lambda i: (i, 0)),
+        in_specs=[vmem()] * (5 + len(units)),
+        out_specs=hbm(),
+        scratch_shapes=[
+            pltpu.VMEM((rows, width), F32),
+            pltpu.SemaphoreType.DMA((rows // PAGE,)),
+        ],
         compiler_params=params(20),
         name="far_gradient",
-    )(far, *operands)
+    )(far, sums, totals, positives, targets, *units)
 
 
 def on_device(
@@ -638,14 +648,15 @@
         if not last:
             prior = outs[2]
         if c == 0:
-            own = unit_negatives(arrived[0], 2 * neg_half, units + list(arrived[1][1:2]))
+            own = unit_negatives(arrived[0], 2 * neg_half, units)
             parts = [own]
             for s in range(1, users):
                 parts.append(lax.ppermute(own, "user", [(u, u ^ s) for u in range(users)]))
         first += size
     near = join(parts, units[1:])
     far = lax.ppermute(near, "table", cores)
-    return far_gradient(far, *near_gradient(seq_lengths, seq_owner, near, units, items))
+    parts = near_gradient(seq_lengths, seq_owner, near, units, items)
+    return far_gradient(far, *parts, units)
 
 
 def solution(mesh):

time: 48.2 us -> 48.1 us (level)
  transfers between devices with their start and end apart: 13 -> 13, of which waited for: 3 -> 4; matrix products, arithmetic and copies ran while one was open for 0% -> 0% of each run, Pallas kernels for 36% -> 36%
where the time goes in v7:
time: 48.1 us; the launch traced here: 47.9 us
  Pallas kernels  27.7 us (58%)
  starting transfers between devices  17.1 us (36%)
  waiting for transfers between devices  2.74 us (6%)
    pallas_call x9, Pallas kernels, run(): pl.pallas_call(body, out_shape=out_shape, in_specs=in_specs + [anywhere()...  25.4 us
    ppermute x6, starting transfers between devices, on_device(): blocks[s] = lax.ppermute(blocks[s], 'table', moves)  10.1 us
    ppermute x1, starting transfers between devices, on_device(): far = lax.ppermute(near, 'table', cores)  2.86 us
    ppermute x3, starting transfers between devices, on_device(): parts.append(lax.ppermute(own, 'user', [(u, u ^ s) for u in range(users)]))  2.71 us
    ppermute x3, waiting for transfers between devices, on_device(): got = [lax.ppermute(give, 'table', cores) for give in gives]  2.63 us
    pallas_call x1, Pallas kernels, far_gradient(): pl.pallas_call(functools.partial(far_kernel, len(units)), out_shape=jax.S...  2.3 us
    ppermute x3, starting transfers between devices, on_device(): got = [lax.ppermute(give, 'table', cores) for give in gives]  1.48 us
  transfers between devices with their start and end apart: 13, of which 4 were waited for; matrix products, arithmetic and copies ran while one was open for 0% of the time, Pallas kernels for 36%

profile of v7, /device:TPU:1, one launch (start us, length us, event | category | flops | bytes accessed | tf_op | source)
XLA Modules:
  0.0 47.9 jit_solution(5175901423421551474)
XLA Ops:
  0.0 8.1 %gather_rows.2 = (f32[32768,128]{1,0:T(8,128)S(1)}, bf16[832,128]{1,0:T(8,128)(2,1)S(1)}, bf16[832,128]{1,0:T(8,128)(2,1)S(1)}) custom-call(s32[4096]{0:T(1024)} %refs_0_.6, s32[1,16]{1,0:T(1,128)} %refs_0_.9, s32[1,16]{1,0:T(1,128)} %refs_1_.9, s32[256]{0:T(256)} %refs_3_.1, bf16[64,32768]{1,0:T(8,128)(2,1)} %bitcast.1), custom_call_target="tpu_custom_call" | custom-call | tf_op jit(solution)/shard_map/gather_rows/pallas_call | solution.py:42
  8.2 0.1 collective-permute-start
  8.3 1.4 %collective-permute-done.refs_1_ = bf16[832,128]{1,0:T(8,128)(2,1)S(1)} collective-permute-done((bf16[832,128]{1,0:T(8,128)(2,1)S(1)}, bf16[832,128]{1,0:T(8,128)(2,1)S(1)}, u32[]{:S(2)}, u32[]{:S(2)}) %collective-permute-start) | collective-permute-done | bytes 213024 | tf_op jit(solution)/shard_map/ppermute | solution.py:628
  9.7 0.2 merge_columns.2
  9.9 3.5 %collective-permute-start.2 = (bf16[512,128]{1,0:T(8,128)(2,1)S(1)}, bf16[512,128]{1,0:T(8,128)(2,1)S(1)}, u32[]{:S(2)}, u32[]{:S(2)}) collective-permute-start(bf16[512,128]{1,0:T(8,128)(2,1)S(1)} %get-tuple-element.32), channel_id=1, source_target_pairs={{0,16},{4,20},{8,24},{12,28},{16,0},{20,4},{24,8},{28,12},{1,17},{... | collective-permute-start | bytes 393224 | tf_op jit(solution)/shard_map/ppermute | solution.py:633
  13.4 1.3 %collective-permute-start.1 = (bf16[512,128]{1,0:T(8,128)(2,1)S(1)}, bf16[512,128]{1,0:T(8,128)(2,1)S(1)}, u32[]{:S(2)}, u32[]{:S(2)}) collective-permute-start(bf16[512,128]{1,0:T(8,128)(2,1)S(1)} %get-tuple-element.31), channel_id=1, source_target_pairs={{0,8},{4,12},{8,16},{12,20},{16,24},{20,28},{24,0},{28,4},{1,9},{5... | collective-permute-start | bytes 393224 | tf_op jit(solution)/shard_map/ppermute | solution.py:633
  14.7 2.0 %collective-permute-start.3 = (bf16[512,128]{1,0:T(8,128)(2,1)S(1)}, bf16[512,128]{1,0:T(8,128)(2,1)S(1)}, u32[]{:S(2)}, u32[]{:S(2)}) collective-permute-start(bf16[512,128]{1,0:T(8,128)(2,1)S(1)} %get-tuple-element.33), channel_id=1, source_target_pairs={{0,24},{4,28},{8,0},{12,4},{16,8},{20,12},{24,16},{28,20},{1,25},{... | collective-permute-start | bytes 393224 | tf_op jit(solution)/shard_map/ppermute | solution.py:633
  16.6 0.0 copy-start
  16.6 0.0 copy-start.1
  16.6 0.0 copy-start.2
  16.6 0.0 copy-start.3
  16.6 0.0 copy-start.4
  16.7 0.0 copy-start.5
  16.7 3.3 %gather_rows.3 = (bf16[768,128]{1,0:T(8,128)(2,1)S(1)}, bf16[384,128]{1,0:T(8,128)(2,1)S(1)}, bf16[384,128]{1,0:T(8,128)(2,1)S(1)}) custom-call(s32[4096]{0:T(1024)} %refs_0_.6, s32[1,16]{1,0:T(1,128)} %refs_0_.9, s32[1,16]{1,0:T(1,128)} %refs_1_.9, f32[32768,128]{1,0:T(8,128)S(1)} %get-tuple-element.34.refs_3_, ...), custom_call_target="tpu_custom_call" | custom-call | tf_op jit(solution)/shard_map/gather_rows/pallas_call | solution.py:42
  19.9 1.3 %collective-permute-start.4 = (bf16[384,128]{1,0:T(8,128)(2,1)S(1)}, bf16[384,128]{1,0:T(8,128)(2,1)S(1)}, u32[]{:S(2)}, u32[]{:S(2)}) collective-permute-start(bf16[384,128]{1,0:T(8,128)(2,1)S(1)} %get-tuple-element.36), channel_id=1, source_target_pairs={{0,4},{4,0},{8,12},{12,8},{16,20},{20,16},{24,28},{28,24},{1,5},{5... | collective-permute-start | bytes 294920 | tf_op jit(solution)/shard_map/ppermute | solution.py:628
  21.2 0.1 collective-permute-start.5
  21.3 0.9 %collective-permute-done.4.refs_1_ = bf16[384,128]{1,0:T(8,128)(2,1)S(1)} collective-permute-done((bf16[384,128]{1,0:T(8,128)(2,1)S(1)}, bf16[384,128]{1,0:T(8,128)(2,1)S(1)}, u32[]{:S(2)}, u32[]{:S(2)}) %collective-permute-start.4) | collective-permute-done | bytes 98336 | tf_op jit(solution)/shard_map/ppermute | solution.py:628
  22.2 0.4 collective-permute-done.5.refs_2_
  22.5 0.1 collective-permute-done.2.refs_3_.refs_4_.refs_2_
  22.6 0.2 merge_columns.3
  22.8 0.1 collective-permute-start.9
  22.8 1.8 %collective-permute-start.10 = (bf16[384,128]{1,0:T(8,128)(2,1)S(1)}, bf16[384,128]{1,0:T(8,128)(2,1)S(1)}, u32[]{:S(2)}, u32[]{:S(2)}) collective-permute-start(bf16[384,128]{1,0:T(8,128)(2,1)S(1)} %get-tuple-element.41), channel_id=1, source_target_pairs={{0,16},{4,20},{8,24},{12,28},{16,0},{20,4},{24,8},{28,12},{1,17},{... | collective-permute-start | bytes 294920 | tf_op jit(solution)/shard_map/ppermute | solution.py:633
  24.6 1.5 %collective-permute-start.11 = (bf16[384,128]{1,0:T(8,128)(2,1)S(1)}, bf16[384,128]{1,0:T(8,128)(2,1)S(1)}, u32[]{:S(2)}, u32[]{:S(2)}) collective-permute-start(bf16[384,128]{1,0:T(8,128)(2,1)S(1)} %get-tuple-element.42), channel_id=1, source_target_pairs={{0,24},{4,28},{8,0},{12,4},{16,8},{20,12},{24,16},{28,20},{1,25},{... | collective-permute-start | bytes 294920 | tf_op jit(solution)/shard_map/ppermute | solution.py:633
  26.1 0.0 collective-permute-done.1.refs_3_.refs_1_
  26.1 0.0 collective-permute-done.3.refs_5_.refs_3_
  26.1 0.0 copy-done
  26.1 0.0 copy-done.1
  26.1 0.0 copy-done.2
  26.1 0.0 copy-done.3
  26.1 0.0 copy-done.4
  26.1 0.0 copy-done.5
  26.2 5.4 %layer.2 = (bf16[384,512]{1,0:T(8,128)(2,1)S(1)}, bf16[384,512]{1,0:T(8,128)(2,1)S(1)}, bf16[384,1024]{1,0:T(8,128)(2,1)S(1)}) custom-call(s32[1,16]{1,0:T(1,128)S(1)} %copy-done, s32[1,16]{1,0:T(1,128)S(1)} %copy-done.1, bf16[512,128]{1,0:T(8,128)(2,1)S(1)} %get-tuple-element.30.refs_4_.refs_2_.refs_0_, ...), custom_call_target="tpu_custom_call" | custom-call | flops 2415919104 | bytes 8053063 | tf_op jit(solution)/shard_map/layer/pallas_call | solution.py:42
  31.6 0.2 unit_negatives.1.refs_0_
  31.8 2.2 %collective-permute-start.8 = (bf16[128,512]{1,0:T(8,128)(2,1)S(1)}, bf16[128,512]{1,0:T(8,128)(2,1)S(1)}, u32[]{:S(2)}, u32[]{:S(2)}) collective-permute-start(bf16[128,512]{1,0:T(8,128)(2,1)S(1)} %unit_negatives.1.refs_0_), channel_id=1, source_target_pairs={{0,3},{1,2},{2,1},{3,0},{4,7},{5,6},{6,5},{7,4},{8,11},{9,10},{10,... | collective-permute-start | bytes 393224 | tf_op jit(solution)/shard_map/ppermute | solution.py:654
  33.9 0.2 collective-permute-start.7
  34.2 0.0 collective-permute-done.9.refs_3_
  34.2 0.3 collective-permute-start.6
  34.5 0.0 collective-permute-done.10.refs_4_
  34.5 0.0 collective-permute-done.11.refs_5_
  34.5 5.9 %layer.3 = (bf16[384,512]{1,0:T(8,128)(2,1)S(1)}, bf16[384,512]{1,0:T(8,128)(2,1)S(1)}) custom-call(s32[1,16]{1,0:T(1,128)S(1)} %copy-done, s32[1,16]{1,0:T(1,128)S(1)} %copy-done.1, bf16[384,128]{1,0:T(8,128)(2,1)S(1)} %get-tuple-element.38.refs_10_.refs_2_, bf16[384,128]{1,0:T(8,128)(2,1)S(1)} %collective-permute-done.9.refs_3_, ...), custom_call_target="tpu_custom_call" | custom-call | flops 2415919104 | bytes 8053063 | tf_op jit(solution)/shard_map/layer/pallas_call | solution.py:42
  40.4 0.0 collective-permute-done.8.refs_3_
  40.4 0.0 collective-permute-done.7.refs_2_
  40.4 0.0 collective-permute-done.6.refs_1_
  40.5 2.9 %collective-permute-start.12 = (bf16[512,512]{1,0:T(8,128)(2,1)S(1)}, bf16[512,512]{1,0:T(8,128)(2,1)S(1)}, u32[]{:S(2)}, u32[]{:S(2)}) collective-permute-start(bf16[512,512]{1,0:T(8,128)(2,1)S(1)} %join.1.refs_2_), channel_id=1, source_target_pairs={{0,4},{4,0},{8,12},{12,8},{16,20},{20,16},{24,28},{28,24},{1,5},{5... | collective-permute-start | bytes 1572872 | tf_op jit(solution)/shard_map/ppermute | solution.py:657
  43.4 2.1 %near_gradient.1 = (f32[768,512]{1,0:T(8,128)S(1)}, f32[768,1]{1,0:T(8,128)S(1)}, f32[768,1]{1,0:T(8,128)S(1)}, bf16[768,512]{1,0:T(8,128)(2,1)S(1)}) custom-call(s32[1,16]{1,0:T(1,128)S(1)} %copy-done, s32[1,16]{1,0:T(1,128)S(1)} %copy-done.1, bf16[512,512]{1,0:T(8,128)(2,1)S(1)} %join.1.refs_2_, ...), custom_call_target="tpu_custom_call" | custom-call | flops 1207959552 | bytes 4026531 | tf_op jit(solution)/shard_map/near_gradient/pallas_call | solution.py:42
  45.4 0.0 collective-permute-done.12.refs_0_
  45.4 2.3 %far_gradient.1 = f32[768,512]{1,0:T(8,128)} custom-call(bf16[512,512]{1,0:T(8,128)(2,1)S(1)} %collective-permute-done.12.refs_0_, f32[768,512]{1,0:T(8,128)S(1)} %get-tuple-element.47.refs_1_, f32[768,1]{1,0:T(8,128)S(1)} %get-tuple-element.48.refs_2_, f32[768,1]{1,0:T(8,128)S(1)} %get-tuple-element.49.refs_3_, ...), custom_call_target="tpu_custom_call" | custom-call | tf_op jit(solution)/shard_map/far_gradient/pallas_call | solution.py:594
  (1 shorter events, 0.0 us)
Async XLA Ops:
  8.2 1.5 %collective-permute-start = (bf16[832,128]{1,0:T(8,128)(2,1)S(1)}, bf16[832,128]{1,0:T(8,128)(2,1)S(1)}, u32[]{:S(2)}, u32[]{:S(2)}) collective-permute-start(bf16[832,128]{1,0:T(8,128)(2,1)S(1)} %get-tuple-element.29), channel_id=1, source_target_pairs={{0,4},{4,0},{8,12},{12,8},{16,20},{20,16},{24,28},{28,24},{1,5},{5... | collective-permute-start | bytes 638984 | tf_op jit(solution)/shard_map/ppermute | solution.py:628
  9.9 12.7 %collective-permute-start.2 = (bf16[512,128]{1,0:T(8,128)(2,1)S(1)}, bf16[512,128]{1,0:T(8,128)(2,1)S(1)}, u32[]{:S(2)}, u32[]{:S(2)}) collective-permute-start(bf16[512,128]{1,0:T(8,128)(2,1)S(1)} %get-tuple-element.32), channel_id=1, source_target_pairs={{0,16},{4,20},{8,24},{12,28},{16,0},{20,4},{24,8},{28,12},{1,17},{... | collective-permute-start | bytes 393224 | tf_op jit(solution)/shard_map/ppermute | solution.py:633
  13.4 12.7 %collective-permute-start.1 = (bf16[512,128]{1,0:T(8,128)(2,1)S(1)}, bf16[512,128]{1,0:T(8,128)(2,1)S(1)}, u32[]{:S(2)}, u32[]{:S(2)}) collective-permute-start(bf16[512,128]{1,0:T(8,128)(2,1)S(1)} %get-tuple-element.31), channel_id=1, source_target_pairs={{0,8},{4,12},{8,16},{12,20},{16,24},{20,28},{24,0},{28,4},{1,9},{5... | collective-permute-start | bytes 393224 | tf_op jit(solution)/shard_map/ppermute | solution.py:633
  14.7 11.4 %collective-permute-start.3 = (bf16[512,128]{1,0:T(8,128)(2,1)S(1)}, bf16[512,128]{1,0:T(8,128)(2,1)S(1)}, u32[]{:S(2)}, u32[]{:S(2)}) collective-permute-start(bf16[512,128]{1,0:T(8,128)(2,1)S(1)} %get-tuple-element.33), channel_id=1, source_target_pairs={{0,24},{4,28},{8,0},{12,4},{16,8},{20,12},{24,16},{28,20},{1,25},{... | collective-permute-start | bytes 393224 | tf_op jit(solution)/shard_map/ppermute | solution.py:633
  16.6 9.5 %copy-start = (s32[1,16]{1,0:T(1,128)S(1)}, s32[1,16]{1,0:T(1,128)}, u32[]{:S(2)}) copy-start(s32[1,16]{1,0:T(1,128)} %refs_0_.9) | copy-start | bytes 196
  16.6 9.5 %copy-start.1 = (s32[1,16]{1,0:T(1,128)S(1)}, s32[1,16]{1,0:T(1,128)}, u32[]{:S(2)}) copy-start(s32[1,16]{1,0:T(1,128)} %refs_1_.9) | copy-start | bytes 196
  16.6 9.5 %copy-start.2 = (bf16[512,2048]{1,0:T(8,128)(2,1)S(1)}, bf16[512,2048]{1,0:T(8,128)(2,1)}, u32[]{:S(2)}) copy-start(bf16[512,2048]{1,0:T(8,128)(2,1)} %refs_6_.3) | copy-start | bytes 6291460
  16.6 9.5 %copy-start.3 = (bf16[2048,512]{1,0:T(8,128)(2,1)S(1)}, bf16[2048,512]{1,0:T(8,128)(2,1)}, u32[]{:S(2)}) copy-start(bf16[2048,512]{1,0:T(8,128)(2,1)} %refs_7_.3) | copy-start | bytes 6291460
  16.6 9.5 %copy-start.4 = (bf16[512,2048]{1,0:T(8,128)(2,1)S(1)}, bf16[512,2048]{1,0:T(8,128)(2,1)}, u32[]{:S(2)}) copy-start(bf16[512,2048]{1,0:T(8,128)(2,1)} %refs_8_.3) | copy-start | bytes 6291460
  16.7 9.5 %copy-start.5 = (bf16[512,512]{1,0:T(8,128)(2,1)S(1)}, bf16[512,512]{1,0:T(8,128)(2,1)}, u32[]{:S(2)}) copy-start(bf16[512,512]{1,0:T(8,128)(2,1)} %refs_9_.3) | copy-start | bytes 1572868
  19.9 2.2 %collective-permute-start.4 = (bf16[384,128]{1,0:T(8,128)(2,1)S(1)}, bf16[384,128]{1,0:T(8,128)(2,1)S(1)}, u32[]{:S(2)}, u32[]{:S(2)}) collective-permute-start(bf16[384,128]{1,0:T(8,128)(2,1)S(1)} %get-tuple-element.36), channel_id=1, source_target_pairs={{0,4},{4,0},{8,12},{12,8},{16,20},{20,16},{24,28},{28,24},{1,5},{5... | collective-permute-start | bytes 294920 | tf_op jit(solution)/shard_map/ppermute | solution.py:628
  21.2 1.3 %collective-permute-start.5 = (bf16[384,128]{1,0:T(8,128)(2,1)S(1)}, bf16[384,128]{1,0:T(8,128)(2,1)S(1)}, u32[]{:S(2)}, u32[]{:S(2)}) collective-permute-start(bf16[384,128]{1,0:T(8,128)(2,1)S(1)} %get-tuple-element.37), channel_id=1, source_target_pairs={{0,4},{4,0},{8,12},{12,8},{16,20},{20,16},{24,28},{28,24},{1,5},{5... | collective-permute-start | bytes 294920 | tf_op jit(solution)/shard_map/ppermute | solution.py:628
  22.8 11.4 %collective-permute-start.9 = (bf16[384,128]{1,0:T(8,128)(2,1)S(1)}, bf16[384,128]{1,0:T(8,128)(2,1)S(1)}, u32[]{:S(2)}, u32[]{:S(2)}) collective-permute-start(bf16[384,128]{1,0:T(8,128)(2,1)S(1)} %get-tuple-element.40), channel_id=1, source_target_pairs={{0,8},{4,12},{8,16},{12,20},{16,24},{20,28},{24,0},{28,4},{1,9},{5... | collective-permute-start | bytes 294920 | tf_op jit(solution)/shard_map/ppermute | solution.py:633
  22.8 11.7 %collective-permute-start.10 = (bf16[384,128]{1,0:T(8,128)(2,1)S(1)}, bf16[384,128]{1,0:T(8,128)(2,1)S(1)}, u32[]{:S(2)}, u32[]{:S(2)}) collective-permute-start(bf16[384,128]{1,0:T(8,128)(2,1)S(1)} %get-tuple-element.41), channel_id=1, source_target_pairs={{0,16},{4,20},{8,24},{12,28},{16,0},{20,4},{24,8},{28,12},{1,17},{... | collective-permute-start | bytes 294920 | tf_op jit(solution)/shard_map/ppermute | solution.py:633
  24.6 9.9 %collective-permute-start.11 = (bf16[384,128]{1,0:T(8,128)(2,1)S(1)}, bf16[384,128]{1,0:T(8,128)(2,1)S(1)}, u32[]{:S(2)}, u32[]{:S(2)}) collective-permute-start(bf16[384,128]{1,0:T(8,128)(2,1)S(1)} %get-tuple-element.42), channel_id=1, source_target_pairs={{0,24},{4,28},{8,0},{12,4},{16,8},{20,12},{24,16},{28,20},{1,25},{... | collective-permute-start | bytes 294920 | tf_op jit(solution)/shard_map/ppermute | solution.py:633
  31.8 8.7 %collective-permute-start.8 = (bf16[128,512]{1,0:T(8,128)(2,1)S(1)}, bf16[128,512]{1,0:T(8,128)(2,1)S(1)}, u32[]{:S(2)}, u32[]{:S(2)}) collective-permute-start(bf16[128,512]{1,0:T(8,128)(2,1)S(1)} %unit_negatives.1.refs_0_), channel_id=1, source_target_pairs={{0,3},{1,2},{2,1},{3,0},{4,7},{5,6},{6,5},{7,4},{8,11},{9,10},{10,... | collective-permute-start | bytes 393224 | tf_op jit(solution)/shard_map/ppermute | solution.py:654
  33.9 6.5 %collective-permute-start.7 = (bf16[128,512]{1,0:T(8,128)(2,1)S(1)}, bf16[128,512]{1,0:T(8,128)(2,1)S(1)}, u32[]{:S(2)}, u32[]{:S(2)}) collective-permute-start(bf16[128,512]{1,0:T(8,128)(2,1)S(1)} %unit_negatives.1.refs_0_), channel_id=1, source_target_pairs={{0,2},{1,3},{2,0},{3,1},{4,6},{5,7},{6,4},{7,5},{8,10},{9,11},{10,... | collective-permute-start | bytes 393224 | tf_op jit(solution)/shard_map/ppermute | solution.py:654
  34.2 6.3 %collective-permute-start.6 = (bf16[128,512]{1,0:T(8,128)(2,1)S(1)}, bf16[128,512]{1,0:T(8,128)(2,1)S(1)}, u32[]{:S(2)}, u32[]{:S(2)}) collective-permute-start(bf16[128,512]{1,0:T(8,128)(2,1)S(1)} %unit_negatives.1.refs_0_), channel_id=1, source_target_pairs={{0,1},{1,0},{2,3},{3,2},{4,5},{5,4},{6,7},{7,6},{8,9},{9,8},{10,11... | collective-permute-start | bytes 393224 | tf_op jit(solution)/shard_map/ppermute | solution.py:654
  40.5 4.9 %collective-permute-start.12 = (bf16[512,512]{1,0:T(8,128)(2,1)S(1)}, bf16[512,512]{1,0:T(8,128)(2,1)S(1)}, u32[]{:S(2)}, u32[]{:S(2)}) collective-permute-start(bf16[512,512]{1,0:T(8,128)(2,1)S(1)} %join.1.refs_2_), channel_id=1, source_target_pairs={{0,4},{4,0},{8,12},{12,8},{16,20},{20,16},{24,28},{28,24},{1,5},{5... | collective-permute-start | bytes 1572872 | tf_op jit(solution)/shard_map/ppermute | solution.py:657

commit v8 on v7

--- a/solution.py
+++ b/solution.py
@@ -21,7 +21,7 @@
 
 BF = jnp.bfloat16
 F32 = jnp.float32
-COPY_PARTS = 8
+COPY_PARTS = 4
 GRADIENT_PAGES = 3
 LAYER_COST = 24
 FAR_PAGES = 3
@@ -127,7 +127,7 @@
             )
             return carry
 
-        lax.fori_loop(0, piece // LANES, turn, 0, unroll=16)
+        lax.fori_loop(0, piece // LANES, turn, 0, unroll=32)
 
 
 def gather_kernel(tables, start, size, negatives, *refs):

time: 48.1 us -> 48 us (level)
  no operation moved by 1% of the time
where the time goes in v8:
time: 48 us; the launch traced here: 47.9 us
  Pallas kernels  27.5 us (57%)
  starting transfers between devices  17.2 us (36%)
  waiting for transfers between devices  2.74 us (6%)
    pallas_call x9, Pallas kernels, run(): pl.pallas_call(body, out_shape=out_shape, in_specs=in_specs + [anywhere()...  25.2 us
    ppermute x6, starting transfers between devices, on_device(): blocks[s] = lax.ppermute(blocks[s], 'table', moves)  10.1 us
    ppermute x1, starting transfers between devices, on_device(): far = lax.ppermute(near, 'table', cores)  2.97 us
    ppermute x3, starting transfers between devices, on_device(): parts.append(lax.ppermute(own, 'user', [(u, u ^ s) for u in range(users)]))  2.71 us
    ppermute x3, waiting for transfers between devices, on_device(): got = [lax.ppermute(give, 'table', cores) for give in gives]  2.63 us
    pallas_call x1, Pallas kernels, far_gradient(): pl.pallas_call(functools.partial(far_kernel, len(units)), out_shape=jax.S...  2.29 us
    ppermute x3, starting transfers between devices, on_device(): got = [lax.ppermute(give, 'table', cores) for give in gives]  1.48 us
  transfers between devices with their start and end apart: 13, of which 4 were waited for; matrix products, arithmetic and copies ran while one was open for 0% of the time, Pallas kernels for 36%

profile of v8, /device:TPU:1, one launch (start us, length us, event | category | flops | bytes accessed | tf_op | source)
XLA Modules:
  0.0 47.9 jit_solution(10328440000663302617)
XLA Ops:
  0.0 8.0 %gather_rows.2 = (f32[32768,128]{1,0:T(8,128)S(1)}, bf16[832,128]{1,0:T(8,128)(2,1)S(1)}, bf16[832,128]{1,0:T(8,128)(2,1)S(1)}) custom-call(s32[4096]{0:T(1024)} %refs_0_.6, s32[1,16]{1,0:T(1,128)} %refs_0_.9, s32[1,16]{1,0:T(1,128)} %refs_1_.9, s32[256]{0:T(256)} %refs_3_.1, bf16[64,32768]{1,0:T(8,128)(2,1)} %bitcast.1), custom_call_target="tpu_custom_call" | custom-call | tf_op jit(solution)/shard_map/gather_rows/pallas_call | solution.py:42
  8.0 0.1 collective-permute-start
  8.1 1.4 %collective-permute-done.refs_1_ = bf16[832,128]{1,0:T(8,128)(2,1)S(1)} collective-permute-done((bf16[832,128]{1,0:T(8,128)(2,1)S(1)}, bf16[832,128]{1,0:T(8,128)(2,1)S(1)}, u32[]{:S(2)}, u32[]{:S(2)}) %collective-permute-start) | collective-permute-done | bytes 213024 | tf_op jit(solution)/shard_map/ppermute | solution.py:628
  9.5 0.2 merge_columns.2
  9.7 3.5 %collective-permute-start.2 = (bf16[512,128]{1,0:T(8,128)(2,1)S(1)}, bf16[512,128]{1,0:T(8,128)(2,1)S(1)}, u32[]{:S(2)}, u32[]{:S(2)}) collective-permute-start(bf16[512,128]{1,0:T(8,128)(2,1)S(1)} %get-tuple-element.32), channel_id=1, source_target_pairs={{0,16},{4,20},{8,24},{12,28},{16,0},{20,4},{24,8},{28,12},{1,17},{... | collective-permute-start | bytes 393224 | tf_op jit(solution)/shard_map/ppermute | solution.py:633
  13.2 1.3 %collective-permute-start.1 = (bf16[512,128]{1,0:T(8,128)(2,1)S(1)}, bf16[512,128]{1,0:T(8,128)(2,1)S(1)}, u32[]{:S(2)}, u32[]{:S(2)}) collective-permute-start(bf16[512,128]{1,0:T(8,128)(2,1)S(1)} %get-tuple-element.31), channel_id=1, source_target_pairs={{0,8},{4,12},{8,16},{12,20},{16,24},{20,28},{24,0},{28,4},{1,9},{5... | collective-permute-start | bytes 393224 | tf_op jit(solution)/shard_map/ppermute | solution.py:633
  14.5 2.0 %collective-permute-start.3 = (bf16[512,128]{1,0:T(8,128)(2,1)S(1)}, bf16[512,128]{1,0:T(8,128)(2,1)S(1)}, u32[]{:S(2)}, u32[]{:S(2)}) collective-permute-start(bf16[512,128]{1,0:T(8,128)(2,1)S(1)} %get-tuple-element.33), channel_id=1, source_target_pairs={{0,24},{4,28},{8,0},{12,4},{16,8},{20,12},{24,16},{28,20},{1,25},{... | collective-permute-start | bytes 393224 | tf_op jit(solution)/shard_map/ppermute | solution.py:633
  16.5 0.0 copy-start
  16.5 0.0 copy-start.1
  16.5 0.0 copy-start.2
  16.5 0.0 copy-start.3
  16.5 0.0 copy-start.4
  16.5 0.0 copy-start.5
  16.5 3.3 %gather_rows.3 = (bf16[768,128]{1,0:T(8,128)(2,1)S(1)}, bf16[384,128]{1,0:T(8,128)(2,1)S(1)}, bf16[384,128]{1,0:T(8,128)(2,1)S(1)}) custom-call(s32[4096]{0:T(1024)} %refs_0_.6, s32[1,16]{1,0:T(1,128)} %refs_0_.9, s32[1,16]{1,0:T(1,128)} %refs_1_.9, f32[32768,128]{1,0:T(8,128)S(1)} %get-tuple-element.34.refs_3_, ...), custom_call_target="tpu_custom_call" | custom-call | tf_op jit(solution)/shard_map/gather_rows/pallas_call | solution.py:42
  19.8 1.3 %collective-permute-start.4 = (bf16[384,128]{1,0:T(8,128)(2,1)S(1)}, bf16[384,128]{1,0:T(8,128)(2,1)S(1)}, u32[]{:S(2)}, u32[]{:S(2)}) collective-permute-start(bf16[384,128]{1,0:T(8,128)(2,1)S(1)} %get-tuple-element.36), channel_id=1, source_target_pairs={{0,4},{4,0},{8,12},{12,8},{16,20},{20,16},{24,28},{28,24},{1,5},{5... | collective-permute-start | bytes 294920 | tf_op jit(solution)/shard_map/ppermute | solution.py:628
  21.1 0.1 collective-permute-start.5
  21.1 0.9 %collective-permute-done.4.refs_1_ = bf16[384,128]{1,0:T(8,128)(2,1)S(1)} collective-permute-done((bf16[384,128]{1,0:T(8,128)(2,1)S(1)}, bf16[384,128]{1,0:T(8,128)(2,1)S(1)}, u32[]{:S(2)}, u32[]{:S(2)}) %collective-permute-start.4) | collective-permute-done | bytes 98336 | tf_op jit(solution)/shard_map/ppermute | solution.py:628
  22.0 0.4 collective-permute-done.5.refs_2_
  22.4 0.1 collective-permute-done.2.refs_3_.refs_4_.refs_2_
  22.5 0.2 merge_columns.3
  22.6 0.1 collective-permute-start.9
  22.7 1.8 %collective-permute-start.10 = (bf16[384,128]{1,0:T(8,128)(2,1)S(1)}, bf16[384,128]{1,0:T(8,128)(2,1)S(1)}, u32[]{:S(2)}, u32[]{:S(2)}) collective-permute-start(bf16[384,128]{1,0:T(8,128)(2,1)S(1)} %get-tuple-element.41), channel_id=1, source_target_pairs={{0,16},{4,20},{8,24},{12,28},{16,0},{20,4},{24,8},{28,12},{1,17},{... | collective-permute-start | bytes 294920 | tf_op jit(solution)/shard_map/ppermute | solution.py:633
  24.4 1.5 %collective-permute-start.11 = (bf16[384,128]{1,0:T(8,128)(2,1)S(1)}, bf16[384,128]{1,0:T(8,128)(2,1)S(1)}, u32[]{:S(2)}, u32[]{:S(2)}) collective-permute-start(bf16[384,128]{1,0:T(8,128)(2,1)S(1)} %get-tuple-element.42), channel_id=1, source_target_pairs={{0,24},{4,28},{8,0},{12,4},{16,8},{20,12},{24,16},{28,20},{1,25},{... | collective-permute-start | bytes 294920 | tf_op jit(solution)/shard_map/ppermute | solution.py:633
  25.9 0.0 collective-permute-done.1.refs_3_.refs_1_
  25.9 0.0 collective-permute-done.3.refs_5_.refs_3_
  26.0 0.0 copy-done
  26.0 0.0 copy-done.1
  26.0 0.0 copy-done.2
  26.0 0.0 copy-done.3
  26.0 0.0 copy-done.4
  26.0 0.0 copy-done.5
  26.0 5.4 %layer.2 = (bf16[384,512]{1,0:T(8,128)(2,1)S(1)}, bf16[384,512]{1,0:T(8,128)(2,1)S(1)}, bf16[384,1024]{1,0:T(8,128)(2,1)S(1)}) custom-call(s32[1,16]{1,0:T(1,128)S(1)} %copy-done, s32[1,16]{1,0:T(1,128)S(1)} %copy-done.1, bf16[512,128]{1,0:T(8,128)(2,1)S(1)} %get-tuple-element.30.refs_4_.refs_2_.refs_0_, ...), custom_call_target="tpu_custom_call" | custom-call | flops 2415919104 | bytes 8053063 | tf_op jit(solution)/shard_map/layer/pallas_call | solution.py:42
  31.5 0.2 unit_negatives.1.refs_0_
  31.6 2.2 %collective-permute-start.8 = (bf16[128,512]{1,0:T(8,128)(2,1)S(1)}, bf16[128,512]{1,0:T(8,128)(2,1)S(1)}, u32[]{:S(2)}, u32[]{:S(2)}) collective-permute-start(bf16[128,512]{1,0:T(8,128)(2,1)S(1)} %unit_negatives.1.refs_0_), channel_id=1, source_target_pairs={{0,3},{1,2},{2,1},{3,0},{4,7},{5,6},{6,5},{7,4},{8,11},{9,10},{10,... | collective-permute-start | bytes 393224 | tf_op jit(solution)/shard_map/ppermute | solution.py:654
  33.8 0.2 collective-permute-start.7
  34.0 0.0 collective-permute-done.9.refs_3_
  34.0 0.3 collective-permute-start.6
  34.3 0.0 collective-permute-done.10.refs_4_
  34.3 0.0 collective-permute-done.11.refs_5_
  34.3 5.9 %layer.3 = (bf16[384,512]{1,0:T(8,128)(2,1)S(1)}, bf16[384,512]{1,0:T(8,128)(2,1)S(1)}) custom-call(s32[1,16]{1,0:T(1,128)S(1)} %copy-done, s32[1,16]{1,0:T(1,128)S(1)} %copy-done.1, bf16[384,128]{1,0:T(8,128)(2,1)S(1)} %get-tuple-element.38.refs_10_.refs_2_, bf16[384,128]{1,0:T(8,128)(2,1)S(1)} %collective-permute-done.9.refs_3_, ...), custom_call_target="tpu_custom_call" | custom-call | flops 2415919104 | bytes 8053063 | tf_op jit(solution)/shard_map/layer/pallas_call | solution.py:42
  40.3 0.0 collective-permute-done.8.refs_3_
  40.3 0.0 collective-permute-done.7.refs_2_
  40.3 0.0 collective-permute-done.6.refs_1_
  40.3 3.0 %collective-permute-start.12 = (bf16[512,512]{1,0:T(8,128)(2,1)S(1)}, bf16[512,512]{1,0:T(8,128)(2,1)S(1)}, u32[]{:S(2)}, u32[]{:S(2)}) collective-permute-start(bf16[512,512]{1,0:T(8,128)(2,1)S(1)} %join.1.refs_2_), channel_id=1, source_target_pairs={{0,4},{4,0},{8,12},{12,8},{16,20},{20,16},{24,28},{28,24},{1,5},{5... | collective-permute-start | bytes 1572872 | tf_op jit(solution)/shard_map/ppermute | solution.py:657
  43.3 2.1 %near_gradient.1 = (f32[768,512]{1,0:T(8,128)S(1)}, f32[768,1]{1,0:T(8,128)S(1)}, f32[768,1]{1,0:T(8,128)S(1)}, bf16[768,512]{1,0:T(8,128)(2,1)S(1)}) custom-call(s32[1,16]{1,0:T(1,128)S(1)} %copy-done, s32[1,16]{1,0:T(1,128)S(1)} %copy-done.1, bf16[512,512]{1,0:T(8,128)(2,1)S(1)} %join.1.refs_2_, ...), custom_call_target="tpu_custom_call" | custom-call | flops 1207959552 | bytes 4026531 | tf_op jit(solution)/shard_map/near_gradient/pallas_call | solution.py:42
  45.4 0.0 collective-permute-done.12.refs_0_
  45.4 2.3 %far_gradient.1 = f32[768,512]{1,0:T(8,128)} custom-call(bf16[512,512]{1,0:T(8,128)(2,1)S(1)} %collective-permute-done.12.refs_0_, f32[768,512]{1,0:T(8,128)S(1)} %get-tuple-element.47.refs_1_, f32[768,1]{1,0:T(8,128)S(1)} %get-tuple-element.48.refs_2_, f32[768,1]{1,0:T(8,128)S(1)} %get-tuple-element.49.refs_3_, ...), custom_call_target="tpu_custom_call" | custom-call | tf_op jit(solution)/shard_map/far_gradient/pallas_call | solution.py:594
  (1 shorter events, 0.0 us)
Async XLA Ops:
  8.0 1.5 %collective-permute-start = (bf16[832,128]{1,0:T(8,128)(2,1)S(1)}, bf16[832,128]{1,0:T(8,128)(2,1)S(1)}, u32[]{:S(2)}, u32[]{:S(2)}) collective-permute-start(bf16[832,128]{1,0:T(8,128)(2,1)S(1)} %get-tuple-element.29), channel_id=1, source_target_pairs={{0,4},{4,0},{8,12},{12,8},{16,20},{20,16},{24,28},{28,24},{1,5},{5... | collective-permute-start | bytes 638984 | tf_op jit(solution)/shard_map/ppermute | solution.py:628
  9.7 12.7 %collective-permute-start.2 = (bf16[512,128]{1,0:T(8,128)(2,1)S(1)}, bf16[512,128]{1,0:T(8,128)(2,1)S(1)}, u32[]{:S(2)}, u32[]{:S(2)}) collective-permute-start(bf16[512,128]{1,0:T(8,128)(2,1)S(1)} %get-tuple-element.32), channel_id=1, source_target_pairs={{0,16},{4,20},{8,24},{12,28},{16,0},{20,4},{24,8},{28,12},{1,17},{... | collective-permute-start | bytes 393224 | tf_op jit(solution)/shard_map/ppermute | solution.py:633
  13.2 12.7 %collective-permute-start.1 = (bf16[512,128]{1,0:T(8,128)(2,1)S(1)}, bf16[512,128]{1,0:T(8,128)(2,1)S(1)}, u32[]{:S(2)}, u32[]{:S(2)}) collective-permute-start(bf16[512,128]{1,0:T(8,128)(2,1)S(1)} %get-tuple-element.31), channel_id=1, source_target_pairs={{0,8},{4,12},{8,16},{12,20},{16,24},{20,28},{24,0},{28,4},{1,9},{5... | collective-permute-start | bytes 393224 | tf_op jit(solution)/shard_map/ppermute | solution.py:633
  14.5 11.4 %collective-permute-start.3 = (bf16[512,128]{1,0:T(8,128)(2,1)S(1)}, bf16[512,128]{1,0:T(8,128)(2,1)S(1)}, u32[]{:S(2)}, u32[]{:S(2)}) collective-permute-start(bf16[512,128]{1,0:T(8,128)(2,1)S(1)} %get-tuple-element.33), channel_id=1, source_target_pairs={{0,24},{4,28},{8,0},{12,4},{16,8},{20,12},{24,16},{28,20},{1,25},{... | collective-permute-start | bytes 393224 | tf_op jit(solution)/shard_map/ppermute | solution.py:633
  16.5 9.5 %copy-start = (s32[1,16]{1,0:T(1,128)S(1)}, s32[1,16]{1,0:T(1,128)}, u32[]{:S(2)}) copy-start(s32[1,16]{1,0:T(1,128)} %refs_0_.9) | copy-start | bytes 196
  16.5 9.5 %copy-start.1 = (s32[1,16]{1,0:T(1,128)S(1)}, s32[1,16]{1,0:T(1,128)}, u32[]{:S(2)}) copy-start(s32[1,16]{1,0:T(1,128)} %refs_1_.9) | copy-start | bytes 196
  16.5 9.5 %copy-start.2 = (bf16[512,2048]{1,0:T(8,128)(2,1)S(1)}, bf16[512,2048]{1,0:T(8,128)(2,1)}, u32[]{:S(2)}) copy-start(bf16[512,2048]{1,0:T(8,128)(2,1)} %refs_6_.3) | copy-start | bytes 6291460
  16.5 9.5 %copy-start.3 = (bf16[2048,512]{1,0:T(8,128)(2,1)S(1)}, bf16[2048,512]{1,0:T(8,128)(2,1)}, u32[]{:S(2)}) copy-start(bf16[2048,512]{1,0:T(8,128)(2,1)} %refs_7_.3) | copy-start | bytes 6291460
  16.5 9.5 %copy-start.4 = (bf16[512,2048]{1,0:T(8,128)(2,1)S(1)}, bf16[512,2048]{1,0:T(8,128)(2,1)}, u32[]{:S(2)}) copy-start(bf16[512,2048]{1,0:T(8,128)(2,1)} %refs_8_.3) | copy-start | bytes 6291460
  16.5 9.5 %copy-start.5 = (bf16[512,512]{1,0:T(8,128)(2,1)S(1)}, bf16[512,512]{1,0:T(8,128)(2,1)}, u32[]{:S(2)}) copy-start(bf16[512,512]{1,0:T(8,128)(2,1)} %refs_9_.3) | copy-start | bytes 1572868
  19.8 2.2 %collective-permute-start.4 = (bf16[384,128]{1,0:T(8,128)(2,1)S(1)}, bf16[384,128]{1,0:T(8,128)(2,1)S(1)}, u32[]{:S(2)}, u32[]{:S(2)}) collective-permute-start(bf16[384,128]{1,0:T(8,128)(2,1)S(1)} %get-tuple-element.36), channel_id=1, source_target_pairs={{0,4},{4,0},{8,12},{12,8},{16,20},{20,16},{24,28},{28,24},{1,5},{5... | collective-permute-start | bytes 294920 | tf_op jit(solution)/shard_map/ppermute | solution.py:628
  21.1 1.3 %collective-permute-start.5 = (bf16[384,128]{1,0:T(8,128)(2,1)S(1)}, bf16[384,128]{1,0:T(8,128)(2,1)S(1)}, u32[]{:S(2)}, u32[]{:S(2)}) collective-permute-start(bf16[384,128]{1,0:T(8,128)(2,1)S(1)} %get-tuple-element.37), channel_id=1, source_target_pairs={{0,4},{4,0},{8,12},{12,8},{16,20},{20,16},{24,28},{28,24},{1,5},{5... | collective-permute-start | bytes 294920 | tf_op jit(solution)/shard_map/ppermute | solution.py:628
  22.6 11.4 %collective-permute-start.9 = (bf16[384,128]{1,0:T(8,128)(2,1)S(1)}, bf16[384,128]{1,0:T(8,128)(2,1)S(1)}, u32[]{:S(2)}, u32[]{:S(2)}) collective-permute-start(bf16[384,128]{1,0:T(8,128)(2,1)S(1)} %get-tuple-element.40), channel_id=1, source_target_pairs={{0,8},{4,12},{8,16},{12,20},{16,24},{20,28},{24,0},{28,4},{1,9},{5... | collective-permute-start | bytes 294920 | tf_op jit(solution)/shard_map/ppermute | solution.py:633
  22.7 11.6 %collective-permute-start.10 = (bf16[384,128]{1,0:T(8,128)(2,1)S(1)}, bf16[384,128]{1,0:T(8,128)(2,1)S(1)}, u32[]{:S(2)}, u32[]{:S(2)}) collective-permute-start(bf16[384,128]{1,0:T(8,128)(2,1)S(1)} %get-tuple-element.41), channel_id=1, source_target_pairs={{0,16},{4,20},{8,24},{12,28},{16,0},{20,4},{24,8},{28,12},{1,17},{... | collective-permute-start | bytes 294920 | tf_op jit(solution)/shard_map/ppermute | solution.py:633
  24.4 9.9 %collective-permute-start.11 = (bf16[384,128]{1,0:T(8,128)(2,1)S(1)}, bf16[384,128]{1,0:T(8,128)(2,1)S(1)}, u32[]{:S(2)}, u32[]{:S(2)}) collective-permute-start(bf16[384,128]{1,0:T(8,128)(2,1)S(1)} %get-tuple-element.42), channel_id=1, source_target_pairs={{0,24},{4,28},{8,0},{12,4},{16,8},{20,12},{24,16},{28,20},{1,25},{... | collective-permute-start | bytes 294920 | tf_op jit(solution)/shard_map/ppermute | solution.py:633
  31.6 8.6 %collective-permute-start.8 = (bf16[128,512]{1,0:T(8,128)(2,1)S(1)}, bf16[128,512]{1,0:T(8,128)(2,1)S(1)}, u32[]{:S(2)}, u32[]{:S(2)}) collective-permute-start(bf16[128,512]{1,0:T(8,128)(2,1)S(1)} %unit_negatives.1.refs_0_), channel_id=1, source_target_pairs={{0,3},{1,2},{2,1},{3,0},{4,7},{5,6},{6,5},{7,4},{8,11},{9,10},{10,... | collective-permute-start | bytes 393224 | tf_op jit(solution)/shard_map/ppermute | solution.py:654
  33.8 6.5 %collective-permute-start.7 = (bf16[128,512]{1,0:T(8,128)(2,1)S(1)}, bf16[128,512]{1,0:T(8,128)(2,1)S(1)}, u32[]{:S(2)}, u32[]{:S(2)}) collective-permute-start(bf16[128,512]{1,0:T(8,128)(2,1)S(1)} %unit_negatives.1.refs_0_), channel_id=1, source_target_pairs={{0,2},{1,3},{2,0},{3,1},{4,6},{5,7},{6,4},{7,5},{8,10},{9,11},{10,... | collective-permute-start | bytes 393224 | tf_op jit(solution)/shard_map/ppermute | solution.py:654
  34.0 6.3 %collective-permute-start.6 = (bf16[128,512]{1,0:T(8,128)(2,1)S(1)}, bf16[128,512]{1,0:T(8,128)(2,1)S(1)}, u32[]{:S(2)}, u32[]{:S(2)}) collective-permute-start(bf16[128,512]{1,0:T(8,128)(2,1)S(1)} %unit_negatives.1.refs_0_), channel_id=1, source_target_pairs={{0,1},{1,0},{2,3},{3,2},{4,5},{5,4},{6,7},{7,6},{8,9},{9,8},{10,11... | collective-permute-start | bytes 393224 | tf_op jit(solution)/shard_map/ppermute | solution.py:654
  40.3 5.1 %collective-permute-start.12 = (bf16[512,512]{1,0:T(8,128)(2,1)S(1)}, bf16[512,512]{1,0:T(8,128)(2,1)S(1)}, u32[]{:S(2)}, u32[]{:S(2)}) collective-permute-start(bf16[512,512]{1,0:T(8,128)(2,1)S(1)} %join.1.refs_2_), channel_id=1, source_target_pairs={{0,4},{4,0},{8,12},{12,8},{16,20},{20,16},{24,28},{28,24},{1,5},{5... | collective-permute-start | bytes 1572872 | tf_op jit(solution)/shard_map/ppermute | solution.py:657
